TPU v7x, 256 devices: a whole 4x4x8 slice. The times are simulated.
256 devices in a mesh: dp: 16 (over z, x_lo), mp: 16 (over y, x_hi, core).
Axes of the slice: x: 4 (x_hi: 2, x_lo: 2; x = x_hi * 2 + x_lo), y: 4, z: 8, core: 2. Of those that a mesh axis runs over, the one named last changes fastest.
Arguments:
- tokens: bfloat16 [4096, 8192], P('dp', 'mp'), may hold values from -6 to 6
- cotangent: bfloat16 [4096, 8192], P('dp', 'mp'), may hold values from -6 to 6
- w_in: bfloat16 [64, 4, 256, 256], P('mp'), may hold values from -0.1875 to 0.1875
- w_out: bfloat16 [64, 4, 256, 256], P('mp'), may hold values from -0.125 to 0.125
- in_blocks: int32 [64, 4], P('mp'), may hold values from 0 to 31, as said below
- out_blocks: int32 [64, 4], P('mp'), may hold values from 0 to 31, as said below
Outputs:
- output: bfloat16 [4096, 8192], P('dp', 'mp')
- grad_tokens: bfloat16 [4096, 8192], P('dp', 'mp')
- grad_in: float32 [64, 4, 256, 256], P('mp', None, 'dp')
- grad_out: float32 [64, 4, 256, 256], P('mp', None, 'dp')
Inputs may be any that keep to these rules, and one draw needn't show every extreme that they name: `in_blocks`: flat butterfly pattern: row j holds p(j mod 32 XOR m) for m = 0, 1, 2, 4, with p a permutation of the 32 input blocks; the 4 entries of a row differ and every block is named by exactly 8 rows. `out_blocks`: the same flat butterfly form with its own permutation q of the 32 output blocks.
All inputs are finite; a program needn't handle non-finite values.
Results may differ from a plain program's by a relative error of at most 0.018.
Values may be sent and summed in bfloat16 or wider, within the bound.
No kernel may reach another device: no remote copies, remote signals or barrier semaphores. Data moves between devices by JAX's collectives and lax.ppermute only.
A program may use at most 128 MiB of HBM per device.

v0:
```python
import math

import jax
import jax.numpy as jnp
from jax import lax
from jax.sharding import PartitionSpec as P

MB = 2


def place_blocks(values, targets, row_blocks):
    step_tok = values.shape[0]
    side = values.shape[-1]
    flat = values.reshape(step_tok, -1, side)
    placed = (
        jnp.zeros((step_tok, row_blocks, side), jnp.float32).at[:, targets.reshape(-1)].add(flat)
    )
    return placed.reshape(step_tok, row_blocks * side)


def shards(tokens, cotangent, w_in, w_out, in_blocks, out_blocks):
    hb_dev, kk, side, _ = w_in.shape
    total_tok = tokens.shape[0]
    width = tokens.shape[1] * lax.axis_size("mp")
    row_blocks = width // side
    passes = MB
    step_tok = total_tok // passes
    grad_in = jnp.zeros(w_in.shape, jnp.float32)
    grad_out = jnp.zeros(w_out.shape, jnp.float32)
    out_share = None
    outputs = []
    backs = []
    for index in range(passes):
        x_part = tokens[index * step_tok : (index + 1) * step_tok]
        dy_part = cotangent[index * step_tok : (index + 1) * step_tok]
        x_full = lax.all_gather(x_part, "mp", axis=1, tiled=True)
        selected = x_full.reshape(step_tok, row_blocks, side)[:, in_blocks]
        pre = jnp.einsum("tjkb,jkbc->tjc", selected, w_in, preferred_element_type=jnp.float32)
        act = jax.nn.gelu(pre).astype(jnp.bfloat16)
        terms = jnp.einsum("tjb,jkbc->tjkc", act, w_out, preferred_element_type=jnp.float32)
        partial_out = place_blocks(terms, out_blocks, row_blocks)
        outputs.append(
            lax.psum_scatter(
                partial_out.astype(jnp.bfloat16), "mp", scatter_dimension=1, tiled=True
            )
        )
        dy_full = lax.all_gather(dy_part, "mp", axis=1, tiled=True)
        picked = dy_full.reshape(step_tok, row_blocks, side)[:, out_blocks]
        d_act = jnp.einsum("tjkc,jkbc->tjb", picked, w_out, preferred_element_type=jnp.float32)
        _, pullback = jax.vjp(jax.nn.gelu, pre)
        d_pre = pullback(d_act)[0].astype(jnp.bfloat16)
        grad_out = grad_out + jnp.einsum(
            "tjb,tjkc->jkbc", act, picked, preferred_element_type=jnp.float32
        )
        grad_in = grad_in + jnp.einsum(
            "tjkb,tjc->jkbc", selected, d_pre, preferred_element_type=jnp.float32
        )
        back = jnp.einsum("tjc,jkbc->tjkb", d_pre, w_in, preferred_element_type=jnp.float32)
        partial_back = place_blocks(back, in_blocks, row_blocks)
        backs.append(
            lax.psum_scatter(
                partial_back.astype(jnp.bfloat16), "mp", scatter_dimension=1, tiled=True
            )
        )
    scale = 1.0 / math.sqrt(total_tok * lax.axis_size("dp"))
    in_share, out_share = (
        lax.psum_scatter(
            grad_in.astype(jnp.bfloat16), "dp", scatter_dimension=2, tiled=True
        ).astype(jnp.float32),
        lax.psum_scatter(
            grad_out.astype(jnp.bfloat16), "dp", scatter_dimension=2, tiled=True
        ).astype(jnp.float32),
    )
    output = jnp.concatenate(outputs, axis=0)
    grad_tokens = jnp.concatenate(backs, axis=0)
    return (output, grad_tokens, in_share * scale, out_share * scale)


def solution(mesh):
    placed = (
        P("dp", "mp"),
        P("dp", "mp"),
        P("mp", None, None, None),
        P("mp", None, None, None),
        P("mp", None),
        P("mp", None),
    )
    return jax.shard_map(
        shards,
        mesh=mesh,
        in_specs=placed,
        out_specs=(
            P("dp", "mp"),
            P("dp", "mp"),
            P("mp", None, "dp", None),
            P("mp", None, "dp", None),
        ),
        check_vma=False,
    )
```

profile of v0, /device:TPU:1, one launch (start us, length us, event | category | flops | bytes accessed | tf_op | source)
XLA Modules:
  0.0 710.1 jit_solution(10971886927328735380)
XLA Ops:
  7.2 1.1 fusion.32
  8.4 0.8 copy.82
  9.2 1.0 fusion.31
  10.2 0.8 copy.84
  11.0 0.8 copy.83
  11.9 0.8 copy.85
  13.0 55.2 %all-gather.5.cloned.1.call-done = bf16[128,8192]{0,1:T(8,128)(2,1)} async-done(((bf16[128,512]{0,1:T(8,128)(2,1)}), bf16[128,8192]{0,1:T(8,128)(2,1)}) %all-gather.5.cloned.1.call-update) | async-done | bytes 2097168 | tf_op jit(solution)/shard_map/all_gather | solution.py:36
  68.2 4.1 copy.37
  72.3 50.7 %all-gather.9.cloned.1.call-done = bf16[128,8192]{0,1:T(8,128)(2,1)} async-done(((bf16[128,512]{0,1:T(8,128)(2,1)}), bf16[128,8192]{0,1:T(8,128)(2,1)}) %all-gather.9.cloned.1.call-update) | async-done | bytes 2097168 | tf_op jit(solution)/shard_map/all_gather | solution.py:47
  123.0 4.1 copy.47
  127.1 2.2 gather_fusion
  129.3 3.2 gather_fusion.2
  133.0 1.3 copy-done.2
  134.6 0.9 fusion.22
  135.5 2.2 fusion.33
  137.7 2.4 broadcast.63.clone.3
  140.1 5.1 scatter_fusion.2
  145.2 3.8 convert_element_type.58
  149.0 4.1 copy.50
  153.2 24.7 %all-gather.7.cloned.1.call-done = bf16[128,8192]{0,1:T(8,128)(2,1)} async-done(((bf16[128,512]{0,1:T(8,128)(2,1)}), bf16[128,8192]{0,1:T(8,128)(2,1)}) %all-gather.7.cloned.1.call-update) | async-done | bytes 2097168 | tf_op jit(solution)/shard_map/all_gather | solution.py:36
  177.8 4.1 copy.42
  181.9 3.2 gather_fusion.1
  185.1 47.4 %all-gather.11.cloned.1.call-done = bf16[128,8192]{0,1:T(8,128)(2,1)} async-done(((bf16[128,512]{0,1:T(8,128)(2,1)}), bf16[128,8192]{0,1:T(8,128)(2,1)}) %all-gather.11.cloned.1.call-update) | async-done | bytes 2097168 | tf_op jit(solution)/shard_map/all_gather | solution.py:47
  232.5 4.1 copy.52
  236.6 3.2 gather_fusion.3
  239.8 1.8 convolution_bitcast_fusion.2
  241.9 0.9 fusion.21
  242.9 2.2 fusion.34
  245.1 2.4 broadcast.63.clone.2
  247.5 4.4 scatter_fusion.3
  251.9 2.6 convert_element_type.61
  254.5 2.9 copy.55
  257.8 1.3 copy-done.4
  259.1 3.0 fusion.27
  262.1 2.4 broadcast.63.clone.1
  264.5 5.1 scatter_fusion
  269.6 3.8 convert_element_type.52
  273.4 4.1 copy.40
  277.6 2.9 fusion.24
  280.5 2.4 broadcast.63.clone
  282.9 4.3 scatter_fusion.1
  287.2 2.5 convert_element_type.55
  289.8 2.9 copy.45
  292.7 0.7 copy.38
  293.9 0.7 copy.43
  294.5 0.7 fusion.5
  295.5 2.0 add_convert_fusion.1
  297.6 1.1 copy-done.13
  298.7 1.3 copy.48
  300.0 0.7 copy.53
  300.7 2.0 fusion.2
  302.8 2.1 fusion
  304.9 6.8 reduce-scatter.11.cloned.1.call-done
  311.7 82.4 %reduce-scatter.13.cloned.1.call-done = bf16[128,512]{0,1:T(8,128)(2,1)} async-done(((bf16[128,8192]{0,1:T(8,128)(2,1)}), bf16[128,512]{0,1:T(8,128)(2,1)}) %reduce-scatter.13.cloned.1.call-update) | async-done | bytes 131088 | tf_op jit(solution)/shard_map/reduce_scatter | solution.py:61
  394.1 1.0 pad_maximum_fusion.1
  395.1 0.8 copy.59
  395.9 80.1 %reduce-scatter.7.cloned.1.call-done = bf16[128,512]{0,1:T(8,128)(2,1)} async-done(((bf16[128,8192]{0,1:T(8,128)(2,1)}), bf16[128,512]{0,1:T(8,128)(2,1)}) %reduce-scatter.7.cloned.1.call-update) | async-done | bytes 131088 | tf_op jit(solution)/shard_map/reduce_scatter | solution.py:43
  476.0 82.5 %reduce-scatter.9.cloned.1.call-done = bf16[128,512]{0,1:T(8,128)(2,1)} async-done(((bf16[128,8192]{0,1:T(8,128)(2,1)}), bf16[128,512]{0,1:T(8,128)(2,1)}) %reduce-scatter.9.cloned.1.call-update) | async-done | bytes 131088 | tf_op jit(solution)/shard_map/reduce_scatter | solution.py:43
  558.5 1.0 pad_maximum_fusion
  559.5 0.8 copy.58
  560.3 64.8 %reduce-scatter.15.cloned.1.call-done = bf16[4,4,16,256]{3,2,1,0:T(8,128)(2,1)} async-done(((bf16[4,4,256,256]{3,2,1,0:T(8,128)(2,1)}), bf16[4,4,16,256]{3,2,1,0:T(8,128)(2,1)}) %reduce-scatter.15.cloned.1.call-update) | async-done | bytes 131088 | tf_op jit(solution)/shard_map/reduce_scatter | solution.py:67
  625.1 1.6 convert_multiply_fusion.1
  626.7 74.9 %reduce-scatter.17.cloned.1.call-done = bf16[4,4,16,256]{3,2,1,0:T(8,128)(2,1)} async-done(((bf16[4,4,256,256]{3,2,1,0:T(8,128)(2,1)}), bf16[4,4,16,256]{3,2,1,0:T(8,128)(2,1)}) %reduce-scatter.17.cloned.1.call-update) | async-done | bytes 131088 | tf_op jit(solution)/shard_map/reduce_scatter | solution.py:70
  701.6 1.6 convert_multiply_fusion
  (68 shorter events, 3.0 us)
Async XLA Ops:
  7.2 125.4 %copy-start = (bf16[4,4,256,256]{3,2,1,0:T(8,128)(2,1)S(1)}, bf16[4,4,256,256]{3,2,1,0:T(8,128)(2,1)}, u32[]{:S(2)}) copy-start(bf16[4,4,256,256]{3,2,1,0:T(8,128)(2,1)} %param.8) | copy-start | bytes 6291460
  7.2 5.5 copy-start.18
  7.2 5.7 copy-start.19
  7.2 61.0 %all-gather.5.cloned.1.call-start = ((), (), s32[]{:S(2)}) async-start(), calls=%async_computation.6 | async-start | bytes 2228224 | tf_op jit(solution)/shard_map/all_gather | solution.py:36
  9.2 113.9 %all-gather.9.cloned.1.call-start = ((), (), s32[]{:S(2)}) async-start(), calls=%async_computation.10 | async-start | bytes 2228224 | tf_op jit(solution)/shard_map/all_gather | solution.py:47
  11.0 166.9 %all-gather.7.cloned.1.call-start = ((), (), s32[]{:S(2)}) async-start(), calls=%async_computation.8 | async-start | bytes 2228224 | tf_op jit(solution)/shard_map/all_gather | solution.py:36
  11.8 220.7 %all-gather.11.cloned.1.call-start = ((), (), s32[]{:S(2)}) async-start(), calls=%async_computation.12 | async-start | bytes 2228224 | tf_op jit(solution)/shard_map/all_gather | solution.py:47
  12.7 299.1 %reduce-scatter.11.cloned.1.call-start = ((), (), s32[]{:S(2)}) async-start(), calls=%async_computation.11 | async-start | bytes 2228224 | tf_op jit(solution)/shard_map/reduce_scatter | solution.py:61
  132.5 1.8 copy-start.2
  132.5 2.0 copy-start.12
  133.0 2.5 copy-start.8
  153.1 241.0 %reduce-scatter.13.cloned.1.call-start = ((), (), s32[]{:S(2)}) async-start(), calls=%async_computation.13 | async-start | bytes 2228224 | tf_op jit(solution)/shard_map/reduce_scatter | solution.py:61
  239.8 1.9 copy-start.3
  239.8 2.2 copy-start.14
  241.6 1.3 copy-start.10
  242.9 2.2 copy-start.16
  245.1 2.4 copy-start.7
  257.5 1.6 copy-start.4
  257.5 218.5 %reduce-scatter.7.cloned.1.call-start = ((), (), s32[]{:S(2)}) async-start(), calls=%async_computation.7 | async-start | bytes 2228224 | tf_op jit(solution)/shard_map/reduce_scatter | solution.py:43
  277.5 281.0 %reduce-scatter.9.cloned.1.call-start = ((), (), s32[]{:S(2)}) async-start(), calls=%async_computation.9 | async-start | bytes 2228224 | tf_op jit(solution)/shard_map/reduce_scatter | solution.py:43
  280.5 2.4 copy-start.5
  292.6 1.2 copy-start.6
  292.7 332.4 %reduce-scatter.15.cloned.1.call-start = ((), (), s32[]{:S(2)}) async-start(), calls=%async_computation.14 | async-start | bytes 2228224 | tf_op jit(solution)/shard_map/reduce_scatter | solution.py:67
  294.5 1.0 copy-start.17
  297.5 1.2 copy-start.13
  297.5 2.5 copy-start.15
  297.5 404.1 %reduce-scatter.17.cloned.1.call-start = ((), (), s32[]{:S(2)}) async-start(), calls=%async_computation.15 | async-start | bytes 2228224 | tf_op jit(solution)/shard_map/reduce_scatter | solution.py:70
  298.7 2.0 copy-start.9
  300.7 2.1 copy-start.11
  304.9 398.4 %copy-start.1 = (bf16[4,4,256,256]{3,2,1,0:T(8,128)(2,1)S(1)}, bf16[4,4,256,256]{3,2,1,0:T(8,128)(2,1)}, u32[]{:S(2)}) copy-start(bf16[4,4,256,256]{3,2,1,0:T(8,128)(2,1)} %param.8) | copy-start | bytes 6291460
Sparse Core Ops, SparseCore 0:
  11.4 56.7 all-gather.4
  71.5 51.4 all-gather.8
  126.4 51.4 all-gather.6
  181.0 51.4 all-gather.10
  236.5 75.1 reduce-scatter.10
  316.3 77.6 reduce-scatter.12
  398.3 77.6 reduce-scatter.6
  480.7 77.6 reduce-scatter.8
  561.0 64.0 reduce-scatter.14
  627.5 74.1 reduce-scatter.16
where the time goes:
time: 722 us; the launch traced here: 710 us
  waiting for transfers between devices  570 us (79%)
  local copies, waits for them, and re-layouts  67.4 us (9%)
  other arithmetic  36.9 us (5%)
  matrix products  21.2 us (3%)
  between operations  14.4 us (2%)
    reduce_scatter x2, waiting for transfers between devices, shards(): lax.psum_scatter(partial_out.astype(jnp.bfloat16), 'mp', scatter_dimensio...  163 us
    all_gather x2, waiting for transfers between devices, shards(): dy_full = lax.all_gather(dy_part, 'mp', axis=1, tiled=True)  98.1 us
    reduce_scatter x2, waiting for transfers between devices, shards(): lax.psum_scatter(partial_back.astype(jnp.bfloat16), 'mp', scatter_dimensi...  89.2 us
    all_gather x2, waiting for transfers between devices, shards(): x_full = lax.all_gather(x_part, 'mp', axis=1, tiled=True)  79.9 us
    reduce_scatter x1, waiting for transfers between devices, shards(): lax.psum_scatter(grad_out.astype(jnp.bfloat16), 'dp', scatter_dimension=2...  74.9 us
    reduce_scatter x1, waiting for transfers between devices, shards(): lax.psum_scatter(grad_in.astype(jnp.bfloat16), 'dp', scatter_dimension=2,...  64.8 us
    scatter-add x4, other arithmetic, place_blocks(): jnp.zeros((step_tok, row_blocks, side), jnp.float32)  18.9 us
  transfers between devices with their start and end apart: 10, of which 10 were waited for; matrix products, arithmetic and copies ran while one was open for 16% of the time, Pallas kernels for 0%

commit v1 on v0

v1 whole, which is shorter than its diff:
```python
import functools
import math

import jax
import jax.numpy as jnp
from jax import lax
from jax.experimental import pallas as pl
from jax.experimental.pallas import tpu as pltpu
from jax.sharding import PartitionSpec as P

SIDE = 256
QUAD = 4 * SIDE
SLICE = 16
VMEM = pl.BlockSpec(memory_space=pltpu.VMEM)
SMEM = pl.BlockSpec(memory_space=pltpu.SMEM)
BF16 = jnp.bfloat16
F32 = jnp.float32


def params():
    return pltpu.CompilerParams(vmem_limit_bytes=48 * 1024 * 1024)


def pack_kernel(n, x_ref, dy_ref, p_ref, q_ref, out_ref):
    lane = lax.broadcasted_iota(jnp.int32, (2 * SLICE, 128), 1)
    lists = jnp.zeros((2 * SLICE, 128), F32)
    for t in range(4):
        lists = jnp.where(lane == t, p_ref[t, 0].astype(F32), lists)
        lists = jnp.where(lane == t + 4, q_ref[t, 0].astype(F32), lists)
    lists = lists.astype(BF16)
    for i in range(n):
        out_ref[i, :SLICE, : 2 * SIDE] = x_ref[pl.ds(i * SLICE, SLICE), :]
        out_ref[i, SLICE:, : 2 * SIDE] = dy_ref[pl.ds(i * SLICE, SLICE), :]
        out_ref[i, :, 2 * SIDE :] = lists


def select_kernel(n, got_ref, out_ref, lists_ref, table, sem):
    lists = jnp.max(got_ref[:, :SLICE, 2 * SIDE :].astype(F32), axis=1).astype(jnp.int32)
    lists_ref[...] = lists
    copy = pltpu.make_async_copy(lists_ref, table, sem)
    copy.start()
    copy.wait()
    for quad in range(n // 2):
        for t in range(4):
            for row, column in ((0, t), (SLICE, t + 4)):
                block = table[quad, column]
                owner = lax.shift_right_logical(block, 1)
                half = pl.multiple_of((block & 1) * SIDE, SIDE)
                piece = got_ref[owner, pl.ds(row, SLICE), pl.ds(half, SIDE)]
                out_ref[quad, pl.ds(row, SLICE), pl.ds(t * SIDE, SIDE)] = piece
                out_ref[quad + n // 2, pl.ds(row, SLICE), pl.ds(t * SIDE, SIDE)] = piece


def block_of(ref, row, slot):
    piece = ref[:, pl.ds(row, SLICE), pl.ds(slot * SIDE, SIDE)]
    return piece.reshape(-1, SIDE)


def dot(a, b, da, db):
    return lax.dot_general(a, b, (((da,), (db,)), ((), ())), preferred_element_type=F32)


def hidden_kernel(own_ref, oth_ref, win_ref, wout_ref, grads_ref, act_ref, dpre_ref):
    j = pl.program_id(0)
    slots = [j, j ^ 1, j ^ 2]
    xs = [block_of(own_ref, 0, s) for s in slots] + [block_of(oth_ref, 0, j)]
    dys = [block_of(own_ref, SLICE, s) for s in slots] + [block_of(oth_ref, SLICE, j)]
    pre = sum(dot(xs[k], win_ref[0, k], 1, 0) for k in range(4))
    d_act = sum(dot(dys[k], wout_ref[0, k], 1, 1) for k in range(4))
    c = math.sqrt(2.0 / math.pi)
    square = pre * pre
    th = jnp.tanh(c * (pre + 0.044715 * (square * pre)))
    half = 0.5 * (1.0 + th)
    act = (pre * half).astype(BF16)
    slope = half + (0.5 * c) * pre * (1.0 - th * th) * (1.0 + (3 * 0.044715) * square)
    d_pre = (d_act * slope).astype(BF16)
    act_ref[...] = act
    dpre_ref[...] = d_pre
    zs, xl = grads_ref.shape[0], grads_ref.shape[1]
    for k in range(4):
        g_in = dot(xs[k], d_pre, 0, 0).astype(BF16)
        g_out = dot(act, dys[k], 0, 0).astype(BF16)
        grads_ref[:, :, 0, 0, k] = g_in.reshape(zs, xl, SLICE, SIDE)
        grads_ref[:, :, 1, 0, k] = g_out.reshape(zs, xl, SLICE, SIDE)


def project_kernel(act_ref, dpre_ref, win_ref, wout_ref, own_ref, oth_ref):
    acts = [act_ref[:, t * SIDE : (t + 1) * SIDE] for t in range(4)]
    dpres = [dpre_ref[:, t * SIDE : (t + 1) * SIDE] for t in range(4)]
    for s in range(4):
        lanes = pl.ds(s * SIDE, SIDE)
        own = sum(dot(acts[s ^ m], wout_ref[s ^ m, k], 1, 0) for k, m in enumerate((0, 1, 2)))
        oth = dot(acts[s], wout_ref[s, 3], 1, 0)
        own_ref[:, :SLICE, lanes] = own.astype(BF16).reshape(-1, SLICE, SIDE)
        oth_ref[:, :SLICE, lanes] = oth.astype(BF16).reshape(-1, SLICE, SIDE)
        own = sum(dot(dpres[s ^ m], win_ref[s ^ m, k], 1, 1) for k, m in enumerate((0, 1, 2)))
        oth = dot(dpres[s], win_ref[s, 3], 1, 1)
        own_ref[:, SLICE:, lanes] = own.astype(BF16).reshape(-1, SLICE, SIDE)
        oth_ref[:, SLICE:, lanes] = oth.astype(BF16).reshape(-1, SLICE, SIDE)


def sort_kernel(n, table, got_ref, out_ref):
    for quad in range(n // 2):
        for t in range(4):
            for row, column in ((0, t + 4), (SLICE, t)):
                block = table[quad, column]
                owner = lax.shift_right_logical(block, 1)
                half = pl.multiple_of((block & 1) * SIDE, SIDE)
                rows, lanes = pl.ds(row, SLICE), pl.ds(t * SIDE, SIDE)
                total = got_ref[quad, rows, lanes].astype(F32)
                total = total + got_ref[quad + n // 2, rows, lanes].astype(F32)
                out_ref[owner, rows, pl.ds(half, SIDE)] = total.astype(BF16)


def shards(tokens, cotangent, w_in, w_out, in_blocks, out_blocks):
    n = lax.axis_size("mp")
    n_dp = lax.axis_size("dp")
    zs = n_dp // 2
    tok = tokens.shape[0]
    total_tok = tok * n_dp
    mate = [(i, i ^ 1) for i in range(n)]

    packed = pl.pallas_call(
        functools.partial(pack_kernel, n),
        out_shape=jax.ShapeDtypeStruct((n, 2 * SLICE, 2 * SIDE + 128), BF16),
        in_specs=[VMEM, VMEM, SMEM, SMEM],
        out_specs=VMEM,
        compiler_params=params(),
        name="pack",
    )(tokens, cotangent, in_blocks, out_blocks)
    got = lax.all_to_all(packed, "mp", 0, 0, tiled=True)
    chosen, table = pl.pallas_call(
        functools.partial(select_kernel, n),
        out_shape=(
            jax.ShapeDtypeStruct((n, 2 * SLICE, QUAD), BF16),
            jax.ShapeDtypeStruct((n, 128), jnp.int32),
        ),
        in_specs=[VMEM],
        out_specs=(VMEM, VMEM),
        scratch_shapes=[pltpu.SMEM((n, 128), jnp.int32), pltpu.SemaphoreType.DMA],
        compiler_params=params(),
        name="select",
    )(got)
    own = lax.all_to_all(chosen, "mp", 0, 0, tiled=True)
    oth = lax.ppermute(own, "mp", mate)

    whole = lambda shape: pl.BlockSpec(shape, lambda j: (0,) * len(shape))
    grads, act, d_pre = pl.pallas_call(
        hidden_kernel,
        grid=(4,),
        out_shape=(
            jax.ShapeDtypeStruct((zs, 2, 2, 4, 4, SLICE, SIDE), BF16),
            jax.ShapeDtypeStruct((tok, QUAD), BF16),
            jax.ShapeDtypeStruct((tok, QUAD), BF16),
        ),
        in_specs=[
            whole(own.shape),
            whole(oth.shape),
            pl.BlockSpec((1, 4, SIDE, SIDE), lambda j: (j, 0, 0, 0)),
            pl.BlockSpec((1, 4, SIDE, SIDE), lambda j: (j, 0, 0, 0)),
        ],
        out_specs=(
            pl.BlockSpec((zs, 2, 2, 1, 4, SLICE, SIDE), lambda j: (0, 0, 0, j, 0, 0, 0)),
            pl.BlockSpec((tok, SIDE), lambda j: (0, j)),
            pl.BlockSpec((tok, SIDE), lambda j: (0, j)),
        ),
        compiler_params=params(),
        name="hidden",
    )(own, oth, w_in, w_out)

    columns = [[z * 2 + xl for z in range(zs)] for xl in range(2)]
    grad_sum = lax.psum_scatter(
        grads.reshape(-1, SIDE), "dp", scatter_dimension=0, axis_index_groups=columns, tiled=True
    )

    share = jax.ShapeDtypeStruct((n, 2 * SLICE, QUAD), BF16)
    part_own, part_oth = pl.pallas_call(
        project_kernel,
        out_shape=(share, share),
        in_specs=[VMEM] * 4,
        out_specs=(VMEM, VMEM),
        compiler_params=params(),
        name="project",
    )(act, d_pre, w_in, w_out)
    part_mate = lax.ppermute(part_oth, "mp", mate)
    part = (part_own.astype(F32) + part_mate.astype(F32)).astype(BF16)
    slices = lax.all_to_all(part, "mp", 0, 0, tiled=True)
    sorted_ = pl.pallas_call(
        functools.partial(sort_kernel, n),
        out_shape=jax.ShapeDtypeStruct((n, 2 * SLICE, 2 * SIDE), BF16),
        in_specs=[SMEM, VMEM],
        out_specs=VMEM,
        compiler_params=params(),
        name="sort",
    )(table, slices)
    final = lax.all_to_all(sorted_, "mp", 0, 0, tiled=True)
    output = final[:, :SLICE].reshape(tok, 2 * SIDE)
    grad_tokens = final[:, SLICE:].reshape(tok, 2 * SIDE)

    side = lax.rem(lax.axis_index("dp"), 2)
    halves = grad_sum.reshape(2, 2, 4, 4, SLICE, SIDE)
    away = lax.dynamic_index_in_dim(halves, 1 - side, 0, keepdims=False)
    mine = lax.dynamic_index_in_dim(halves, side, 0, keepdims=False)
    came = lax.ppermute(away, "dp", [(i, i ^ 1) for i in range(n_dp)])
    scale = 1.0 / math.sqrt(total_tok)
    both = (mine.astype(F32) + came.astype(F32)) * scale
    return output, grad_tokens, both[0], both[1]


def solution(mesh):
    placed = (
        P("dp", "mp"),
        P("dp", "mp"),
        P("mp", None, None, None),
        P("mp", None, None, None),
        P("mp", None),
        P("mp", None),
    )
    return jax.shard_map(
        shards,
        mesh=mesh,
        in_specs=placed,
        out_specs=(
            P("dp", "mp"),
            P("dp", "mp"),
            P("mp", None, "dp", None),
            P("mp", None, "dp", None),
        ),
        check_vma=False,
    )
```

time: 722 us -> 135 us (0.19); the launches traced: 710 us -> 134 us
  waiting for transfers between devices: 570 us -> 31.3 us
  local copies, waits for them, and re-layouts: 67.4 us -> 5.88 us
  blocking collectives: 0 us -> 61.5 us
  other arithmetic: 36.9 us -> 1.43 us
  matrix products: 21.2 us -> 0 us
  Pallas kernels: 0 us -> 12.4 us
    reduce_scatter x6 -> x1, waiting for transfers between devices: 391 us -> 21.5 us  [shards(): lax.psum_scatter(grads.reshape(-1, SIDE), 'dp', scatter_dimension=0, axis...]
    all_gather x4 -> x0, waiting for transfers between devices: 178 us -> none  [the longest x2 98.1 us: shards(): dy_full = lax.all_gather(dy_part, 'mp', axis=1, tiled=True)]
    all_to_all x0 -> x3, blocking collectives: none -> 61.5 us  [the longest x1 21.6 us: shards(): got = lax.all_to_all(packed, 'mp', 0, 0, tiled=True)]
    dot_general x12 -> x0, matrix products: 21.2 us -> none  [the longest x2 5.87 us: shards(): jnp.einsum('tjb,jkbc->tjkc', act, w_out, preferred_element_type=jnp.float32)]
    scatter-add x4 -> x0, other arithmetic: 18.9 us -> none  [place_blocks(): jnp.zeros((step_tok, row_blocks, side), jnp.float32)]
    reshape x6 -> x0, local copies, waits for them, and re-layouts: 16.5 us -> none  [the longest x2 8.15 us: shards(): selected = x_full.reshape(step_tok, row_blocks, side)[:, in_blocks]]
    gather x8 -> x0, local copies, waits for them, and re-layouts: 15.1 us -> none  [the longest x4 8.39 us: shards(): picked = dy_full.reshape(step_tok, row_blocks, side)[:, out_blocks]]
    convert_element_type x4 -> x0, local copies, waits for them, and re-layouts: 14 us -> none  [the longest x2 7.01 us: shards(): partial_back.astype(jnp.bfloat16)]
  transfers between devices with their start and end apart: 10 -> 5, of which waited for: 10 -> 4; matrix products, arithmetic and copies ran while one was open for 16% -> 2% of each run, Pallas kernels for 0% -> 3%
where the time goes in v1:
time: 135 us; the launch traced here: 134 us
  blocking collectives  61.5 us (46%)
  waiting for transfers between devices  31.3 us (23%)
  between operations  14.1 us (10%)
  Pallas kernels  12.4 us (9%)
  starting transfers between devices  7.47 us (6%)
  local copies, waits for them, and re-layouts  5.88 us (4%)
  other arithmetic  1.43 us (1%)
    all_to_all x1, blocking collectives, shards(): got = lax.all_to_all(packed, 'mp', 0, 0, tiled=True)  21.6 us
    reduce_scatter x1, waiting for transfers between devices, shards(): lax.psum_scatter(grads.reshape(-1, SIDE), 'dp', scatter_dimension=0, axis...  21.5 us
    all_to_all x1, blocking collectives, shards(): own = lax.all_to_all(chosen, 'mp', 0, 0, tiled=True)  20.1 us
    all_to_all x1, blocking collectives, shards(): slices = lax.all_to_all(part, 'mp', 0, 0, tiled=True)  19.8 us
    pallas_call x1, Pallas kernels, shards(): pl.pallas_call(hidden_kernel, grid=(4,), out_shape=(jax.ShapeDtypeStruct(...  6.45 us
    ppermute x1, waiting for transfers between devices, shards(): came = lax.ppermute(away, 'dp', [(i, i ^ 1) for i in range(n_dp)])  5.2 us
    all_to_all x1, starting transfers between devices, shards(): final = lax.all_to_all(sorted_, 'mp', 0, 0, tiled=True)  4.53 us
    unnamed x10, local copies, waits for them, and re-layouts  3.26 us
  transfers between devices with their start and end apart: 5, of which 4 were waited for; matrix products, arithmetic and copies ran while one was open for 2% of the time, Pallas kernels for 3%

profile of v1, /device:TPU:1, one launch (start us, length us, event | category | flops | bytes accessed | tf_op | source)
XLA Modules:
  0.0 134.1 jit_solution(9333144773714550311)
XLA Ops:
  7.2 0.0 reduce-scatter.2.cloned.1.call-start
  7.2 0.0 copy-start.1
  7.2 0.9 copy-done.1
  8.2 0.0 copy-start.2
  8.2 0.9 copy-done.2
  9.1 0.0 copy-start.3
  9.1 0.7 copy-done.3
  9.8 0.0 copy-start.4
  9.8 0.7 copy-done.4
  10.5 0.6 pack.1
  11.1 0.0 copy-start
  11.1 21.6 %all_to_all.20.got_ref = bf16[16,32,640]{2,1,0:T(8,128)(2,1)S(1)} all-to-all(bf16[16,32,640]{2,1,0:T(8,128)(2,1)S(1)} %pack.1), channel_id=1, replica_groups=mesh['dp'=16,'mp'=16] {'mp'}, dimensions={0} | all-to-all | bytes 1310720 | tf_op jit(solution)/shard_map/all_to_all | solution.py:131
  32.8 0.9 select.3
  33.6 20.1 %all_to_all.21.own_ref = bf16[16,32,1024]{2,1,0:T(8,128)(2,1)S(1)} all-to-all(bf16[16,32,1024]{2,1,0:T(8,128)(2,1)S(1)} %get-tuple-element.12), channel_id=1, replica_groups=mesh['dp'=16,'mp'=16] {'mp'}, dimensions={0} | all-to-all | bytes 2097152 | tf_op jit(solution)/shard_map/all_to_all | solution.py:144
  53.7 1.2 collective-permute-start
  54.9 2.3 %collective-permute-done.oth_ref = bf16[16,32,1024]{2,1,0:T(8,128)(2,1)S(1)} collective-permute-done((bf16[16,32,1024]{2,1,0:T(8,128)(2,1)S(1)}, bf16[16,32,1024]{2,1,0:T(8,128)(2,1)S(1)}, u32[]{:S(2)}, u32[]{:S(2)}) %collective-permute-start) | collective-permute-done | bytes 1048608 | tf_op jit(solution)/shard_map/ppermute | solution.py:145
  57.2 0.0 copy-done
  57.2 6.5 %hidden.1 = (bf16[8,2,2,4,4,16,256]{6,5,4,3,2,1,0:T(8,128)(2,1)}, bf16[256,1024]{1,0:T(8,128)(2,1)S(1)}, bf16[256,1024]{1,0:T(8,128)(2,1)S(1)}) custom-call(bf16[16,32,1024]{2,1,0:T(8,128)(2,1)S(1)} %all_to_all.21.own_ref, bf16[16,32,1024]{2,1,0:T(8,128)(2,1)S(1)} %collective-permute-done.oth_ref, bf16[4,4,256,256]{3,2,1,0:T(8,128)(2,1)S(1)} %copy-done, ...), custom_call_target="tpu_custom_call" | custom-call | tf_op jit(solution)/shard_map/hidden/pallas_call | solution.py:148
  63.7 0.0 reduce-scatter.2.cloned.1.call-update
  63.7 2.9 %project.1 = (bf16[16,32,1024]{2,1,0:T(8,128)(2,1)S(1)}, bf16[16,32,1024]{2,1,0:T(8,128)(2,1)S(1)}) custom-call(bf16[256,1024]{1,0:T(8,128)(2,1)S(1)} %get-tuple-element.13.act_ref, bf16[256,1024]{1,0:T(8,128)(2,1)S(1)} %get-tuple-element.14.dpre_ref, bf16[4,4,256,256]{3,2,1,0:T(8,128)(2,1)S(1)} %copy-done, bf16[4,4,256,256]{3,2,1,0:T(8,128)(2,1)} %wout_ref.3), custom_call_target="tpu_custom_call" | custom-call | tf_op jit(solution)/shard_map/project/pallas_call | solution.py:177
  66.5 0.5 collective-permute-start.1
  67.0 2.3 %collective-permute-done.1 = bf16[16,32,1024]{2,1,0:T(8,128)(2,1)S(1)} collective-permute-done((bf16[16,32,1024]{2,1,0:T(8,128)(2,1)S(1)}, bf16[16,32,1024]{2,1,0:T(8,128)(2,1)S(1)}, u32[]{:S(2)}, u32[]{:S(2)}) %collective-permute-start.1) | collective-permute-done | bytes 1048608 | tf_op jit(solution)/shard_map/ppermute | solution.py:185
  69.3 0.4 add_convert_fusion
  69.7 19.8 %all_to_all.22.got_ref = bf16[16,32,1024]{2,1,0:T(8,128)(2,1)S(1)} all-to-all(bf16[16,32,1024]{2,1,0:T(8,128)(2,1)S(1)} %add_convert_fusion), channel_id=1, replica_groups=mesh['dp'=16,'mp'=16] {'mp'}, dimensions={0} | all-to-all | bytes 2097152 | tf_op jit(solution)/shard_map/all_to_all | solution.py:187
  89.5 1.6 %sort.1 = bf16[16,32,512]{2,1,0:T(8,128)(2,1)} custom-call(s32[16,128]{1,0:T(8,128)S(1)} %get-tuple-element.11.table, bf16[16,32,1024]{2,1,0:T(8,128)(2,1)S(1)} %all_to_all.22.got_ref), custom_call_target="tpu_custom_call" | custom-call | tf_op jit(solution)/shard_map/sort/pallas_call | solution.py:188
  91.1 4.5 %all-to-all-start.3 = ((bf16[16,32,512]{2,1,0:T(8,128)(2,1)}), bf16[16,32,512]{2,1,0:T(8,128)(2,1)S(1)}, u32[]{:S(2)}, u32[]{:S(2)}) async-start(bf16[16,32,512]{2,1,0:T(8,128)(2,1)} %sort.1), calls=%async_computation.3 | async-start | bytes 1048576 | tf_op jit(solution)/shard_map/all_to_all | solution.py:196
  95.7 21.5 %reduce-scatter.2.cloned.1.call-done = bf16[1024,256]{1,0:T(8,128)(2,1)} async-done(((bf16[8192,256]{1,0:T(8,128)(2,1)}), bf16[1024,256]{1,0:T(8,128)(2,1)}) %reduce-scatter.2.cloned.1.call-update) | async-done | bytes 524304 | tf_op jit(solution)/shard_map/reduce_scatter | solution.py:172
  117.1 1.0 dynamic-slice_bitcast_fusion
  118.1 1.3 collective-permute-start.2
  119.4 0.0 all-to-all-done.3
  119.4 0.8 fusion.1
  120.2 5.2 %collective-permute-done.2 = bf16[2,4,4,16,256]{4,3,2,1,0:T(8,128)(2,1)S(1)} collective-permute-done((bf16[2,4,4,16,256]{4,3,2,1,0:T(8,128)(2,1)S(1)}, bf16[2,4,4,16,256]{4,3,2,1,0:T(8,128)(2,1)S(1)}, u32[]{:S(2)}, u32[]{:S(2)}) %collective-permute-start.2) | collective-permute-done | bytes 262176 | tf_op jit(solution)/shard_map/ppermute | solution.py:204
  125.4 1.0 fusion
  126.5 0.8 slice_bitcast_fusion
Async XLA Ops:
  7.2 110.0 %reduce-scatter.2.cloned.1.call-start = ((), (), s32[]{:S(2)}) async-start(), calls=%async_computation.5 | async-start | bytes 4718592 | tf_op jit(solution)/shard_map/reduce_scatter | solution.py:172
  7.2 1.0 copy-start.1
  8.2 0.9 copy-start.2
  9.1 0.7 copy-start.3
  9.8 0.7 copy-start.4
  11.1 46.1 %copy-start = (bf16[4,4,256,256]{3,2,1,0:T(8,128)(2,1)S(1)}, bf16[4,4,256,256]{3,2,1,0:T(8,128)(2,1)}, u32[]{:S(2)}) copy-start(bf16[4,4,256,256]{3,2,1,0:T(8,128)(2,1)} %win_ref.3) | copy-start | bytes 6291460
  53.7 3.5 %collective-permute-start = (bf16[16,32,1024]{2,1,0:T(8,128)(2,1)S(1)}, bf16[16,32,1024]{2,1,0:T(8,128)(2,1)S(1)}, u32[]{:S(2)}, u32[]{:S(2)}) collective-permute-start(bf16[16,32,1024]{2,1,0:T(8,128)(2,1)S(1)} %all_to_all.21.own_ref), channel_id=1, source_target_pairs={{0,1},{1,0},{2,3},{3,2},{4,5},{5,4},{6,7},{7,6},{8,9},{9,8},{10,11... | collective-permute-start | bytes 3145736 | tf_op jit(solution)/shard_map/ppermute | solution.py:145
  66.5 2.7 %collective-permute-start.1 = (bf16[16,32,1024]{2,1,0:T(8,128)(2,1)S(1)}, bf16[16,32,1024]{2,1,0:T(8,128)(2,1)S(1)}, u32[]{:S(2)}, u32[]{:S(2)}) collective-permute-start(bf16[16,32,1024]{2,1,0:T(8,128)(2,1)S(1)} %get-tuple-element.16), channel_id=1, source_target_pairs={{0,1},{1,0},{2,3},{3,2},{4,5},{5,4},{6,7},{7,6},{8,9},{9,8},{10,11... | collective-permute-start | bytes 3145736 | tf_op jit(solution)/shard_map/ppermute | solution.py:185
  91.1 28.3 %all-to-all-start.3 = ((bf16[16,32,512]{2,1,0:T(8,128)(2,1)}), bf16[16,32,512]{2,1,0:T(8,128)(2,1)S(1)}, u32[]{:S(2)}, u32[]{:S(2)}) async-start(bf16[16,32,512]{2,1,0:T(8,128)(2,1)} %sort.1), calls=%async_computation.3 | async-start | bytes 1048576 | tf_op jit(solution)/shard_map/all_to_all | solution.py:196
  118.1 7.3 %collective-permute-start.2 = (bf16[2,4,4,16,256]{4,3,2,1,0:T(8,128)(2,1)S(1)}, bf16[2,4,4,16,256]{4,3,2,1,0:T(8,128)(2,1)S(1)}, u32[]{:S(2)}, u32[]{:S(2)}) collective-permute-start(bf16[2,4,4,16,256]{4,3,2,1,0:T(8,128)(2,1)S(1)} %dynamic-slice_bitcast_fusion), channel_id=1, source_target_pairs={{0,16},{16,0},{32,48},{48,32},{64,80},{80,64},{96,112},{112,96},{1... | collective-permute-start | bytes 786440 | tf_op jit(solution)/shard_map/ppermute | solution.py:204
Sparse Core Ops, SparseCore 0:
  63.8 53.3 reduce-scatter.1

commit v2 on v1

v2 whole, which is shorter than its diff:
```python
import math

import jax
import jax.numpy as jnp
from jax import lax
from jax.experimental import pallas as pl
from jax.experimental.pallas import tpu as pltpu
from jax.sharding import PartitionSpec as P

SIDE = 256
QUAD = 4 * SIDE
SLICE = 16
VMEM = pl.BlockSpec(memory_space=pltpu.VMEM)
ANY = pl.BlockSpec(memory_space=pl.ANY)
SMEM = pl.BlockSpec(memory_space=pltpu.SMEM)
BF16 = jnp.bfloat16
F32 = jnp.float32


def params():
    return pltpu.CompilerParams(vmem_limit_bytes=40 * 1024 * 1024)


def pack_kernel(x_ref, dy_ref, p_ref, q_ref, out_ref, lists, sems):
    features = pl.ds(0, 2 * SIDE)
    copies = [
        pltpu.make_async_copy(p_ref, lists.at[0], sems.at[0]),
        pltpu.make_async_copy(q_ref, lists.at[1], sems.at[1]),
        pltpu.make_async_copy(x_ref, out_ref.at[:, pl.ds(0, SLICE), features], sems.at[2]),
        pltpu.make_async_copy(dy_ref, out_ref.at[:, pl.ds(SLICE, SLICE), features], sems.at[3]),
    ]
    for copy in copies:
        copy.start()
    row = lax.broadcasted_iota(jnp.int32, (4, 128), 0)
    lane = lax.broadcasted_iota(jnp.int32, (4, 128), 1)
    total = jnp.zeros((1, 128), F32)
    for part in range(2):
        copies[part].wait()
        column = jnp.broadcast_to(lists[part][:, 0:1], (4, 128)).astype(F32)
        total = total + jnp.sum(jnp.where(lane == row + 4 * part, column, 0.0), axis=0, keepdims=True)
    tail = out_ref.shape[:2] + (128,)
    out_ref[:, :, 2 * SIDE :] = jnp.broadcast_to(total[None], tail).astype(BF16)
    copies[2].wait()
    copies[3].wait()


def select_kernel(got_ref, out_ref, lists_ref, table, sem):
    lists = jnp.max(got_ref[:, :SLICE, 2 * SIDE :].astype(F32), axis=1).astype(jnp.int32)
    lists_ref[...] = lists
    copy = pltpu.make_async_copy(lists_ref, table, sem)
    copy.start()
    copy.wait()
    chips = out_ref.shape[0]
    for group in range(chips // 2):
        for slot in range(8):
            for row, column in ((0, slot % 4), (SLICE, slot % 4 + 4)):
                block = table[2 * group + slot // 4, column]
                owner = lax.shift_right_logical(block, 1)
                half = pl.multiple_of((block & 1) * SIDE, SIDE)
                piece = got_ref[owner, pl.ds(row, SLICE), pl.ds(half, SIDE)]
                out_ref[group, slot, pl.ds(row, SLICE), :] = piece
                out_ref[group + chips // 2, slot, pl.ds(row, SLICE), :] = piece


def dot(a, b, da, db):
    return lax.dot_general(a, b, (((da,), (db,)), ((), ())), preferred_element_type=F32)


def slots_of(j):
    core = lax.axis_index("mp") & 1
    return [4 * core + (j ^ m) for m in (0, 1, 2)] + [4 * (1 - core) + j]


def hidden_kernel(own_ref, oth_ref, win_ref, wout_ref, grads_ref, act_ref, dpre_ref, held, sems):
    def block_of(row, slot):
        pieces = [ref[:, slot, pl.ds(row, SLICE), :].reshape(-1, SIDE) for ref in (own_ref, oth_ref)]
        return jnp.concatenate(pieces, axis=0)

    side = lax.axis_index("dp") & 1
    c = math.sqrt(2.0 / math.pi)
    copies = []
    for j in range(4):
        slots = slots_of(j)
        xs = [block_of(0, s) for s in slots]
        dys = [block_of(SLICE, s) for s in slots]
        pre = sum(dot(xs[k], win_ref[j, k], 1, 0) for k in range(4))
        d_act = sum(dot(dys[k], wout_ref[j, k], 1, 1) for k in range(4))
        square = pre * pre
        th = jnp.tanh(c * (pre + 0.044715 * (square * pre)))
        half = 0.5 * (1.0 + th)
        act = (pre * half).astype(BF16)
        slope = half + (0.5 * c) * pre * (1.0 - th * th) * (1.0 + (3 * 0.044715) * square)
        d_pre = (d_act * slope).astype(BF16)
        act_ref[:, j * SIDE : (j + 1) * SIDE] = act
        dpre_ref[:, j * SIDE : (j + 1) * SIDE] = d_pre
        zs = held.shape[1]
        for k in range(4):
            g_in = dot(xs[k], d_pre, 0, 0).astype(BF16).reshape(zs, 2, SLICE, SIDE)
            g_out = dot(act, dys[k], 0, 0).astype(BF16).reshape(zs, 2, SLICE, SIDE)
            for away in range(2):
                held[j, :, away ^ side, 0, k] = g_in[:, away]
                held[j, :, away ^ side, 1, k] = g_out[:, away]
        copies.append(pltpu.make_async_copy(held.at[j], grads_ref.at[:, :, :, j], sems.at[j]))
        copies[-1].start()
    for copy in copies:
        copy.wait()


def project_kernel(act_ref, dpre_ref, win_ref, wout_ref, own_ref, oth_ref):
    core = lax.axis_index("mp") & 1
    acts = [act_ref[:, t * SIDE : (t + 1) * SIDE] for t in range(4)]
    dpres = [dpre_ref[:, t * SIDE : (t + 1) * SIDE] for t in range(4)]

    def put(row, slot, total):
        pieces = total.astype(BF16).reshape(2, -1, SLICE, SIDE)
        own_ref[:, slot, pl.ds(row, SLICE), :] = pieces[0]
        oth_ref[:, slot, pl.ds(row, SLICE), :] = pieces[1]

    for s in range(4):
        near, far = 4 * core + s, 4 * (1 - core) + s
        three = [(k, s ^ m) for k, m in enumerate((0, 1, 2))]
        put(0, near, sum(dot(acts[j], wout_ref[j, k], 1, 0) for k, j in three))
        put(0, far, dot(acts[s], wout_ref[s, 3], 1, 0))
        put(SLICE, near, sum(dot(dpres[j], win_ref[j, k], 1, 1) for k, j in three))
        put(SLICE, far, dot(dpres[s], win_ref[s, 3], 1, 1))


def sort_kernel(table, got_ref, out_ref):
    chips = got_ref.shape[0]
    for group in range(chips // 2):
        for slot in range(8):
            for row, column in ((0, slot % 4 + 4), (SLICE, slot % 4)):
                block = table[2 * group + slot // 4, column]
                owner = lax.shift_right_logical(block, 1)
                half = pl.multiple_of((block & 1) * SIDE, SIDE)
                rows = pl.ds(row, SLICE)
                total = got_ref[group, slot, rows, :].astype(F32)
                total = total + got_ref[group + chips // 2, slot, rows, :].astype(F32)
                out_ref[owner, rows, pl.ds(half, SIDE)] = total.astype(BF16)


def shards(tokens, cotangent, w_in, w_out, in_blocks, out_blocks):
    n = lax.axis_size("mp")
    n_dp = lax.axis_size("dp")
    zs = n_dp // 2
    tok = tokens.shape[0]
    total_tok = tok * n_dp
    mate = [(i, i ^ 1) for i in range(n)]
    same_core = [[2 * chip + core for chip in range(n // 2)] for core in range(2)]

    packed = pl.pallas_call(
        pack_kernel,
        out_shape=jax.ShapeDtypeStruct((n, 2 * SLICE, 2 * SIDE + 128), BF16),
        in_specs=[ANY] * 4,
        out_specs=VMEM,
        scratch_shapes=[pltpu.VMEM((2, 4, 4), jnp.int32), pltpu.SemaphoreType.DMA((4,))],
        compiler_params=params(),
        name="pack",
    )(
        tokens.reshape(n, SLICE, 2 * SIDE),
        cotangent.reshape(n, SLICE, 2 * SIDE),
        in_blocks,
        out_blocks,
    )
    got = lax.all_to_all(packed, "mp", 0, 0, tiled=True)
    share = jax.ShapeDtypeStruct((n // 2, 8, 2 * SLICE, SIDE), BF16)
    chosen, table = pl.pallas_call(
        select_kernel,
        out_shape=(share, jax.ShapeDtypeStruct((n, 128), jnp.int32)),
        in_specs=[VMEM],
        out_specs=(VMEM, VMEM),
        scratch_shapes=[pltpu.SMEM((n, 128), jnp.int32), pltpu.SemaphoreType.DMA],
        compiler_params=params(),
        name="select",
    )(got)
    own = lax.all_to_all(chosen, "mp", 0, 0, axis_index_groups=same_core, tiled=True)
    oth = lax.ppermute(own, "mp", mate)

    quad = jax.ShapeDtypeStruct((tok, QUAD), BF16)
    grads, act, d_pre = pl.pallas_call(
        hidden_kernel,
        out_shape=(jax.ShapeDtypeStruct((zs, 2, 2, 4, 4, SLICE, SIDE), BF16), quad, quad),
        in_specs=[VMEM] * 4,
        out_specs=(ANY, VMEM, VMEM),
        scratch_shapes=[
            pltpu.VMEM((4, zs, 2, 2, 4, SLICE, SIDE), BF16),
            pltpu.SemaphoreType.DMA((4,)),
        ],
        compiler_params=params(),
        name="hidden",
    )(own, oth, w_in, w_out)

    columns = [[z * 2 + xl for z in range(zs)] for xl in range(2)]
    grad_sum = lax.psum_scatter(
        grads.reshape(-1, SIDE), "dp", scatter_dimension=0, axis_index_groups=columns, tiled=True
    )

    part_own, part_oth = pl.pallas_call(
        project_kernel,
        out_shape=(share, share),
        in_specs=[VMEM] * 4,
        out_specs=(VMEM, VMEM),
        compiler_params=params(),
        name="project",
    )(act, d_pre, w_in, w_out)
    part_mate = lax.ppermute(part_oth, "mp", mate)
    part = (part_own.astype(F32) + part_mate.astype(F32)).astype(BF16)
    slices = lax.all_to_all(part, "mp", 0, 0, axis_index_groups=same_core, tiled=True)
    sorted_ = pl.pallas_call(
        sort_kernel,
        out_shape=jax.ShapeDtypeStruct((n, 2 * SLICE, 2 * SIDE), BF16),
        in_specs=[SMEM, VMEM],
        out_specs=VMEM,
        compiler_params=params(),
        name="sort",
    )(table, slices)
    final = lax.all_to_all(sorted_, "mp", 0, 0, tiled=True)
    output = final[:, :SLICE].reshape(tok, 2 * SIDE)
    grad_tokens = final[:, SLICE:].reshape(tok, 2 * SIDE)

    grad_sum, output, grad_tokens = lax.optimization_barrier((grad_sum, output, grad_tokens))
    halves = grad_sum.reshape(2, 2, 4, 4, SLICE, SIDE)
    came = lax.ppermute(halves[1], "dp", [(i, i ^ 1) for i in range(n_dp)])
    scale = 1.0 / math.sqrt(total_tok)
    both = (halves[0].astype(F32) + came.astype(F32)) * scale
    return output, grad_tokens, both[0], both[1]


def solution(mesh):
    placed = (
        P("dp", "mp"),
        P("dp", "mp"),
        P("mp", None, None, None),
        P("mp", None, None, None),
        P("mp", None),
        P("mp", None),
    )
    return jax.shard_map(
        shards,
        mesh=mesh,
        in_specs=placed,
        out_specs=(
            P("dp", "mp"),
            P("dp", "mp"),
            P("mp", None, "dp", None),
            P("mp", None, "dp", None),
        ),
        check_vma=False,
    )
```

time: 135 us -> 133 us (0.985)
  blocking collectives: 61.5 us -> 74.9 us
  waiting for transfers between devices: 31.3 us -> 22.5 us
  Pallas kernels: 12.4 us -> 7.58 us
  starting transfers between devices: 7.47 us -> 3.59 us
  local copies, waits for them, and re-layouts: 5.88 us -> 9.52 us
    all_to_all x2 -> x3, blocking collectives: 39.9 us -> 53.2 us  [the longest x1 18.9 us: shards(): lax.all_to_all(part, 'mp', 0, 0, axis_index_groups=same_core, tiled=True)]
    reduce_scatter x1, waiting for transfers between devices: 21.5 us -> 11.9 us  [shards(): lax.psum_scatter(grads.reshape(-1, SIDE), 'dp', scatter_dimension=0, axis...]
    all_to_all x1 -> x0, starting transfers between devices: 4.53 us -> none  [shards(): final = lax.all_to_all(sorted_, 'mp', 0, 0, tiled=True)]
    unnamed x10 -> x16, local copies, waits for them, and re-layouts: 3.26 us -> 6.81 us
    pallas_call x4, Pallas kernels: 9.58 us -> 6.31 us  [the longest x1 4.38 us: shards(): pl.pallas_call(hidden_kernel, out_shape=(jax.ShapeDtypeStruct((zs, 2, 2,...]
    pallas_call x1, Pallas kernels: 2.85 us -> 1.26 us  [shards(): pl.pallas_call(project_kernel, out_shape=(share, share), in_specs=[VMEM]...]
  transfers between devices with their start and end apart: 5 -> 4, of which waited for: 4 -> 4; matrix products, arithmetic and copies ran while one was open for 2% -> 1% of each run, Pallas kernels for 3% -> 2%
where the time goes in v2:
time: 133 us
  blocking collectives  74.9 us (56%)
  waiting for transfers between devices  22.5 us (17%)
  between operations  14.1 us (11%)
  local copies, waits for them, and re-layouts  9.52 us (7%)
  Pallas kernels  7.58 us (6%)
  starting transfers between devices  3.59 us (3%)
    all_to_all x1, blocking collectives, shards(): got = lax.all_to_all(packed, 'mp', 0, 0, tiled=True)  21.8 us
    all_to_all x1, blocking collectives, shards(): lax.all_to_all(part, 'mp', 0, 0, axis_index_groups=same_core, tiled=True)  18.9 us
    all_to_all x1, blocking collectives, shards(): lax.all_to_all(chosen, 'mp', 0, 0, axis_index_groups=same_core, tiled=True)  18.8 us
    all_to_all x1, blocking collectives, shards(): final = lax.all_to_all(sorted_, 'mp', 0, 0, tiled=True)  15.5 us
    reduce_scatter x1, waiting for transfers between devices, shards(): lax.psum_scatter(grads.reshape(-1, SIDE), 'dp', scatter_dimension=0, axis...  11.9 us
    unnamed x16, local copies, waits for them, and re-layouts  6.81 us
    ppermute x1, waiting for transfers between devices, shards(): came = lax.ppermute(halves[1], 'dp', [(i, i ^ 1) for i in range(n_dp)])  6.08 us
    pallas_call x1, Pallas kernels, shards(): pl.pallas_call(hidden_kernel, out_shape=(jax.ShapeDtypeStruct((zs, 2, 2,...  4.38 us
  transfers between devices with their start and end apart: 4, of which 4 were waited for; matrix products, arithmetic and copies ran while one was open for 1% of the time, Pallas kernels for 2%

profile of v2, /device:TPU:1, one launch (start us, length us, event | category | flops | bytes accessed | tf_op | source)
XLA Modules:
  0.0 132.8 jit_solution(3919682417600432638)
XLA Ops:
  7.2 0.0 reduce-scatter.2.cloned.1.call-start
  7.2 0.0 copy-start.4
  7.2 0.9 copy-done.4
  8.2 0.0 copy-start.5
  8.2 0.9 copy-done.5
  9.1 0.0 copy-start.6
  9.1 0.7 copy-done.6
  9.8 0.0 copy-start.7
  9.8 0.7 copy-done.7
  10.5 0.0 copy-start.1
  10.5 0.3 pack.1
  10.7 0.0 copy-start
  10.8 21.8 %all_to_all.20.got_ref = bf16[16,32,640]{2,1,0:T(8,128)(2,1)S(1)} all-to-all(bf16[16,32,640]{2,1,0:T(8,128)(2,1)S(1)} %pack.1), channel_id=1, replica_groups=mesh['dp'=16,'mp'=16] {'mp'}, dimensions={0} | all-to-all | bytes 1310720 | tf_op jit(solution)/shard_map/all_to_all | solution.py:165
  32.5 0.9 select.1
  33.4 18.8 %all_to_all.21.own_ref = bf16[8,8,32,256]{3,2,1,0:T(8,128)(2,1)S(1)} all-to-all(bf16[8,8,32,256]{3,2,1,0:T(8,128)(2,1)S(1)} %get-tuple-element.14), channel_id=1, replica_groups={{0,2,4,6,8,10,12,14},{1,3,5,7,9,11,13,15},{16,18,20,22,24,26,28,30},{17..., dimensions={0} | all-to-all | bytes 2097152 | tf_op jit(solution)/shard_map/all_to_all | solution.py:176
  52.1 1.8 %collective-permute-start = (bf16[8,8,32,256]{3,2,1,0:T(8,128)(2,1)S(1)}, bf16[8,8,32,256]{3,2,1,0:T(8,128)(2,1)S(1)}, u32[]{:S(2)}, u32[]{:S(2)}) collective-permute-start(bf16[8,8,32,256]{3,2,1,0:T(8,128)(2,1)S(1)} %all_to_all.21.own_ref), channel_id=1, source_target_pairs={{0,1},{1,0},{2,3},{3,2},{4,5},{5,4},{6,7},{7,6},{8,9},{9,8},{10,11... | collective-permute-start | bytes 3145736 | tf_op jit(solution)/shard_map/ppermute | solution.py:177
  54.0 2.3 %collective-permute-done.oth_ref = bf16[8,8,32,256]{3,2,1,0:T(8,128)(2,1)S(1)} collective-permute-done((bf16[8,8,32,256]{3,2,1,0:T(8,128)(2,1)S(1)}, bf16[8,8,32,256]{3,2,1,0:T(8,128)(2,1)S(1)}, u32[]{:S(2)}, u32[]{:S(2)}) %collective-permute-start) | collective-permute-done | bytes 1048608 | tf_op jit(solution)/shard_map/ppermute | solution.py:177
  56.3 0.0 copy-done.1
  56.3 0.0 copy-done
  56.3 4.4 %hidden.1 = (bf16[8,2,2,4,4,16,256]{6,5,4,3,2,1,0:T(8,128)(2,1)S(1)}, bf16[256,1024]{1,0:T(8,128)(2,1)S(1)}, bf16[256,1024]{1,0:T(8,128)(2,1)S(1)}) custom-call(bf16[8,8,32,256]{3,2,1,0:T(8,128)(2,1)S(1)} %all_to_all.21.own_ref, bf16[8,8,32,256]{3,2,1,0:T(8,128)(2,1)S(1)} %collective-permute-done.oth_ref, bf16[4,4,256,256]{3,2,1,0:T(8,128)(2,1)S(1)} %copy-done, ...), custom_call_target="tpu_custom_call" | custom-call | tf_op jit(solution)/shard_map/hidden/pallas_call | solution.py:180
  60.7 0.0 copy-start.3
  60.7 2.0 %copy-done.3 = bf16[8,2,2,4,4,16,256]{6,5,4,3,2,1,0:T(8,128)(2,1)} copy-done((bf16[8,2,2,4,4,16,256]{6,5,4,3,2,1,0:T(8,128)(2,1)}, bf16[8,2,2,4,4,16,256]{6,5,4,3,2,1,0:T(8,128)(2,1)S(1)}, u32[]{:S(2)}) %copy-start.3) | copy-done | bytes 4194328
  62.6 0.0 reduce-scatter.2.cloned.1.call-update
  62.6 0.0 copy-start.2
  62.7 1.6 %copy-done.2 = bf16[4,4,256,256]{3,2,1,0:T(8,128)(2,1)S(1)} copy-done((bf16[4,4,256,256]{3,2,1,0:T(8,128)(2,1)S(1)}, bf16[4,4,256,256]{3,2,1,0:T(8,128)(2,1)}, u32[]{:S(2)}) %copy-start.2) | copy-done | bytes 2097176
  64.2 1.3 project.1
  65.5 0.5 collective-permute-start.1
  66.0 2.3 %collective-permute-done.1 = bf16[8,8,32,256]{3,2,1,0:T(8,128)(2,1)S(1)} collective-permute-done((bf16[8,8,32,256]{3,2,1,0:T(8,128)(2,1)S(1)}, bf16[8,8,32,256]{3,2,1,0:T(8,128)(2,1)S(1)}, u32[]{:S(2)}, u32[]{:S(2)}) %collective-permute-start.1) | collective-permute-done | bytes 1048608 | tf_op jit(solution)/shard_map/ppermute | solution.py:206
  68.3 0.4 add_convert_fusion
  68.7 18.9 %all_to_all.22.got_ref = bf16[8,8,32,256]{3,2,1,0:T(8,128)(2,1)S(1)} all-to-all(bf16[8,8,32,256]{3,2,1,0:T(8,128)(2,1)S(1)} %add_convert_fusion), channel_id=1, replica_groups={{0,2,4,6,8,10,12,14},{1,3,5,7,9,11,13,15},{16,18,20,22,24,26,28,30},{17..., dimensions={0} | all-to-all | bytes 2097152 | tf_op jit(solution)/shard_map/all_to_all | solution.py:208
  87.7 0.8 sort.1
  88.5 15.5 %all_to_all.23 = bf16[16,32,512]{2,1,0:T(8,128)(2,1)S(1)} all-to-all(bf16[16,32,512]{2,1,0:T(8,128)(2,1)S(1)} %sort.1), channel_id=1, replica_groups=mesh['dp'=16,'mp'=16] {'mp'}, dimensions={0} | all-to-all | bytes 1048576 | tf_op jit(solution)/shard_map/all_to_all | solution.py:217
  103.9 0.8 fusion.2
  104.8 11.9 %reduce-scatter.2.cloned.1.call-done = bf16[1024,256]{1,0:T(8,128)(2,1)} async-done(((bf16[8192,256]{1,0:T(8,128)(2,1)}), bf16[1024,256]{1,0:T(8,128)(2,1)}) %reduce-scatter.2.cloned.1.call-update) | async-done | bytes 524304 | tf_op jit(solution)/shard_map/reduce_scatter | solution.py:194
  116.6 1.1 fusion.1
  117.7 1.3 collective-permute-start.2
  119.0 6.1 %collective-permute-done.2 = bf16[2,4,4,16,256]{4,3,2,1,0:T(8,128)(2,1)S(1)} collective-permute-done((bf16[2,4,4,16,256]{4,3,2,1,0:T(8,128)(2,1)S(1)}, bf16[2,4,4,16,256]{4,3,2,1,0:T(8,128)(2,1)S(1)}, u32[]{:S(2)}, u32[]{:S(2)}) %collective-permute-start.2) | collective-permute-done | bytes 262176 | tf_op jit(solution)/shard_map/ppermute | solution.py:223
  125.0 0.1 fusion
  125.1 0.8 slice_bitcast_fusion
Async XLA Ops:
  7.2 109.5 %reduce-scatter.2.cloned.1.call-start = ((), (), s32[]{:S(2)}) async-start(), calls=%async_computation.5 | async-start | bytes 4718592 | tf_op jit(solution)/shard_map/reduce_scatter | solution.py:194
  7.2 1.0 copy-start.4
  8.2 0.9 copy-start.5
  9.1 0.7 copy-start.6
  9.8 0.7 copy-start.7
  10.5 45.8 %copy-start.1 = (bf16[4,4,256,256]{3,2,1,0:T(8,128)(2,1)S(1)}, bf16[4,4,256,256]{3,2,1,0:T(8,128)(2,1)}, u32[]{:S(2)}) copy-start(bf16[4,4,256,256]{3,2,1,0:T(8,128)(2,1)} %wout_ref.3) | copy-start | bytes 6291460
  10.7 45.5 %copy-start = (bf16[4,4,256,256]{3,2,1,0:T(8,128)(2,1)S(1)}, bf16[4,4,256,256]{3,2,1,0:T(8,128)(2,1)}, u32[]{:S(2)}) copy-start(bf16[4,4,256,256]{3,2,1,0:T(8,128)(2,1)} %win_ref.3) | copy-start | bytes 6291460
  52.1 4.1 %collective-permute-start = (bf16[8,8,32,256]{3,2,1,0:T(8,128)(2,1)S(1)}, bf16[8,8,32,256]{3,2,1,0:T(8,128)(2,1)S(1)}, u32[]{:S(2)}, u32[]{:S(2)}) collective-permute-start(bf16[8,8,32,256]{3,2,1,0:T(8,128)(2,1)S(1)} %all_to_all.21.own_ref), channel_id=1, source_target_pairs={{0,1},{1,0},{2,3},{3,2},{4,5},{5,4},{6,7},{7,6},{8,9},{9,8},{10,11... | collective-permute-start | bytes 3145736 | tf_op jit(solution)/shard_map/ppermute | solution.py:177
  60.7 2.0 %copy-start.3 = (bf16[8,2,2,4,4,16,256]{6,5,4,3,2,1,0:T(8,128)(2,1)}, bf16[8,2,2,4,4,16,256]{6,5,4,3,2,1,0:T(8,128)(2,1)S(1)}, u32[]{:S(2)}) copy-start(bf16[8,2,2,4,4,16,256]{6,5,4,3,2,1,0:T(8,128)(2,1)S(1)} %get-tuple-element.15) | copy-start | bytes 12582916
  62.6 1.6 %copy-start.2 = (bf16[4,4,256,256]{3,2,1,0:T(8,128)(2,1)S(1)}, bf16[4,4,256,256]{3,2,1,0:T(8,128)(2,1)}, u32[]{:S(2)}) copy-start(bf16[4,4,256,256]{3,2,1,0:T(8,128)(2,1)} %wout_ref.3) | copy-start | bytes 6291460
  65.5 2.7 %collective-permute-start.1 = (bf16[8,8,32,256]{3,2,1,0:T(8,128)(2,1)S(1)}, bf16[8,8,32,256]{3,2,1,0:T(8,128)(2,1)S(1)}, u32[]{:S(2)}, u32[]{:S(2)}) collective-permute-start(bf16[8,8,32,256]{3,2,1,0:T(8,128)(2,1)S(1)} %get-tuple-element.20), channel_id=1, source_target_pairs={{0,1},{1,0},{2,3},{3,2},{4,5},{5,4},{6,7},{7,6},{8,9},{9,8},{10,11... | collective-permute-start | bytes 3145736 | tf_op jit(solution)/shard_map/ppermute | solution.py:206
  117.7 7.4 %collective-permute-start.2 = (bf16[2,4,4,16,256]{4,3,2,1,0:T(8,128)(2,1)S(1)}, bf16[2,4,4,16,256]{4,3,2,1,0:T(8,128)(2,1)S(1)}, u32[]{:S(2)}, u32[]{:S(2)}) collective-permute-start(bf16[2,4,4,16,256]{4,3,2,1,0:T(8,128)(2,1)S(1)} %bitcast.18), channel_id=1, source_target_pairs={{0,16},{16,0},{32,48},{48,32},{64,80},{80,64},{96,112},{112,96},{1... | collective-permute-start | bytes 786440 | tf_op jit(solution)/shard_map/ppermute | solution.py:223
Sparse Core Ops, SparseCore 0:
  62.8 53.8 reduce-scatter.1

commit v3 on v2

--- a/solution.py
+++ b/solution.py
@@ -1,3 +1,4 @@
+import functools
 import math
 
 import jax
@@ -10,42 +11,51 @@
 SIDE = 256
 QUAD = 4 * SIDE
 SLICE = 16
+LANES = 128
+TILES = 2 * SIDE // LANES
 VMEM = pl.BlockSpec(memory_space=pltpu.VMEM)
-ANY = pl.BlockSpec(memory_space=pl.ANY)
+HBM = pl.BlockSpec(memory_space=pltpu.HBM)
 SMEM = pl.BlockSpec(memory_space=pltpu.SMEM)
 BF16 = jnp.bfloat16
 F32 = jnp.float32
 
 
+def in_hbm(array):
+    return pltpu.with_memory_space_constraint(array, pltpu.HBM)
+
+
 def params():
     return pltpu.CompilerParams(vmem_limit_bytes=40 * 1024 * 1024)
 
 
 def pack_kernel(x_ref, dy_ref, p_ref, q_ref, out_ref, lists, sems):
-    features = pl.ds(0, 2 * SIDE)
     copies = [
         pltpu.make_async_copy(p_ref, lists.at[0], sems.at[0]),
         pltpu.make_async_copy(q_ref, lists.at[1], sems.at[1]),
-        pltpu.make_async_copy(x_ref, out_ref.at[:, pl.ds(0, SLICE), features], sems.at[2]),
-        pltpu.make_async_copy(dy_ref, out_ref.at[:, pl.ds(SLICE, SLICE), features], sems.at[3]),
     ]
+    for part, ref in enumerate((x_ref, dy_ref)):
+        for tile in range(TILES):
+            at = part * TILES + tile
+            source = ref.at[:, :, pl.ds(tile * LANES, LANES)]
+            target = out_ref.at[:, pl.ds(at * SLICE, SLICE), :]
+            copies.append(pltpu.make_async_copy(source, target, sems.at[2 + at]))
     for copy in copies:
         copy.start()
-    row = lax.broadcasted_iota(jnp.int32, (4, 128), 0)
-    lane = lax.broadcasted_iota(jnp.int32, (4, 128), 1)
-    total = jnp.zeros((1, 128), F32)
+    row = lax.broadcasted_iota(jnp.int32, (4, LANES), 0)
+    lane = lax.broadcasted_iota(jnp.int32, (4, LANES), 1)
+    total = jnp.zeros((1, LANES), F32)
     for part in range(2):
         copies[part].wait()
-        column = jnp.broadcast_to(lists[part][:, 0:1], (4, 128)).astype(F32)
+        column = jnp.broadcast_to(lists[part][:, 0:1], (4, LANES)).astype(F32)
         total = total + jnp.sum(jnp.where(lane == row + 4 * part, column, 0.0), axis=0, keepdims=True)
-    tail = out_ref.shape[:2] + (128,)
-    out_ref[:, :, 2 * SIDE :] = jnp.broadcast_to(total[None], tail).astype(BF16)
-    copies[2].wait()
-    copies[3].wait()
+    shape = (out_ref.shape[0], SLICE, LANES)
+    out_ref[:, pl.ds(2 * TILES * SLICE, SLICE), :] = jnp.broadcast_to(total[None], shape).astype(BF16)
+    for copy in copies[2:]:
+        copy.wait()
 
 
 def select_kernel(got_ref, out_ref, lists_ref, table, sem):
-    lists = jnp.max(got_ref[:, :SLICE, 2 * SIDE :].astype(F32), axis=1).astype(jnp.int32)
+    lists = jnp.max(got_ref[:, pl.ds(2 * TILES * SLICE, SLICE), :].astype(F32), axis=1).astype(jnp.int32)
     lists_ref[...] = lists
     copy = pltpu.make_async_copy(lists_ref, table, sem)
     copy.start()
@@ -56,10 +66,13 @@
             for row, column in ((0, slot % 4), (SLICE, slot % 4 + 4)):
                 block = table[2 * group + slot // 4, column]
                 owner = lax.shift_right_logical(block, 1)
-                half = pl.multiple_of((block & 1) * SIDE, SIDE)
-                piece = got_ref[owner, pl.ds(row, SLICE), pl.ds(half, SIDE)]
-                out_ref[group, slot, pl.ds(row, SLICE), :] = piece
-                out_ref[group + chips // 2, slot, pl.ds(row, SLICE), :] = piece
+                first = row * TILES + (block & 1) * (2 * SLICE)
+                for tile in range(2):
+                    rows = pl.ds(pl.multiple_of(first + tile * SLICE, SLICE), SLICE)
+                    piece = got_ref[owner, rows, :]
+                    lanes = pl.ds(tile * LANES, LANES)
+                    out_ref[group, slot, pl.ds(row, SLICE), lanes] = piece
+                    out_ref[group + chips // 2, slot, pl.ds(row, SLICE), lanes] = piece
 
 
 def dot(a, b, da, db):
@@ -139,6 +152,11 @@
                 out_ref[owner, rows, pl.ds(half, SIDE)] = total.astype(BF16)
 
 
+def finish_kernel(scale, own_ref, came_ref, in_ref, out_ref):
+    for which, ref in enumerate((in_ref, out_ref)):
+        ref[...] = (own_ref[0, which].astype(F32) + came_ref[which].astype(F32)) * scale
+
+
 def shards(tokens, cotangent, w_in, w_out, in_blocks, out_blocks):
     n = lax.axis_size("mp")
     n_dp = lax.axis_size("dp")
@@ -150,26 +168,26 @@
 
     packed = pl.pallas_call(
         pack_kernel,
-        out_shape=jax.ShapeDtypeStruct((n, 2 * SLICE, 2 * SIDE + 128), BF16),
-        in_specs=[ANY] * 4,
+        out_shape=jax.ShapeDtypeStruct((n, (2 * TILES + 1) * SLICE, LANES), BF16),
+        in_specs=[HBM] * 4,
         out_specs=VMEM,
-        scratch_shapes=[pltpu.VMEM((2, 4, 4), jnp.int32), pltpu.SemaphoreType.DMA((4,))],
+        scratch_shapes=[pltpu.VMEM((2, 4, 4), jnp.int32), pltpu.SemaphoreType.DMA((2 + 2 * TILES,))],
         compiler_params=params(),
         name="pack",
     )(
-        tokens.reshape(n, SLICE, 2 * SIDE),
-        cotangent.reshape(n, SLICE, 2 * SIDE),
-        in_blocks,
-        out_blocks,
+        in_hbm(tokens.reshape(n, SLICE, 2 * SIDE)),
+        in_hbm(cotangent.reshape(n, SLICE, 2 * SIDE)),
+        in_hbm(in_blocks),
+        in_hbm(out_blocks),
     )
     got = lax.all_to_all(packed, "mp", 0, 0, tiled=True)
     share = jax.ShapeDtypeStruct((n // 2, 8, 2 * SLICE, SIDE), BF16)
     chosen, table = pl.pallas_call(
         select_kernel,
-        out_shape=(share, jax.ShapeDtypeStruct((n, 128), jnp.int32)),
+        out_shape=(share, jax.ShapeDtypeStruct((n, LANES), jnp.int32)),
         in_specs=[VMEM],
         out_specs=(VMEM, VMEM),
-        scratch_shapes=[pltpu.SMEM((n, 128), jnp.int32), pltpu.SemaphoreType.DMA],
+        scratch_shapes=[pltpu.SMEM((n, LANES), jnp.int32), pltpu.SemaphoreType.DMA],
         compiler_params=params(),
         name="select",
     )(got)
@@ -179,9 +197,9 @@
     quad = jax.ShapeDtypeStruct((tok, QUAD), BF16)
     grads, act, d_pre = pl.pallas_call(
         hidden_kernel,
-        out_shape=(jax.ShapeDtypeStruct((zs, 2, 2, 4, 4, SLICE, SIDE), BF16), quad, quad),
+        out_shape=(pltpu.HBM((zs, 2, 2, 4, 4, SLICE, SIDE), BF16), quad, quad),
         in_specs=[VMEM] * 4,
-        out_specs=(ANY, VMEM, VMEM),
+        out_specs=(HBM, VMEM, VMEM),
         scratch_shapes=[
             pltpu.VMEM((4, zs, 2, 2, 4, SLICE, SIDE), BF16),
             pltpu.SemaphoreType.DMA((4,)),
@@ -221,9 +239,23 @@
     grad_sum, output, grad_tokens = lax.optimization_barrier((grad_sum, output, grad_tokens))
     halves = grad_sum.reshape(2, 2, 4, 4, SLICE, SIDE)
     came = lax.ppermute(halves[1], "dp", [(i, i ^ 1) for i in range(n_dp)])
-    scale = 1.0 / math.sqrt(total_tok)
-    both = (halves[0].astype(F32) + came.astype(F32)) * scale
-    return output, grad_tokens, both[0], both[1]
+    grad_shape = jax.ShapeDtypeStruct((4, 4, SLICE, SIDE), F32)
+    grad_in, grad_out = pl.pallas_call(
+        functools.partial(finish_kernel, 1.0 / math.sqrt(total_tok)),
+        grid=(1,),
+        out_shape=(grad_shape, grad_shape),
+        in_specs=[
+            pl.BlockSpec((1, 2, 4, 4, SLICE, SIDE), lambda i: (0,) * 6),
+            pl.BlockSpec((2, 4, 4, SLICE, SIDE), lambda i: (0,) * 5),
+        ],
+        out_specs=(
+            pl.BlockSpec((4, 4, SLICE, SIDE), lambda i: (0,) * 4),
+            pl.BlockSpec((4, 4, SLICE, SIDE), lambda i: (0,) * 4),
+        ),
+        compiler_params=params(),
+        name="finish",
+    )(in_hbm(halves), came)
+    return output, grad_tokens, grad_in, grad_out
 
 
 def solution(mesh):

time: 133 us -> 129 us (0.970)
  local copies, waits for them, and re-layouts: 9.52 us -> 3.39 us
  Pallas kernels: 7.58 us -> 10.6 us
    unnamed x16 -> x6, local copies, waits for them, and re-layouts: 6.81 us -> 1.6 us
    pallas_call x2 -> x3, Pallas kernels: 4.63 us -> 7.53 us  [the longest x1 4.41 us: shards(): pl.pallas_call(hidden_kernel, out_shape=(pltpu.HBM((zs, 2, 2, 4, 4, SLICE...]
where the time goes in v3:
time: 129 us
  blocking collectives  74.8 us (58%)
  waiting for transfers between devices  22.6 us (18%)
  between operations  14.1 us (11%)
  Pallas kernels  10.6 us (8%)
  local copies, waits for them, and re-layouts  3.39 us (3%)
  starting transfers between devices  3.04 us (2%)
    all_to_all x1, blocking collectives, shards(): got = lax.all_to_all(packed, 'mp', 0, 0, tiled=True)  21.1 us
    all_to_all x1, blocking collectives, shards(): lax.all_to_all(chosen, 'mp', 0, 0, axis_index_groups=same_core, tiled=True)  19.3 us
    all_to_all x1, blocking collectives, shards(): lax.all_to_all(part, 'mp', 0, 0, axis_index_groups=same_core, tiled=True)  19 us
    all_to_all x1, blocking collectives, shards(): final = lax.all_to_all(sorted_, 'mp', 0, 0, tiled=True)  15.4 us
    reduce_scatter x1, waiting for transfers between devices, shards(): lax.psum_scatter(grads.reshape(-1, SIDE), 'dp', scatter_dimension=0, axis...  11.9 us
    ppermute x1, waiting for transfers between devices, shards(): came = lax.ppermute(halves[1], 'dp', [(i, i ^ 1) for i in range(n_dp)])  6.08 us
    pallas_call x1, Pallas kernels, shards(): pl.pallas_call(hidden_kernel, out_shape=(pltpu.HBM((zs, 2, 2, 4, 4, SLICE...  4.41 us
  transfers between devices with their start and end apart: 4, of which 4 were waited for; matrix products, arithmetic and copies ran while one was open for 1% of the time, Pallas kernels for 2%

profile of v3, /device:TPU:1, one launch (start us, length us, event | category | flops | bytes accessed | tf_op | source)
XLA Modules:
  0.0 129.0 jit_solution(14481936936161414934)
XLA Ops:
  7.2 0.0 reduce-scatter.2.cloned.1.call-start
  7.2 0.0 copy-start.1
  7.2 1.3 %pack.1 = bf16[16,144,128]{2,1,0:T(8,128)(2,1)S(1)} custom-call(bf16[16,16,512]{2,1,0:T(8,128)(2,1)} %bitcast.9, bf16[16,16,512]{2,1,0:T(8,128)(2,1)} %bitcast.10, s32[4,4]{1,0:T(4,128)} %p_ref.1, s32[4,4]{1,0:T(4,128)} %q_ref.1), custom_call_target="tpu_custom_call" | custom-call | tf_op jit(solution)/shard_map/pack/pallas_call | solution.py:169
  8.6 0.0 copy-start
  8.6 21.1 %all_to_all.20.got_ref = bf16[16,144,128]{2,1,0:T(8,128)(2,1)S(1)} all-to-all(bf16[16,144,128]{2,1,0:T(8,128)(2,1)S(1)} %pack.1), channel_id=1, replica_groups=mesh['dp'=16,'mp'=16] {'mp'}, dimensions={0} | all-to-all | bytes 1179648 | tf_op jit(solution)/shard_map/all_to_all | solution.py:183
  29.7 1.0 select.1
  30.7 19.3 %all_to_all.21.own_ref = bf16[8,8,32,256]{3,2,1,0:T(8,128)(2,1)S(1)} all-to-all(bf16[8,8,32,256]{3,2,1,0:T(8,128)(2,1)S(1)} %get-tuple-element.16), channel_id=1, replica_groups={{0,2,4,6,8,10,12,14},{1,3,5,7,9,11,13,15},{16,18,20,22,24,26,28,30},{17..., dimensions={0} | all-to-all | bytes 2097152 | tf_op jit(solution)/shard_map/all_to_all | solution.py:194
  50.0 1.3 collective-permute-start
  51.3 2.3 %collective-permute-done.oth_ref = bf16[8,8,32,256]{3,2,1,0:T(8,128)(2,1)S(1)} collective-permute-done((bf16[8,8,32,256]{3,2,1,0:T(8,128)(2,1)S(1)}, bf16[8,8,32,256]{3,2,1,0:T(8,128)(2,1)S(1)}, u32[]{:S(2)}, u32[]{:S(2)}) %collective-permute-start) | collective-permute-done | bytes 1048608 | tf_op jit(solution)/shard_map/ppermute | solution.py:195
  53.6 0.0 copy-done.1
  53.6 0.0 copy-done
  53.6 4.4 %hidden.1 = (bf16[8,2,2,4,4,16,256]{6,5,4,3,2,1,0:T(8,128)(2,1)}, bf16[256,1024]{1,0:T(8,128)(2,1)S(1)}, bf16[256,1024]{1,0:T(8,128)(2,1)S(1)}) custom-call(bf16[8,8,32,256]{3,2,1,0:T(8,128)(2,1)S(1)} %all_to_all.21.own_ref, bf16[8,8,32,256]{3,2,1,0:T(8,128)(2,1)S(1)} %collective-permute-done.oth_ref, bf16[4,4,256,256]{3,2,1,0:T(8,128)(2,1)S(1)} %copy-done, ...), custom_call_target="tpu_custom_call" | custom-call | tf_op jit(solution)/shard_map/hidden/pallas_call | solution.py:198
  58.0 0.0 reduce-scatter.2.cloned.1.call-update
  58.1 0.0 copy-start.2
  58.1 1.6 %copy-done.2 = bf16[4,4,256,256]{3,2,1,0:T(8,128)(2,1)S(1)} copy-done((bf16[4,4,256,256]{3,2,1,0:T(8,128)(2,1)S(1)}, bf16[4,4,256,256]{3,2,1,0:T(8,128)(2,1)}, u32[]{:S(2)}) %copy-start.2) | copy-done | bytes 2097176
  59.6 1.3 project.1
  60.9 0.5 collective-permute-start.1
  61.4 2.3 %collective-permute-done.1 = bf16[8,8,32,256]{3,2,1,0:T(8,128)(2,1)S(1)} collective-permute-done((bf16[8,8,32,256]{3,2,1,0:T(8,128)(2,1)S(1)}, bf16[8,8,32,256]{3,2,1,0:T(8,128)(2,1)S(1)}, u32[]{:S(2)}, u32[]{:S(2)}) %collective-permute-start.1) | collective-permute-done | bytes 1048608 | tf_op jit(solution)/shard_map/ppermute | solution.py:224
  63.7 0.4 add_convert_fusion
  64.1 19.0 %all_to_all.22.got_ref = bf16[8,8,32,256]{3,2,1,0:T(8,128)(2,1)S(1)} all-to-all(bf16[8,8,32,256]{3,2,1,0:T(8,128)(2,1)S(1)} %add_convert_fusion), channel_id=1, replica_groups={{0,2,4,6,8,10,12,14},{1,3,5,7,9,11,13,15},{16,18,20,22,24,26,28,30},{17..., dimensions={0} | all-to-all | bytes 2097152 | tf_op jit(solution)/shard_map/all_to_all | solution.py:226
  83.1 0.8 sort.1
  83.9 15.4 %all_to_all.23 = bf16[16,32,512]{2,1,0:T(8,128)(2,1)S(1)} all-to-all(bf16[16,32,512]{2,1,0:T(8,128)(2,1)S(1)} %sort.1), channel_id=1, replica_groups=mesh['dp'=16,'mp'=16] {'mp'}, dimensions={0} | all-to-all | bytes 1048576 | tf_op jit(solution)/shard_map/all_to_all | solution.py:235
  99.3 0.8 fusion
  100.1 11.9 %reduce-scatter.2.cloned.1.call-done = bf16[1024,256]{1,0:T(8,128)(2,1)} async-done(((bf16[8192,256]{1,0:T(8,128)(2,1)}), bf16[1024,256]{1,0:T(8,128)(2,1)}) %reduce-scatter.2.cloned.1.call-update) | async-done | bytes 524304 | tf_op jit(solution)/shard_map/reduce_scatter | solution.py:212
  112.0 1.0 slice.12
  113.0 1.3 collective-permute-start.2
  114.3 6.1 %collective-permute-done.2.came_ref = bf16[2,4,4,16,256]{4,3,2,1,0:T(8,128)(2,1)S(1)} collective-permute-done((bf16[2,4,4,16,256]{4,3,2,1,0:T(8,128)(2,1)S(1)}, bf16[2,4,4,16,256]{4,3,2,1,0:T(8,128)(2,1)S(1)}, u32[]{:S(2)}, u32[]{:S(2)}) %collective-permute-start.2) | collective-permute-done | bytes 262176 | tf_op jit(solution)/shard_map/ppermute | solution.py:241
  120.3 1.8 %finish.1 = (f32[4,4,16,256]{3,2,1,0:T(8,128)}, f32[4,4,16,256]{3,2,1,0:T(8,128)}) custom-call(bf16[2,2,4,4,16,256]{5,4,3,2,1,0:T(8,128)(2,1)} %bitcast.8, bf16[2,4,4,16,256]{4,3,2,1,0:T(8,128)(2,1)S(1)} %collective-permute-done.2.came_ref), custom_call_target="tpu_custom_call" | custom-call | tf_op jit(solution)/shard_map/finish/pallas_call | solution.py:243
Async XLA Ops:
  7.2 104.9 %reduce-scatter.2.cloned.1.call-start = ((), (), s32[]{:S(2)}) async-start(), calls=%async_computation.5 | async-start | bytes 4718592 | tf_op jit(solution)/shard_map/reduce_scatter | solution.py:212
  7.2 46.4 %copy-start.1 = (bf16[4,4,256,256]{3,2,1,0:T(8,128)(2,1)S(1)}, bf16[4,4,256,256]{3,2,1,0:T(8,128)(2,1)}, u32[]{:S(2)}) copy-start(bf16[4,4,256,256]{3,2,1,0:T(8,128)(2,1)} %wout_ref.3) | copy-start | bytes 6291460
  8.6 45.0 %copy-start = (bf16[4,4,256,256]{3,2,1,0:T(8,128)(2,1)S(1)}, bf16[4,4,256,256]{3,2,1,0:T(8,128)(2,1)}, u32[]{:S(2)}) copy-start(bf16[4,4,256,256]{3,2,1,0:T(8,128)(2,1)} %win_ref.3) | copy-start | bytes 6291460
  50.0 3.6 %collective-permute-start = (bf16[8,8,32,256]{3,2,1,0:T(8,128)(2,1)S(1)}, bf16[8,8,32,256]{3,2,1,0:T(8,128)(2,1)S(1)}, u32[]{:S(2)}, u32[]{:S(2)}) collective-permute-start(bf16[8,8,32,256]{3,2,1,0:T(8,128)(2,1)S(1)} %all_to_all.21.own_ref), channel_id=1, source_target_pairs={{0,1},{1,0},{2,3},{3,2},{4,5},{5,4},{6,7},{7,6},{8,9},{9,8},{10,11... | collective-permute-start | bytes 3145736 | tf_op jit(solution)/shard_map/ppermute | solution.py:195
  58.1 1.6 %copy-start.2 = (bf16[4,4,256,256]{3,2,1,0:T(8,128)(2,1)S(1)}, bf16[4,4,256,256]{3,2,1,0:T(8,128)(2,1)}, u32[]{:S(2)}) copy-start(bf16[4,4,256,256]{3,2,1,0:T(8,128)(2,1)} %wout_ref.3) | copy-start | bytes 6291460
  60.9 2.8 %collective-permute-start.1 = (bf16[8,8,32,256]{3,2,1,0:T(8,128)(2,1)S(1)}, bf16[8,8,32,256]{3,2,1,0:T(8,128)(2,1)S(1)}, u32[]{:S(2)}, u32[]{:S(2)}) collective-permute-start(bf16[8,8,32,256]{3,2,1,0:T(8,128)(2,1)S(1)} %get-tuple-element.22), channel_id=1, source_target_pairs={{0,1},{1,0},{2,3},{3,2},{4,5},{5,4},{6,7},{7,6},{8,9},{9,8},{10,11... | collective-permute-start | bytes 3145736 | tf_op jit(solution)/shard_map/ppermute | solution.py:224
  113.0 7.3 %collective-permute-start.2 = (bf16[2,4,4,16,256]{4,3,2,1,0:T(8,128)(2,1)S(1)}, bf16[2,4,4,16,256]{4,3,2,1,0:T(8,128)(2,1)S(1)}, u32[]{:S(2)}, u32[]{:S(2)}) collective-permute-start(bf16[2,4,4,16,256]{4,3,2,1,0:T(8,128)(2,1)S(1)} %bitcast.11), channel_id=1, source_target_pairs={{0,16},{16,0},{32,48},{48,32},{64,80},{80,64},{96,112},{112,96},{1... | collective-permute-start | bytes 786440 | tf_op jit(solution)/shard_map/ppermute | solution.py:241
Sparse Core Ops, SparseCore 0:
  58.2 53.8 reduce-scatter.1

commit v4 on v3

--- a/solution.py
+++ b/solution.py
@@ -106,15 +106,15 @@
         d_pre = (d_act * slope).astype(BF16)
         act_ref[:, j * SIDE : (j + 1) * SIDE] = act
         dpre_ref[:, j * SIDE : (j + 1) * SIDE] = d_pre
-        zs = held.shape[1]
+        zs = held.shape[2]
         for k in range(4):
             g_in = dot(xs[k], d_pre, 0, 0).astype(BF16).reshape(zs, 2, SLICE, SIDE)
             g_out = dot(act, dys[k], 0, 0).astype(BF16).reshape(zs, 2, SLICE, SIDE)
             for away in range(2):
-                held[j, :, away ^ side, 0, k] = g_in[:, away]
-                held[j, :, away ^ side, 1, k] = g_out[:, away]
-        copies.append(pltpu.make_async_copy(held.at[j], grads_ref.at[:, :, :, j], sems.at[j]))
-        copies[-1].start()
+                held[j, k, :, away ^ side, 0] = g_in[:, away]
+                held[j, k, :, away ^ side, 1] = g_out[:, away]
+            copies.append(pltpu.make_async_copy(held.at[j, k], grads_ref.at[:, :, :, j, k], sems.at[j, k]))
+            copies[-1].start()
     for copy in copies:
         copy.wait()
 
@@ -152,9 +152,25 @@
                 out_ref[owner, rows, pl.ds(half, SIDE)] = total.astype(BF16)
 
 
-def finish_kernel(scale, own_ref, came_ref, in_ref, out_ref):
+def fetch_kernel(sum_ref, own_ref, away_ref, sems):
+    copies = [
+        pltpu.make_async_copy(sum_ref.at[half], ref, sems.at[half])
+        for half, ref in enumerate((own_ref, away_ref))
+    ]
+    for copy in copies:
+        copy.start()
+    for copy in copies:
+        copy.wait()
+
+
+def finish_kernel(scale, own_ref, came_ref, in_ref, out_ref, held, sems):
+    copies = []
     for which, ref in enumerate((in_ref, out_ref)):
-        ref[...] = (own_ref[0, which].astype(F32) + came_ref[which].astype(F32)) * scale
+        held[which] = (own_ref[which].astype(F32) + came_ref[which].astype(F32)) * scale
+        copies.append(pltpu.make_async_copy(held.at[which], ref, sems.at[which]))
+        copies[-1].start()
+    for copy in copies:
+        copy.wait()
 
 
 def shards(tokens, cotangent, w_in, w_out, in_blocks, out_blocks):
@@ -201,8 +217,8 @@
         in_specs=[VMEM] * 4,
         out_specs=(HBM, VMEM, VMEM),
         scratch_shapes=[
-            pltpu.VMEM((4, zs, 2, 2, 4, SLICE, SIDE), BF16),
-            pltpu.SemaphoreType.DMA((4,)),
+            pltpu.VMEM((4, 4, zs, 2, 2, SLICE, SIDE), BF16),
+            pltpu.SemaphoreType.DMA((4, 4)),
         ],
         compiler_params=params(),
         name="hidden",
@@ -238,23 +254,30 @@
 
     grad_sum, output, grad_tokens = lax.optimization_barrier((grad_sum, output, grad_tokens))
     halves = grad_sum.reshape(2, 2, 4, 4, SLICE, SIDE)
-    came = lax.ppermute(halves[1], "dp", [(i, i ^ 1) for i in range(n_dp)])
-    grad_shape = jax.ShapeDtypeStruct((4, 4, SLICE, SIDE), F32)
+    half = jax.ShapeDtypeStruct((2, 4, 4, SLICE, SIDE), BF16)
+    mine, away = pl.pallas_call(
+        fetch_kernel,
+        out_shape=(half, half),
+        in_specs=[HBM],
+        out_specs=(VMEM, VMEM),
+        scratch_shapes=[pltpu.SemaphoreType.DMA((2,))],
+        compiler_params=params(),
+        name="fetch",
+    )(in_hbm(halves))
+    came = lax.ppermute(away, "dp", [(i, i ^ 1) for i in range(n_dp)])
+    grad_shape = pltpu.HBM((4, 4, SLICE, SIDE), F32)
     grad_in, grad_out = pl.pallas_call(
         functools.partial(finish_kernel, 1.0 / math.sqrt(total_tok)),
-        grid=(1,),
         out_shape=(grad_shape, grad_shape),
-        in_specs=[
-            pl.BlockSpec((1, 2, 4, 4, SLICE, SIDE), lambda i: (0,) * 6),
-            pl.BlockSpec((2, 4, 4, SLICE, SIDE), lambda i: (0,) * 5),
+        in_specs=[VMEM, VMEM],
+        out_specs=(HBM, HBM),
+        scratch_shapes=[
+            pltpu.VMEM((2, 4, 4, SLICE, SIDE), F32),
+            pltpu.SemaphoreType.DMA((2,)),
         ],
-        out_specs=(
-            pl.BlockSpec((4, 4, SLICE, SIDE), lambda i: (0,) * 4),
-            pl.BlockSpec((4, 4, SLICE, SIDE), lambda i: (0,) * 4),
-        ),
         compiler_params=params(),
         name="finish",
-    )(in_hbm(halves), came)
+    )(mine, came)
     return output, grad_tokens, grad_in, grad_out
 
 

time: 129 us -> 128 us (level)
  no operation moved by 1% of the time
where the time goes in v4:
time: 128 us
  blocking collectives  74.8 us (58%)
  waiting for transfers between devices  22.5 us (18%)
  between operations  14.1 us (11%)
  Pallas kernels  10.6 us (8%)
  starting transfers between devices  3.05 us (2%)
  local copies, waits for them, and re-layouts  2.42 us (2%)
    all_to_all x1, blocking collectives, shards(): got = lax.all_to_all(packed, 'mp', 0, 0, tiled=True)  21.1 us
    all_to_all x1, blocking collectives, shards(): lax.all_to_all(chosen, 'mp', 0, 0, axis_index_groups=same_core, tiled=True)  19.3 us
    all_to_all x1, blocking collectives, shards(): lax.all_to_all(part, 'mp', 0, 0, axis_index_groups=same_core, tiled=True)  19 us
    all_to_all x1, blocking collectives, shards(): final = lax.all_to_all(sorted_, 'mp', 0, 0, tiled=True)  15.4 us
    reduce_scatter x1, waiting for transfers between devices, shards(): lax.psum_scatter(grads.reshape(-1, SIDE), 'dp', scatter_dimension=0, axis...  11.9 us
    ppermute x1, waiting for transfers between devices, shards(): came = lax.ppermute(away, 'dp', [(i, i ^ 1) for i in range(n_dp)])  6.04 us
    pallas_call x1, Pallas kernels, shards(): pl.pallas_call(hidden_kernel, out_shape=(pltpu.HBM((zs, 2, 2, 4, 4, SLICE...  4.31 us
  transfers between devices with their start and end apart: 4, of which 4 were waited for; matrix products, arithmetic and copies ran while one was open for 1% of the time, Pallas kernels for 2%

profile of v4, /device:TPU:1, one launch (start us, length us, event | category | flops | bytes accessed | tf_op | source)
XLA Modules:
  0.0 128.0 jit_solution(14501032912948261443)
XLA Ops:
  7.2 0.0 reduce-scatter.2.cloned.1.call-start
  7.2 0.0 copy-start.1
  7.2 1.3 %pack.1 = bf16[16,144,128]{2,1,0:T(8,128)(2,1)S(1)} custom-call(bf16[16,16,512]{2,1,0:T(8,128)(2,1)} %bitcast.8, bf16[16,16,512]{2,1,0:T(8,128)(2,1)} %bitcast.9, s32[4,4]{1,0:T(4,128)} %p_ref.1, s32[4,4]{1,0:T(4,128)} %q_ref.1), custom_call_target="tpu_custom_call" | custom-call | tf_op jit(solution)/shard_map/pack/pallas_call | solution.py:185
  8.6 0.0 copy-start
  8.6 21.1 %all_to_all.20.got_ref = bf16[16,144,128]{2,1,0:T(8,128)(2,1)S(1)} all-to-all(bf16[16,144,128]{2,1,0:T(8,128)(2,1)S(1)} %pack.1), channel_id=1, replica_groups=mesh['dp'=16,'mp'=16] {'mp'}, dimensions={0} | all-to-all | bytes 1179648 | tf_op jit(solution)/shard_map/all_to_all | solution.py:199
  29.7 1.0 select.1
  30.7 19.3 %all_to_all.21.own_ref = bf16[8,8,32,256]{3,2,1,0:T(8,128)(2,1)S(1)} all-to-all(bf16[8,8,32,256]{3,2,1,0:T(8,128)(2,1)S(1)} %get-tuple-element.18), channel_id=1, replica_groups={{0,2,4,6,8,10,12,14},{1,3,5,7,9,11,13,15},{16,18,20,22,24,26,28,30},{17..., dimensions={0} | all-to-all | bytes 2097152 | tf_op jit(solution)/shard_map/all_to_all | solution.py:210
  50.0 1.3 collective-permute-start
  51.3 2.3 %collective-permute-done.oth_ref = bf16[8,8,32,256]{3,2,1,0:T(8,128)(2,1)S(1)} collective-permute-done((bf16[8,8,32,256]{3,2,1,0:T(8,128)(2,1)S(1)}, bf16[8,8,32,256]{3,2,1,0:T(8,128)(2,1)S(1)}, u32[]{:S(2)}, u32[]{:S(2)}) %collective-permute-start) | collective-permute-done | bytes 1048608 | tf_op jit(solution)/shard_map/ppermute | solution.py:211
  53.6 0.0 copy-done.1
  53.6 0.0 copy-done
  53.6 4.3 %hidden.1 = (bf16[8,2,2,4,4,16,256]{6,5,4,3,2,1,0:T(8,128)(2,1)}, bf16[256,1024]{1,0:T(8,128)(2,1)S(1)}, bf16[256,1024]{1,0:T(8,128)(2,1)S(1)}) custom-call(bf16[8,8,32,256]{3,2,1,0:T(8,128)(2,1)S(1)} %all_to_all.21.own_ref, bf16[8,8,32,256]{3,2,1,0:T(8,128)(2,1)S(1)} %collective-permute-done.oth_ref, bf16[4,4,256,256]{3,2,1,0:T(8,128)(2,1)S(1)} %copy-done, ...), custom_call_target="tpu_custom_call" | custom-call | tf_op jit(solution)/shard_map/hidden/pallas_call | solution.py:214
  57.9 0.0 reduce-scatter.2.cloned.1.call-update
  58.0 0.0 copy-start.2
  58.0 1.6 %copy-done.2 = bf16[4,4,256,256]{3,2,1,0:T(8,128)(2,1)S(1)} copy-done((bf16[4,4,256,256]{3,2,1,0:T(8,128)(2,1)S(1)}, bf16[4,4,256,256]{3,2,1,0:T(8,128)(2,1)}, u32[]{:S(2)}) %copy-start.2) | copy-done | bytes 2097176
  59.6 1.3 project.1
  60.8 0.5 collective-permute-start.1
  61.3 2.3 %collective-permute-done.1 = bf16[8,8,32,256]{3,2,1,0:T(8,128)(2,1)S(1)} collective-permute-done((bf16[8,8,32,256]{3,2,1,0:T(8,128)(2,1)S(1)}, bf16[8,8,32,256]{3,2,1,0:T(8,128)(2,1)S(1)}, u32[]{:S(2)}, u32[]{:S(2)}) %collective-permute-start.1) | collective-permute-done | bytes 1048608 | tf_op jit(solution)/shard_map/ppermute | solution.py:240
  63.6 0.4 add_convert_fusion
  64.0 19.0 %all_to_all.22.got_ref = bf16[8,8,32,256]{3,2,1,0:T(8,128)(2,1)S(1)} all-to-all(bf16[8,8,32,256]{3,2,1,0:T(8,128)(2,1)S(1)} %add_convert_fusion), channel_id=1, replica_groups={{0,2,4,6,8,10,12,14},{1,3,5,7,9,11,13,15},{16,18,20,22,24,26,28,30},{17..., dimensions={0} | all-to-all | bytes 2097152 | tf_op jit(solution)/shard_map/all_to_all | solution.py:242
  83.0 0.8 sort.1
  83.8 15.4 %all_to_all.23 = bf16[16,32,512]{2,1,0:T(8,128)(2,1)S(1)} all-to-all(bf16[16,32,512]{2,1,0:T(8,128)(2,1)S(1)} %sort.1), channel_id=1, replica_groups=mesh['dp'=16,'mp'=16] {'mp'}, dimensions={0} | all-to-all | bytes 1048576 | tf_op jit(solution)/shard_map/all_to_all | solution.py:251
  99.2 0.8 fusion
  100.0 11.9 %reduce-scatter.2.cloned.1.call-done = bf16[1024,256]{1,0:T(8,128)(2,1)} async-done(((bf16[8192,256]{1,0:T(8,128)(2,1)}), bf16[1024,256]{1,0:T(8,128)(2,1)}) %reduce-scatter.2.cloned.1.call-update) | async-done | bytes 524304 | tf_op jit(solution)/shard_map/reduce_scatter | solution.py:228
  111.9 1.0 fetch.1
  113.0 1.3 collective-permute-start.2
  114.3 6.0 %collective-permute-done.2.came_ref = bf16[2,4,4,16,256]{4,3,2,1,0:T(8,128)(2,1)S(1)} collective-permute-done((bf16[2,4,4,16,256]{4,3,2,1,0:T(8,128)(2,1)S(1)}, bf16[2,4,4,16,256]{4,3,2,1,0:T(8,128)(2,1)S(1)}, u32[]{:S(2)}, u32[]{:S(2)}) %collective-permute-start.2) | collective-permute-done | bytes 262176 | tf_op jit(solution)/shard_map/ppermute | solution.py:267
  120.3 0.8 finish.1
Async XLA Ops:
  7.2 104.8 %reduce-scatter.2.cloned.1.call-start = ((), (), s32[]{:S(2)}) async-start(), calls=%async_computation.5 | async-start | bytes 4718592 | tf_op jit(solution)/shard_map/reduce_scatter | solution.py:228
  7.2 46.4 %copy-start.1 = (bf16[4,4,256,256]{3,2,1,0:T(8,128)(2,1)S(1)}, bf16[4,4,256,256]{3,2,1,0:T(8,128)(2,1)}, u32[]{:S(2)}) copy-start(bf16[4,4,256,256]{3,2,1,0:T(8,128)(2,1)} %wout_ref.3) | copy-start | bytes 6291460
  8.6 45.0 %copy-start = (bf16[4,4,256,256]{3,2,1,0:T(8,128)(2,1)S(1)}, bf16[4,4,256,256]{3,2,1,0:T(8,128)(2,1)}, u32[]{:S(2)}) copy-start(bf16[4,4,256,256]{3,2,1,0:T(8,128)(2,1)} %win_ref.3) | copy-start | bytes 6291460
  50.0 3.6 %collective-permute-start = (bf16[8,8,32,256]{3,2,1,0:T(8,128)(2,1)S(1)}, bf16[8,8,32,256]{3,2,1,0:T(8,128)(2,1)S(1)}, u32[]{:S(2)}, u32[]{:S(2)}) collective-permute-start(bf16[8,8,32,256]{3,2,1,0:T(8,128)(2,1)S(1)} %all_to_all.21.own_ref), channel_id=1, source_target_pairs={{0,1},{1,0},{2,3},{3,2},{4,5},{5,4},{6,7},{7,6},{8,9},{9,8},{10,11... | collective-permute-start | bytes 3145736 | tf_op jit(solution)/shard_map/ppermute | solution.py:211
  58.0 1.6 %copy-start.2 = (bf16[4,4,256,256]{3,2,1,0:T(8,128)(2,1)S(1)}, bf16[4,4,256,256]{3,2,1,0:T(8,128)(2,1)}, u32[]{:S(2)}) copy-start(bf16[4,4,256,256]{3,2,1,0:T(8,128)(2,1)} %wout_ref.3) | copy-start | bytes 6291460
  60.8 2.7 %collective-permute-start.1 = (bf16[8,8,32,256]{3,2,1,0:T(8,128)(2,1)S(1)}, bf16[8,8,32,256]{3,2,1,0:T(8,128)(2,1)S(1)}, u32[]{:S(2)}, u32[]{:S(2)}) collective-permute-start(bf16[8,8,32,256]{3,2,1,0:T(8,128)(2,1)S(1)} %get-tuple-element.24), channel_id=1, source_target_pairs={{0,1},{1,0},{2,3},{3,2},{4,5},{5,4},{6,7},{7,6},{8,9},{9,8},{10,11... | collective-permute-start | bytes 3145736 | tf_op jit(solution)/shard_map/ppermute | solution.py:240
  113.0 7.3 %collective-permute-start.2 = (bf16[2,4,4,16,256]{4,3,2,1,0:T(8,128)(2,1)S(1)}, bf16[2,4,4,16,256]{4,3,2,1,0:T(8,128)(2,1)S(1)}, u32[]{:S(2)}, u32[]{:S(2)}) collective-permute-start(bf16[2,4,4,16,256]{4,3,2,1,0:T(8,128)(2,1)S(1)} %get-tuple-element.29), channel_id=1, source_target_pairs={{0,16},{16,0},{32,48},{48,32},{64,80},{80,64},{96,112},{112,96},{1... | collective-permute-start | bytes 786440 | tf_op jit(solution)/shard_map/ppermute | solution.py:267
Sparse Core Ops, SparseCore 0:
  58.1 53.8 reduce-scatter.1

commit v5 on v4

--- a/solution.py
+++ b/solution.py
@@ -54,17 +54,14 @@
         copy.wait()
 
 
-def select_kernel(got_ref, out_ref, lists_ref, table, sem):
+def select_kernel(got_ref, out_ref, lists_ref):
     lists = jnp.max(got_ref[:, pl.ds(2 * TILES * SLICE, SLICE), :].astype(F32), axis=1).astype(jnp.int32)
     lists_ref[...] = lists
-    copy = pltpu.make_async_copy(lists_ref, table, sem)
-    copy.start()
-    copy.wait()
     chips = out_ref.shape[0]
     for group in range(chips // 2):
         for slot in range(8):
             for row, column in ((0, slot % 4), (SLICE, slot % 4 + 4)):
-                block = table[2 * group + slot // 4, column]
+                block = lists[2 * group + slot // 4, column]
                 owner = lax.shift_right_logical(block, 1)
                 first = row * TILES + (block & 1) * (2 * SLICE)
                 for tile in range(2):
@@ -84,32 +81,47 @@
     return [4 * core + (j ^ m) for m in (0, 1, 2)] + [4 * (1 - core) + j]
 
 
-def hidden_kernel(own_ref, oth_ref, win_ref, wout_ref, grads_ref, act_ref, dpre_ref, held, sems):
-    def block_of(row, slot):
-        pieces = [ref[:, slot, pl.ds(row, SLICE), :].reshape(-1, SIDE) for ref in (own_ref, oth_ref)]
-        return jnp.concatenate(pieces, axis=0)
-
+def block_of(ref, row, slot):
+    return ref[:, slot, pl.ds(row, SLICE), :].reshape(-1, SIDE)
+
+
+def activations(ref, win_ref, wout_ref, j):
+    slots = slots_of(j)
+    pre = sum(dot(block_of(ref, 0, slots[k]), win_ref[j, k], 1, 0) for k in range(4))
+    d_act = sum(dot(block_of(ref, SLICE, slots[k]), wout_ref[j, k], 1, 1) for k in range(4))
+    c = math.sqrt(2.0 / math.pi)
+    square = pre * pre
+    th = jnp.tanh(c * (pre + 0.044715 * (square * pre)))
+    half = 0.5 * (1.0 + th)
+    slope = half + (0.5 * c) * pre * (1.0 - th * th) * (1.0 + (3 * 0.044715) * square)
+    return (pre * half).astype(BF16), (d_act * slope).astype(BF16)
+
+
+def first_kernel(own_ref, win_ref, wout_ref, act_ref, dpre_ref):
+    for j in range(4):
+        lanes = pl.ds(j * SIDE, SIDE)
+        act_ref[:, lanes], dpre_ref[:, lanes] = activations(own_ref, win_ref, wout_ref, j)
+
+
+def hidden_kernel(
+    own_ref, oth_ref, act_ref, dpre_ref, win_ref, wout_ref,
+    grads_ref, all_act_ref, all_dpre_ref, held, sems,
+):
     side = lax.axis_index("dp") & 1
-    c = math.sqrt(2.0 / math.pi)
+    zs = held.shape[2]
     copies = []
     for j in range(4):
-        slots = slots_of(j)
-        xs = [block_of(0, s) for s in slots]
-        dys = [block_of(SLICE, s) for s in slots]
-        pre = sum(dot(xs[k], win_ref[j, k], 1, 0) for k in range(4))
-        d_act = sum(dot(dys[k], wout_ref[j, k], 1, 1) for k in range(4))
-        square = pre * pre
-        th = jnp.tanh(c * (pre + 0.044715 * (square * pre)))
-        half = 0.5 * (1.0 + th)
-        act = (pre * half).astype(BF16)
-        slope = half + (0.5 * c) * pre * (1.0 - th * th) * (1.0 + (3 * 0.044715) * square)
-        d_pre = (d_act * slope).astype(BF16)
-        act_ref[:, j * SIDE : (j + 1) * SIDE] = act
-        dpre_ref[:, j * SIDE : (j + 1) * SIDE] = d_pre
-        zs = held.shape[2]
-        for k in range(4):
-            g_in = dot(xs[k], d_pre, 0, 0).astype(BF16).reshape(zs, 2, SLICE, SIDE)
-            g_out = dot(act, dys[k], 0, 0).astype(BF16).reshape(zs, 2, SLICE, SIDE)
+        lanes = pl.ds(j * SIDE, SIDE)
+        act, d_pre = activations(oth_ref, win_ref, wout_ref, j)
+        act = jnp.concatenate([act_ref[:, lanes], act], axis=0)
+        d_pre = jnp.concatenate([dpre_ref[:, lanes], d_pre], axis=0)
+        all_act_ref[:, lanes] = act
+        all_dpre_ref[:, lanes] = d_pre
+        for k, slot in enumerate(slots_of(j)):
+            x = jnp.concatenate([block_of(own_ref, 0, slot), block_of(oth_ref, 0, slot)], axis=0)
+            dy = jnp.concatenate([block_of(own_ref, SLICE, slot), block_of(oth_ref, SLICE, slot)], axis=0)
+            g_in = dot(x, d_pre, 0, 0).astype(BF16).reshape(zs, 2, SLICE, SIDE)
+            g_out = dot(act, dy, 0, 0).astype(BF16).reshape(zs, 2, SLICE, SIDE)
             for away in range(2):
                 held[j, k, :, away ^ side, 0] = g_in[:, away]
                 held[j, k, :, away ^ side, 1] = g_out[:, away]
@@ -203,18 +215,26 @@
         out_shape=(share, jax.ShapeDtypeStruct((n, LANES), jnp.int32)),
         in_specs=[VMEM],
         out_specs=(VMEM, VMEM),
-        scratch_shapes=[pltpu.SMEM((n, LANES), jnp.int32), pltpu.SemaphoreType.DMA],
         compiler_params=params(),
         name="select",
     )(got)
     own = lax.all_to_all(chosen, "mp", 0, 0, axis_index_groups=same_core, tiled=True)
     oth = lax.ppermute(own, "mp", mate)
 
+    half = jax.ShapeDtypeStruct((tok // 2, QUAD), BF16)
+    first_act, first_dpre = pl.pallas_call(
+        first_kernel,
+        out_shape=(half, half),
+        in_specs=[VMEM] * 3,
+        out_specs=(VMEM, VMEM),
+        compiler_params=params(),
+        name="first",
+    )(own, w_in, w_out)
     quad = jax.ShapeDtypeStruct((tok, QUAD), BF16)
     grads, act, d_pre = pl.pallas_call(
         hidden_kernel,
         out_shape=(pltpu.HBM((zs, 2, 2, 4, 4, SLICE, SIDE), BF16), quad, quad),
-        in_specs=[VMEM] * 4,
+        in_specs=[VMEM] * 6,
         out_specs=(HBM, VMEM, VMEM),
         scratch_shapes=[
             pltpu.VMEM((4, 4, zs, 2, 2, SLICE, SIDE), BF16),
@@ -222,7 +242,7 @@
         ],
         compiler_params=params(),
         name="hidden",
-    )(own, oth, w_in, w_out)
+    )(own, oth, first_act, first_dpre, w_in, w_out)
 
     columns = [[z * 2 + xl for z in range(zs)] for xl in range(2)]
     grad_sum = lax.psum_scatter(

time: 128 us -> 127 us (level)
  no operation moved by 1% of the time
where the time goes in v5:
time: 127 us
  blocking collectives  74.8 us (59%)
  waiting for transfers between devices  21.4 us (17%)
  between operations  14.1 us (11%)
  Pallas kernels  10.9 us (9%)
  starting transfers between devices  3.04 us (2%)
  local copies, waits for them, and re-layouts  2.42 us (2%)
    all_to_all x1, blocking collectives, shards(): got = lax.all_to_all(packed, 'mp', 0, 0, tiled=True)  21.1 us
    all_to_all x1, blocking collectives, shards(): lax.all_to_all(chosen, 'mp', 0, 0, axis_index_groups=same_core, tiled=True)  19.3 us
    all_to_all x1, blocking collectives, shards(): lax.all_to_all(part, 'mp', 0, 0, axis_index_groups=same_core, tiled=True)  19 us
    all_to_all x1, blocking collectives, shards(): final = lax.all_to_all(sorted_, 'mp', 0, 0, tiled=True)  15.4 us
    reduce_scatter x1, waiting for transfers between devices, shards(): lax.psum_scatter(grads.reshape(-1, SIDE), 'dp', scatter_dimension=0, axis...  11.9 us
    ppermute x1, waiting for transfers between devices, shards(): came = lax.ppermute(away, 'dp', [(i, i ^ 1) for i in range(n_dp)])  6.05 us
    pallas_call x1, Pallas kernels, shards(): pl.pallas_call(hidden_kernel, out_shape=(pltpu.HBM((zs, 2, 2, 4, 4, SLICE...  4.05 us
  transfers between devices with their start and end apart: 4, of which 4 were waited for; matrix products, arithmetic and copies ran while one was open for 1% of the time, Pallas kernels for 2%

profile of v5, /device:TPU:1, one launch (start us, length us, event | category | flops | bytes accessed | tf_op | source)
XLA Modules:
  0.0 127.1 jit_solution(15753510240611267778)
XLA Ops:
  7.2 0.0 reduce-scatter.2.cloned.1.call-start
  7.2 0.0 copy-start.1
  7.2 1.3 %pack.1 = bf16[16,144,128]{2,1,0:T(8,128)(2,1)S(1)} custom-call(bf16[16,16,512]{2,1,0:T(8,128)(2,1)} %bitcast.8, bf16[16,16,512]{2,1,0:T(8,128)(2,1)} %bitcast.9, s32[4,4]{1,0:T(4,128)} %p_ref.1, s32[4,4]{1,0:T(4,128)} %q_ref.1), custom_call_target="tpu_custom_call" | custom-call | tf_op jit(solution)/shard_map/pack/pallas_call | solution.py:197
  8.6 0.0 copy-start
  8.6 21.1 %all_to_all.20.got_ref = bf16[16,144,128]{2,1,0:T(8,128)(2,1)S(1)} all-to-all(bf16[16,144,128]{2,1,0:T(8,128)(2,1)S(1)} %pack.1), channel_id=1, replica_groups=mesh['dp'=16,'mp'=16] {'mp'}, dimensions={0} | all-to-all | bytes 1179648 | tf_op jit(solution)/shard_map/all_to_all | solution.py:211
  29.7 0.4 select.1
  30.1 19.3 %all_to_all.21.own_ref = bf16[8,8,32,256]{3,2,1,0:T(8,128)(2,1)S(1)} all-to-all(bf16[8,8,32,256]{3,2,1,0:T(8,128)(2,1)S(1)} %get-tuple-element.20), channel_id=1, replica_groups={{0,2,4,6,8,10,12,14},{1,3,5,7,9,11,13,15},{16,18,20,22,24,26,28,30},{17..., dimensions={0} | all-to-all | bytes 2097152 | tf_op jit(solution)/shard_map/all_to_all | solution.py:221
  49.4 1.3 %collective-permute-start = (bf16[8,8,32,256]{3,2,1,0:T(8,128)(2,1)S(1)}, bf16[8,8,32,256]{3,2,1,0:T(8,128)(2,1)S(1)}, u32[]{:S(2)}, u32[]{:S(2)}) collective-permute-start(bf16[8,8,32,256]{3,2,1,0:T(8,128)(2,1)S(1)} %all_to_all.21.own_ref), channel_id=1, source_target_pairs={{0,1},{1,0},{2,3},{3,2},{4,5},{5,4},{6,7},{7,6},{8,9},{9,8},{10,11... | collective-permute-start | bytes 3145736 | tf_op jit(solution)/shard_map/ppermute | solution.py:222
  50.7 0.0 copy-done.1
  50.7 0.0 copy-done
  50.7 1.1 first.1
  51.8 1.2 collective-permute-done.oth_ref
  53.0 4.0 %hidden.1 = (bf16[8,2,2,4,4,16,256]{6,5,4,3,2,1,0:T(8,128)(2,1)}, bf16[256,1024]{1,0:T(8,128)(2,1)S(1)}, bf16[256,1024]{1,0:T(8,128)(2,1)S(1)}) custom-call(bf16[8,8,32,256]{3,2,1,0:T(8,128)(2,1)S(1)} %all_to_all.21.own_ref, bf16[8,8,32,256]{3,2,1,0:T(8,128)(2,1)S(1)} %collective-permute-done.oth_ref, bf16[128,1024]{1,0:T(8,128)(2,1)S(1)} %get-tuple-element.21.act_ref, ...), custom_call_target="tpu_custom_call" | custom-call | tf_op jit(solution)/shard_map/hidden/pallas_call | solution.py:234
  57.1 0.0 reduce-scatter.2.cloned.1.call-update
  57.1 0.0 copy-start.2
  57.1 1.6 %copy-done.2 = bf16[4,4,256,256]{3,2,1,0:T(8,128)(2,1)S(1)} copy-done((bf16[4,4,256,256]{3,2,1,0:T(8,128)(2,1)S(1)}, bf16[4,4,256,256]{3,2,1,0:T(8,128)(2,1)}, u32[]{:S(2)}) %copy-start.2) | copy-done | bytes 2097176
  58.7 1.3 project.1
  60.0 0.5 collective-permute-start.1
  60.4 2.3 %collective-permute-done.1 = bf16[8,8,32,256]{3,2,1,0:T(8,128)(2,1)S(1)} collective-permute-done((bf16[8,8,32,256]{3,2,1,0:T(8,128)(2,1)S(1)}, bf16[8,8,32,256]{3,2,1,0:T(8,128)(2,1)S(1)}, u32[]{:S(2)}, u32[]{:S(2)}) %collective-permute-start.1) | collective-permute-done | bytes 1048608 | tf_op jit(solution)/shard_map/ppermute | solution.py:260
  62.7 0.4 add_convert_fusion
  63.1 19.0 %all_to_all.22.got_ref = bf16[8,8,32,256]{3,2,1,0:T(8,128)(2,1)S(1)} all-to-all(bf16[8,8,32,256]{3,2,1,0:T(8,128)(2,1)S(1)} %add_convert_fusion), channel_id=1, replica_groups={{0,2,4,6,8,10,12,14},{1,3,5,7,9,11,13,15},{16,18,20,22,24,26,28,30},{17..., dimensions={0} | all-to-all | bytes 2097152 | tf_op jit(solution)/shard_map/all_to_all | solution.py:262
  82.1 0.8 sort.1
  82.9 15.4 %all_to_all.23 = bf16[16,32,512]{2,1,0:T(8,128)(2,1)S(1)} all-to-all(bf16[16,32,512]{2,1,0:T(8,128)(2,1)S(1)} %sort.1), channel_id=1, replica_groups=mesh['dp'=16,'mp'=16] {'mp'}, dimensions={0} | all-to-all | bytes 1048576 | tf_op jit(solution)/shard_map/all_to_all | solution.py:271
  98.4 0.8 fusion
  99.2 11.9 %reduce-scatter.2.cloned.1.call-done = bf16[1024,256]{1,0:T(8,128)(2,1)} async-done(((bf16[8192,256]{1,0:T(8,128)(2,1)}), bf16[1024,256]{1,0:T(8,128)(2,1)}) %reduce-scatter.2.cloned.1.call-update) | async-done | bytes 524304 | tf_op jit(solution)/shard_map/reduce_scatter | solution.py:248
  111.1 1.0 fetch.1
  112.1 1.3 collective-permute-start.2
  113.4 6.1 %collective-permute-done.2.came_ref = bf16[2,4,4,16,256]{4,3,2,1,0:T(8,128)(2,1)S(1)} collective-permute-done((bf16[2,4,4,16,256]{4,3,2,1,0:T(8,128)(2,1)S(1)}, bf16[2,4,4,16,256]{4,3,2,1,0:T(8,128)(2,1)S(1)}, u32[]{:S(2)}, u32[]{:S(2)}) %collective-permute-start.2) | collective-permute-done | bytes 262176 | tf_op jit(solution)/shard_map/ppermute | solution.py:287
  119.4 0.8 finish.1
Async XLA Ops:
  7.2 103.9 %reduce-scatter.2.cloned.1.call-start = ((), (), s32[]{:S(2)}) async-start(), calls=%async_computation.5 | async-start | bytes 4718592 | tf_op jit(solution)/shard_map/reduce_scatter | solution.py:248
  7.2 43.5 %copy-start.1 = (bf16[4,4,256,256]{3,2,1,0:T(8,128)(2,1)S(1)}, bf16[4,4,256,256]{3,2,1,0:T(8,128)(2,1)}, u32[]{:S(2)}) copy-start(bf16[4,4,256,256]{3,2,1,0:T(8,128)(2,1)} %wout_ref.5) | copy-start | bytes 6291460
  8.6 42.2 %copy-start = (bf16[4,4,256,256]{3,2,1,0:T(8,128)(2,1)S(1)}, bf16[4,4,256,256]{3,2,1,0:T(8,128)(2,1)}, u32[]{:S(2)}) copy-start(bf16[4,4,256,256]{3,2,1,0:T(8,128)(2,1)} %win_ref.5) | copy-start | bytes 6291460
  49.4 3.6 %collective-permute-start = (bf16[8,8,32,256]{3,2,1,0:T(8,128)(2,1)S(1)}, bf16[8,8,32,256]{3,2,1,0:T(8,128)(2,1)S(1)}, u32[]{:S(2)}, u32[]{:S(2)}) collective-permute-start(bf16[8,8,32,256]{3,2,1,0:T(8,128)(2,1)S(1)} %all_to_all.21.own_ref), channel_id=1, source_target_pairs={{0,1},{1,0},{2,3},{3,2},{4,5},{5,4},{6,7},{7,6},{8,9},{9,8},{10,11... | collective-permute-start | bytes 3145736 | tf_op jit(solution)/shard_map/ppermute | solution.py:222
  57.1 1.6 %copy-start.2 = (bf16[4,4,256,256]{3,2,1,0:T(8,128)(2,1)S(1)}, bf16[4,4,256,256]{3,2,1,0:T(8,128)(2,1)}, u32[]{:S(2)}) copy-start(bf16[4,4,256,256]{3,2,1,0:T(8,128)(2,1)} %wout_ref.5) | copy-start | bytes 6291460
  60.0 2.7 %collective-permute-start.1 = (bf16[8,8,32,256]{3,2,1,0:T(8,128)(2,1)S(1)}, bf16[8,8,32,256]{3,2,1,0:T(8,128)(2,1)S(1)}, u32[]{:S(2)}, u32[]{:S(2)}) collective-permute-start(bf16[8,8,32,256]{3,2,1,0:T(8,128)(2,1)S(1)} %get-tuple-element.28), channel_id=1, source_target_pairs={{0,1},{1,0},{2,3},{3,2},{4,5},{5,4},{6,7},{7,6},{8,9},{9,8},{10,11... | collective-permute-start | bytes 3145736 | tf_op jit(solution)/shard_map/ppermute | solution.py:260
  112.1 7.3 %collective-permute-start.2 = (bf16[2,4,4,16,256]{4,3,2,1,0:T(8,128)(2,1)S(1)}, bf16[2,4,4,16,256]{4,3,2,1,0:T(8,128)(2,1)S(1)}, u32[]{:S(2)}, u32[]{:S(2)}) collective-permute-start(bf16[2,4,4,16,256]{4,3,2,1,0:T(8,128)(2,1)S(1)} %get-tuple-element.33), channel_id=1, source_target_pairs={{0,16},{16,0},{32,48},{48,32},{64,80},{80,64},{96,112},{112,96},{1... | collective-permute-start | bytes 786440 | tf_op jit(solution)/shard_map/ppermute | solution.py:287
Sparse Core Ops, SparseCore 0:
  57.2 53.8 reduce-scatter.1

commit v6 on v5

--- a/solution.py
+++ b/solution.py
@@ -105,7 +105,7 @@
 
 def hidden_kernel(
     own_ref, oth_ref, act_ref, dpre_ref, win_ref, wout_ref,
-    grads_ref, all_act_ref, all_dpre_ref, held, sems,
+    grads_ref, more_act_ref, more_dpre_ref, held, sems,
 ):
     side = lax.axis_index("dp") & 1
     zs = held.shape[2]
@@ -113,10 +113,10 @@
     for j in range(4):
         lanes = pl.ds(j * SIDE, SIDE)
         act, d_pre = activations(oth_ref, win_ref, wout_ref, j)
+        more_act_ref[:, lanes] = act
+        more_dpre_ref[:, lanes] = d_pre
         act = jnp.concatenate([act_ref[:, lanes], act], axis=0)
         d_pre = jnp.concatenate([dpre_ref[:, lanes], d_pre], axis=0)
-        all_act_ref[:, lanes] = act
-        all_dpre_ref[:, lanes] = d_pre
         for k, slot in enumerate(slots_of(j)):
             x = jnp.concatenate([block_of(own_ref, 0, slot), block_of(oth_ref, 0, slot)], axis=0)
             dy = jnp.concatenate([block_of(own_ref, SLICE, slot), block_of(oth_ref, SLICE, slot)], axis=0)
@@ -131,10 +131,17 @@
         copy.wait()
 
 
-def project_kernel(act_ref, dpre_ref, win_ref, wout_ref, own_ref, oth_ref):
+def project_kernel(
+    act_ref, dpre_ref, more_act_ref, more_dpre_ref, win_ref, wout_ref, own_ref, oth_ref
+):
     core = lax.axis_index("mp") & 1
-    acts = [act_ref[:, t * SIDE : (t + 1) * SIDE] for t in range(4)]
-    dpres = [dpre_ref[:, t * SIDE : (t + 1) * SIDE] for t in range(4)]
+
+    def joined(first_ref, more_ref, t):
+        lanes = pl.ds(t * SIDE, SIDE)
+        return jnp.concatenate([first_ref[:, lanes], more_ref[:, lanes]], axis=0)
+
+    acts = [joined(act_ref, more_act_ref, t) for t in range(4)]
+    dpres = [joined(dpre_ref, more_dpre_ref, t) for t in range(4)]
 
     def put(row, slot, total):
         pieces = total.astype(BF16).reshape(2, -1, SLICE, SIDE)
@@ -164,15 +171,10 @@
                 out_ref[owner, rows, pl.ds(half, SIDE)] = total.astype(BF16)
 
 
-def fetch_kernel(sum_ref, own_ref, away_ref, sems):
-    copies = [
-        pltpu.make_async_copy(sum_ref.at[half], ref, sems.at[half])
-        for half, ref in enumerate((own_ref, away_ref))
-    ]
-    for copy in copies:
-        copy.start()
-    for copy in copies:
-        copy.wait()
+def fetch_kernel(which, sum_ref, half_ref, sem):
+    copy = pltpu.make_async_copy(sum_ref.at[which], half_ref, sem)
+    copy.start()
+    copy.wait()
 
 
 def finish_kernel(scale, own_ref, came_ref, in_ref, out_ref, held, sems):
@@ -230,10 +232,9 @@
         compiler_params=params(),
         name="first",
     )(own, w_in, w_out)
-    quad = jax.ShapeDtypeStruct((tok, QUAD), BF16)
-    grads, act, d_pre = pl.pallas_call(
+    grads, more_act, more_dpre = pl.pallas_call(
         hidden_kernel,
-        out_shape=(pltpu.HBM((zs, 2, 2, 4, 4, SLICE, SIDE), BF16), quad, quad),
+        out_shape=(pltpu.HBM((zs, 2, 2, 4, 4, SLICE, SIDE), BF16), half, half),
         in_specs=[VMEM] * 6,
         out_specs=(HBM, VMEM, VMEM),
         scratch_shapes=[
@@ -252,11 +253,11 @@
     part_own, part_oth = pl.pallas_call(
         project_kernel,
         out_shape=(share, share),
-        in_specs=[VMEM] * 4,
+        in_specs=[VMEM] * 6,
         out_specs=(VMEM, VMEM),
         compiler_params=params(),
         name="project",
-    )(act, d_pre, w_in, w_out)
+    )(first_act, first_dpre, more_act, more_dpre, w_in, w_out)
     part_mate = lax.ppermute(part_oth, "mp", mate)
     part = (part_own.astype(F32) + part_mate.astype(F32)).astype(BF16)
     slices = lax.all_to_all(part, "mp", 0, 0, axis_index_groups=same_core, tiled=True)
@@ -274,17 +275,18 @@
 
     grad_sum, output, grad_tokens = lax.optimization_barrier((grad_sum, output, grad_tokens))
     halves = grad_sum.reshape(2, 2, 4, 4, SLICE, SIDE)
-    half = jax.ShapeDtypeStruct((2, 4, 4, SLICE, SIDE), BF16)
-    mine, away = pl.pallas_call(
-        fetch_kernel,
-        out_shape=(half, half),
+    summed = in_hbm(halves)
+    fetch = lambda which, name: pl.pallas_call(
+        functools.partial(fetch_kernel, which),
+        out_shape=jax.ShapeDtypeStruct((2, 4, 4, SLICE, SIDE), BF16),
         in_specs=[HBM],
-        out_specs=(VMEM, VMEM),
-        scratch_shapes=[pltpu.SemaphoreType.DMA((2,))],
-        compiler_params=params(),
-        name="fetch",
-    )(in_hbm(halves))
-    came = lax.ppermute(away, "dp", [(i, i ^ 1) for i in range(n_dp)])
+        out_specs=VMEM,
+        scratch_shapes=[pltpu.SemaphoreType.DMA],
+        compiler_params=params(),
+        name=name,
+    )(summed)
+    came = lax.ppermute(fetch(1, "fetch_away"), "dp", [(i, i ^ 1) for i in range(n_dp)])
+    mine = fetch(0, "fetch_own")
     grad_shape = pltpu.HBM((4, 4, SLICE, SIDE), F32)
     grad_in, grad_out = pl.pallas_call(
         functools.partial(finish_kernel, 1.0 / math.sqrt(total_tok)),

time: 127 us -> 127 us (level)
  transfers between devices with their start and end apart: 4 -> 4, of which waited for: 4 -> 4; matrix products, arithmetic and copies ran while one was open for 1% -> 1% of each run, Pallas kernels for 2% -> 3%
where the time goes in v6:
time: 127 us
  blocking collectives  74.8 us (59%)
  waiting for transfers between devices  20.5 us (16%)
  between operations  14.1 us (11%)
  Pallas kernels  11.7 us (9%)
  starting transfers between devices  3.04 us (2%)
  local copies, waits for them, and re-layouts  2.42 us (2%)
    all_to_all x1, blocking collectives, shards(): got = lax.all_to_all(packed, 'mp', 0, 0, tiled=True)  21.1 us
    all_to_all x1, blocking collectives, shards(): lax.all_to_all(chosen, 'mp', 0, 0, axis_index_groups=same_core, tiled=True)  19.3 us
    all_to_all x1, blocking collectives, shards(): lax.all_to_all(part, 'mp', 0, 0, axis_index_groups=same_core, tiled=True)  19 us
    all_to_all x1, blocking collectives, shards(): final = lax.all_to_all(sorted_, 'mp', 0, 0, tiled=True)  15.4 us
    reduce_scatter x1, waiting for transfers between devices, shards(): lax.psum_scatter(grads.reshape(-1, SIDE), 'dp', scatter_dimension=0, axis...  11.9 us
    ppermute x1, waiting for transfers between devices, shards(): lax.ppermute(fetch(1, 'fetch_away'), 'dp', [(i, i ^ 1) for i in range(n_d...  5.09 us
    pallas_call x1, Pallas kernels, shards(): pl.pallas_call(hidden_kernel, out_shape=(pltpu.HBM((zs, 2, 2, 4, 4, SLICE...  4 us
  transfers between devices with their start and end apart: 4, of which 4 were waited for; matrix products, arithmetic and copies ran while one was open for 1% of the time, Pallas kernels for 3%

profile of v6, /device:TPU:1, one launch (start us, length us, event | category | flops | bytes accessed | tf_op | source)
XLA Modules:
  0.0 127.0 jit_solution(4892525788055244193)
XLA Ops:
  7.2 0.0 reduce-scatter.2.cloned.1.call-start
  7.2 0.0 copy-start.1
  7.2 1.3 %pack.1 = bf16[16,144,128]{2,1,0:T(8,128)(2,1)S(1)} custom-call(bf16[16,16,512]{2,1,0:T(8,128)(2,1)} %bitcast.9, bf16[16,16,512]{2,1,0:T(8,128)(2,1)} %bitcast.10, s32[4,4]{1,0:T(4,128)} %p_ref.1, s32[4,4]{1,0:T(4,128)} %q_ref.1), custom_call_target="tpu_custom_call" | custom-call | tf_op jit(solution)/shard_map/pack/pallas_call | solution.py:199
  8.6 0.0 copy-start
  8.6 21.1 %all_to_all.20.got_ref = bf16[16,144,128]{2,1,0:T(8,128)(2,1)S(1)} all-to-all(bf16[16,144,128]{2,1,0:T(8,128)(2,1)S(1)} %pack.1), channel_id=1, replica_groups=mesh['dp'=16,'mp'=16] {'mp'}, dimensions={0} | all-to-all | bytes 1179648 | tf_op jit(solution)/shard_map/all_to_all | solution.py:213
  29.7 0.4 select.1
  30.1 19.3 %all_to_all.21.own_ref = bf16[8,8,32,256]{3,2,1,0:T(8,128)(2,1)S(1)} all-to-all(bf16[8,8,32,256]{3,2,1,0:T(8,128)(2,1)S(1)} %get-tuple-element.18), channel_id=1, replica_groups={{0,2,4,6,8,10,12,14},{1,3,5,7,9,11,13,15},{16,18,20,22,24,26,28,30},{17..., dimensions={0} | all-to-all | bytes 2097152 | tf_op jit(solution)/shard_map/all_to_all | solution.py:223
  49.4 1.3 %collective-permute-start = (bf16[8,8,32,256]{3,2,1,0:T(8,128)(2,1)S(1)}, bf16[8,8,32,256]{3,2,1,0:T(8,128)(2,1)S(1)}, u32[]{:S(2)}, u32[]{:S(2)}) collective-permute-start(bf16[8,8,32,256]{3,2,1,0:T(8,128)(2,1)S(1)} %all_to_all.21.own_ref), channel_id=1, source_target_pairs={{0,1},{1,0},{2,3},{3,2},{4,5},{5,4},{6,7},{7,6},{8,9},{9,8},{10,11... | collective-permute-start | bytes 3145736 | tf_op jit(solution)/shard_map/ppermute | solution.py:224
  50.7 0.0 copy-done.1
  50.7 0.0 copy-done
  50.7 1.1 first.1
  51.8 1.2 collective-permute-done.oth_ref
  53.0 4.0 %hidden.1 = (bf16[8,2,2,4,4,16,256]{6,5,4,3,2,1,0:T(8,128)(2,1)}, bf16[128,1024]{1,0:T(8,128)(2,1)S(1)}, bf16[128,1024]{1,0:T(8,128)(2,1)S(1)}) custom-call(bf16[8,8,32,256]{3,2,1,0:T(8,128)(2,1)S(1)} %all_to_all.21.own_ref, bf16[8,8,32,256]{3,2,1,0:T(8,128)(2,1)S(1)} %collective-permute-done.oth_ref, bf16[128,1024]{1,0:T(8,128)(2,1)S(1)} %get-tuple-element.19.act_ref, ...), custom_call_target="tpu_custom_call" | custom-call | tf_op jit(solution)/shard_map/hidden/pallas_call | solution.py:235
  57.0 0.0 reduce-scatter.2.cloned.1.call-update
  57.0 0.0 copy-start.2
  57.1 1.6 %copy-done.2 = bf16[4,4,256,256]{3,2,1,0:T(8,128)(2,1)S(1)} copy-done((bf16[4,4,256,256]{3,2,1,0:T(8,128)(2,1)S(1)}, bf16[4,4,256,256]{3,2,1,0:T(8,128)(2,1)}, u32[]{:S(2)}) %copy-start.2) | copy-done | bytes 2097176
  58.6 1.3 project.1
  59.9 0.5 collective-permute-start.1
  60.4 2.3 %collective-permute-done.1 = bf16[8,8,32,256]{3,2,1,0:T(8,128)(2,1)S(1)} collective-permute-done((bf16[8,8,32,256]{3,2,1,0:T(8,128)(2,1)S(1)}, bf16[8,8,32,256]{3,2,1,0:T(8,128)(2,1)S(1)}, u32[]{:S(2)}, u32[]{:S(2)}) %collective-permute-start.1) | collective-permute-done | bytes 1048608 | tf_op jit(solution)/shard_map/ppermute | solution.py:261
  62.7 0.4 add_convert_fusion
  63.1 19.0 %all_to_all.22.got_ref = bf16[8,8,32,256]{3,2,1,0:T(8,128)(2,1)S(1)} all-to-all(bf16[8,8,32,256]{3,2,1,0:T(8,128)(2,1)S(1)} %add_convert_fusion), channel_id=1, replica_groups={{0,2,4,6,8,10,12,14},{1,3,5,7,9,11,13,15},{16,18,20,22,24,26,28,30},{17..., dimensions={0} | all-to-all | bytes 2097152 | tf_op jit(solution)/shard_map/all_to_all | solution.py:263
  82.0 0.8 sort.1
  82.9 15.4 %all_to_all.23 = bf16[16,32,512]{2,1,0:T(8,128)(2,1)S(1)} all-to-all(bf16[16,32,512]{2,1,0:T(8,128)(2,1)S(1)} %sort.1), channel_id=1, replica_groups=mesh['dp'=16,'mp'=16] {'mp'}, dimensions={0} | all-to-all | bytes 1048576 | tf_op jit(solution)/shard_map/all_to_all | solution.py:272
  98.3 0.8 fusion
  99.1 11.9 %reduce-scatter.2.cloned.1.call-done = bf16[1024,256]{1,0:T(8,128)(2,1)} async-done(((bf16[8192,256]{1,0:T(8,128)(2,1)}), bf16[1024,256]{1,0:T(8,128)(2,1)}) %reduce-scatter.2.cloned.1.call-update) | async-done | bytes 524304 | tf_op jit(solution)/shard_map/reduce_scatter | solution.py:249
  111.0 1.0 fetch_away.1
  112.0 1.3 collective-permute-start.2
  113.2 1.0 fetch_own.1.own_ref
  114.2 5.1 %collective-permute-done.2.came_ref = bf16[2,4,4,16,256]{4,3,2,1,0:T(8,128)(2,1)S(1)} collective-permute-done((bf16[2,4,4,16,256]{4,3,2,1,0:T(8,128)(2,1)S(1)}, bf16[2,4,4,16,256]{4,3,2,1,0:T(8,128)(2,1)S(1)}, u32[]{:S(2)}, u32[]{:S(2)}) %collective-permute-start.2) | collective-permute-done | bytes 262176 | tf_op jit(solution)/shard_map/ppermute | solution.py:288
  119.3 0.8 finish.1
Async XLA Ops:
  7.2 103.9 %reduce-scatter.2.cloned.1.call-start = ((), (), s32[]{:S(2)}) async-start(), calls=%async_computation.5 | async-start | bytes 4718592 | tf_op jit(solution)/shard_map/reduce_scatter | solution.py:249
  7.2 43.5 %copy-start.1 = (bf16[4,4,256,256]{3,2,1,0:T(8,128)(2,1)S(1)}, bf16[4,4,256,256]{3,2,1,0:T(8,128)(2,1)}, u32[]{:S(2)}) copy-start(bf16[4,4,256,256]{3,2,1,0:T(8,128)(2,1)} %wout_ref.5) | copy-start | bytes 6291460
  8.6 42.2 %copy-start = (bf16[4,4,256,256]{3,2,1,0:T(8,128)(2,1)S(1)}, bf16[4,4,256,256]{3,2,1,0:T(8,128)(2,1)}, u32[]{:S(2)}) copy-start(bf16[4,4,256,256]{3,2,1,0:T(8,128)(2,1)} %win_ref.5) | copy-start | bytes 6291460
  49.4 3.6 %collective-permute-start = (bf16[8,8,32,256]{3,2,1,0:T(8,128)(2,1)S(1)}, bf16[8,8,32,256]{3,2,1,0:T(8,128)(2,1)S(1)}, u32[]{:S(2)}, u32[]{:S(2)}) collective-permute-start(bf16[8,8,32,256]{3,2,1,0:T(8,128)(2,1)S(1)} %all_to_all.21.own_ref), channel_id=1, source_target_pairs={{0,1},{1,0},{2,3},{3,2},{4,5},{5,4},{6,7},{7,6},{8,9},{9,8},{10,11... | collective-permute-start | bytes 3145736 | tf_op jit(solution)/shard_map/ppermute | solution.py:224
  57.0 1.6 %copy-start.2 = (bf16[4,4,256,256]{3,2,1,0:T(8,128)(2,1)S(1)}, bf16[4,4,256,256]{3,2,1,0:T(8,128)(2,1)}, u32[]{:S(2)}) copy-start(bf16[4,4,256,256]{3,2,1,0:T(8,128)(2,1)} %wout_ref.5) | copy-start | bytes 6291460
  59.9 2.7 %collective-permute-start.1 = (bf16[8,8,32,256]{3,2,1,0:T(8,128)(2,1)S(1)}, bf16[8,8,32,256]{3,2,1,0:T(8,128)(2,1)S(1)}, u32[]{:S(2)}, u32[]{:S(2)}) collective-permute-start(bf16[8,8,32,256]{3,2,1,0:T(8,128)(2,1)S(1)} %get-tuple-element.26), channel_id=1, source_target_pairs={{0,1},{1,0},{2,3},{3,2},{4,5},{5,4},{6,7},{7,6},{8,9},{9,8},{10,11... | collective-permute-start | bytes 3145736 | tf_op jit(solution)/shard_map/ppermute | solution.py:261
  112.0 7.3 %collective-permute-start.2 = (bf16[2,4,4,16,256]{4,3,2,1,0:T(8,128)(2,1)S(1)}, bf16[2,4,4,16,256]{4,3,2,1,0:T(8,128)(2,1)S(1)}, u32[]{:S(2)}, u32[]{:S(2)}) collective-permute-start(bf16[2,4,4,16,256]{4,3,2,1,0:T(8,128)(2,1)S(1)} %fetch_away.1), channel_id=1, source_target_pairs={{0,16},{16,0},{32,48},{48,32},{64,80},{80,64},{96,112},{112,96},{1... | collective-permute-start | bytes 786440 | tf_op jit(solution)/shard_map/ppermute | solution.py:288
Sparse Core Ops, SparseCore 0:
  57.2 53.8 reduce-scatter.1

commit v7 on v6

--- a/solution.py
+++ b/solution.py
@@ -110,13 +110,15 @@
     side = lax.axis_index("dp") & 1
     zs = held.shape[2]
     copies = []
+    made = []
     for j in range(4):
         lanes = pl.ds(j * SIDE, SIDE)
         act, d_pre = activations(oth_ref, win_ref, wout_ref, j)
         more_act_ref[:, lanes] = act
         more_dpre_ref[:, lanes] = d_pre
         act = jnp.concatenate([act_ref[:, lanes], act], axis=0)
-        d_pre = jnp.concatenate([dpre_ref[:, lanes], d_pre], axis=0)
+        made.append((act, jnp.concatenate([dpre_ref[:, lanes], d_pre], axis=0)))
+    for j, (act, d_pre) in enumerate(made):
         for k, slot in enumerate(slots_of(j)):
             x = jnp.concatenate([block_of(own_ref, 0, slot), block_of(oth_ref, 0, slot)], axis=0)
             dy = jnp.concatenate([block_of(own_ref, SLICE, slot), block_of(oth_ref, SLICE, slot)], axis=0)

time: 127 us -> 127 us (level)
  no operation moved by 1% of the time
where the time goes in v7:
time: 127 us; the launch traced here: 126 us
  blocking collectives  74.8 us (59%)
  waiting for transfers between devices  20.5 us (16%)
  between operations  14.1 us (11%)
  Pallas kernels  11 us (9%)
  starting transfers between devices  3.04 us (2%)
  local copies, waits for them, and re-layouts  2.42 us (2%)
    all_to_all x1, blocking collectives, shards(): got = lax.all_to_all(packed, 'mp', 0, 0, tiled=True)  21.1 us
    all_to_all x1, blocking collectives, shards(): lax.all_to_all(chosen, 'mp', 0, 0, axis_index_groups=same_core, tiled=True)  19.3 us
    all_to_all x1, blocking collectives, shards(): lax.all_to_all(part, 'mp', 0, 0, axis_index_groups=same_core, tiled=True)  19 us
    all_to_all x1, blocking collectives, shards(): final = lax.all_to_all(sorted_, 'mp', 0, 0, tiled=True)  15.4 us
    reduce_scatter x1, waiting for transfers between devices, shards(): lax.psum_scatter(grads.reshape(-1, SIDE), 'dp', scatter_dimension=0, axis...  11.9 us
    ppermute x1, waiting for transfers between devices, shards(): lax.ppermute(fetch(1, 'fetch_away'), 'dp', [(i, i ^ 1) for i in range(n_d...  5.08 us
    pallas_call x1, Pallas kernels, shards(): pl.pallas_call(hidden_kernel, out_shape=(pltpu.HBM((zs, 2, 2, 4, 4, SLICE...  3.27 us
  transfers between devices with their start and end apart: 4, of which 4 were waited for; matrix products, arithmetic and copies ran while one was open for 1% of the time, Pallas kernels for 3%

profile of v7, /device:TPU:1, one launch (start us, length us, event | category | flops | bytes accessed | tf_op | source)
XLA Modules:
  0.0 126.3 jit_solution(869473271342686395)
XLA Ops:
  7.2 0.0 reduce-scatter.2.cloned.1.call-start
  7.2 0.0 copy-start.1
  7.2 1.3 %pack.1 = bf16[16,144,128]{2,1,0:T(8,128)(2,1)S(1)} custom-call(bf16[16,16,512]{2,1,0:T(8,128)(2,1)} %bitcast.9, bf16[16,16,512]{2,1,0:T(8,128)(2,1)} %bitcast.10, s32[4,4]{1,0:T(4,128)} %p_ref.1, s32[4,4]{1,0:T(4,128)} %q_ref.1), custom_call_target="tpu_custom_call" | custom-call | tf_op jit(solution)/shard_map/pack/pallas_call | solution.py:201
  8.6 0.0 copy-start
  8.6 21.1 %all_to_all.20.got_ref = bf16[16,144,128]{2,1,0:T(8,128)(2,1)S(1)} all-to-all(bf16[16,144,128]{2,1,0:T(8,128)(2,1)S(1)} %pack.1), channel_id=1, replica_groups=mesh['dp'=16,'mp'=16] {'mp'}, dimensions={0} | all-to-all | bytes 1179648 | tf_op jit(solution)/shard_map/all_to_all | solution.py:215
  29.7 0.4 select.1
  30.1 19.3 %all_to_all.21.own_ref = bf16[8,8,32,256]{3,2,1,0:T(8,128)(2,1)S(1)} all-to-all(bf16[8,8,32,256]{3,2,1,0:T(8,128)(2,1)S(1)} %get-tuple-element.18), channel_id=1, replica_groups={{0,2,4,6,8,10,12,14},{1,3,5,7,9,11,13,15},{16,18,20,22,24,26,28,30},{17..., dimensions={0} | all-to-all | bytes 2097152 | tf_op jit(solution)/shard_map/all_to_all | solution.py:225
  49.4 1.3 %collective-permute-start = (bf16[8,8,32,256]{3,2,1,0:T(8,128)(2,1)S(1)}, bf16[8,8,32,256]{3,2,1,0:T(8,128)(2,1)S(1)}, u32[]{:S(2)}, u32[]{:S(2)}) collective-permute-start(bf16[8,8,32,256]{3,2,1,0:T(8,128)(2,1)S(1)} %all_to_all.21.own_ref), channel_id=1, source_target_pairs={{0,1},{1,0},{2,3},{3,2},{4,5},{5,4},{6,7},{7,6},{8,9},{9,8},{10,11... | collective-permute-start | bytes 3145736 | tf_op jit(solution)/shard_map/ppermute | solution.py:226
  50.7 0.0 copy-done.1
  50.7 0.0 copy-done
  50.7 1.1 first.1
  51.8 1.2 collective-permute-done.oth_ref
  53.0 3.3 %hidden.1 = (bf16[8,2,2,4,4,16,256]{6,5,4,3,2,1,0:T(8,128)(2,1)}, bf16[128,1024]{1,0:T(8,128)(2,1)S(1)}, bf16[128,1024]{1,0:T(8,128)(2,1)S(1)}) custom-call(bf16[8,8,32,256]{3,2,1,0:T(8,128)(2,1)S(1)} %all_to_all.21.own_ref, bf16[8,8,32,256]{3,2,1,0:T(8,128)(2,1)S(1)} %collective-permute-done.oth_ref, bf16[128,1024]{1,0:T(8,128)(2,1)S(1)} %get-tuple-element.19.act_ref, ...), custom_call_target="tpu_custom_call" | custom-call | tf_op jit(solution)/shard_map/hidden/pallas_call | solution.py:237
  56.3 0.0 reduce-scatter.2.cloned.1.call-update
  56.3 0.0 copy-start.2
  56.3 1.6 %copy-done.2 = bf16[4,4,256,256]{3,2,1,0:T(8,128)(2,1)S(1)} copy-done((bf16[4,4,256,256]{3,2,1,0:T(8,128)(2,1)S(1)}, bf16[4,4,256,256]{3,2,1,0:T(8,128)(2,1)}, u32[]{:S(2)}) %copy-start.2) | copy-done | bytes 2097176
  57.9 1.3 project.1
  59.2 0.5 collective-permute-start.1
  59.6 2.3 %collective-permute-done.1 = bf16[8,8,32,256]{3,2,1,0:T(8,128)(2,1)S(1)} collective-permute-done((bf16[8,8,32,256]{3,2,1,0:T(8,128)(2,1)S(1)}, bf16[8,8,32,256]{3,2,1,0:T(8,128)(2,1)S(1)}, u32[]{:S(2)}, u32[]{:S(2)}) %collective-permute-start.1) | collective-permute-done | bytes 1048608 | tf_op jit(solution)/shard_map/ppermute | solution.py:263
  61.9 0.4 add_convert_fusion
  62.3 19.0 %all_to_all.22.got_ref = bf16[8,8,32,256]{3,2,1,0:T(8,128)(2,1)S(1)} all-to-all(bf16[8,8,32,256]{3,2,1,0:T(8,128)(2,1)S(1)} %add_convert_fusion), channel_id=1, replica_groups={{0,2,4,6,8,10,12,14},{1,3,5,7,9,11,13,15},{16,18,20,22,24,26,28,30},{17..., dimensions={0} | all-to-all | bytes 2097152 | tf_op jit(solution)/shard_map/all_to_all | solution.py:265
  81.3 0.8 sort.1
  82.1 15.4 %all_to_all.23 = bf16[16,32,512]{2,1,0:T(8,128)(2,1)S(1)} all-to-all(bf16[16,32,512]{2,1,0:T(8,128)(2,1)S(1)} %sort.1), channel_id=1, replica_groups=mesh['dp'=16,'mp'=16] {'mp'}, dimensions={0} | all-to-all | bytes 1048576 | tf_op jit(solution)/shard_map/all_to_all | solution.py:274
  97.6 0.8 fusion
  98.4 11.9 %reduce-scatter.2.cloned.1.call-done = bf16[1024,256]{1,0:T(8,128)(2,1)} async-done(((bf16[8192,256]{1,0:T(8,128)(2,1)}), bf16[1024,256]{1,0:T(8,128)(2,1)}) %reduce-scatter.2.cloned.1.call-update) | async-done | bytes 524304 | tf_op jit(solution)/shard_map/reduce_scatter | solution.py:251
  110.3 1.0 fetch_away.1
  111.3 1.3 %collective-permute-start.2 = (bf16[2,4,4,16,256]{4,3,2,1,0:T(8,128)(2,1)S(1)}, bf16[2,4,4,16,256]{4,3,2,1,0:T(8,128)(2,1)S(1)}, u32[]{:S(2)}, u32[]{:S(2)}) collective-permute-start(bf16[2,4,4,16,256]{4,3,2,1,0:T(8,128)(2,1)S(1)} %fetch_away.1), channel_id=1, source_target_pairs={{0,16},{16,0},{32,48},{48,32},{64,80},{80,64},{96,112},{112,96},{1... | collective-permute-start | bytes 786440 | tf_op jit(solution)/shard_map/ppermute | solution.py:290
  112.5 1.0 fetch_own.1.own_ref
  113.5 5.1 %collective-permute-done.2.came_ref = bf16[2,4,4,16,256]{4,3,2,1,0:T(8,128)(2,1)S(1)} collective-permute-done((bf16[2,4,4,16,256]{4,3,2,1,0:T(8,128)(2,1)S(1)}, bf16[2,4,4,16,256]{4,3,2,1,0:T(8,128)(2,1)S(1)}, u32[]{:S(2)}, u32[]{:S(2)}) %collective-permute-start.2) | collective-permute-done | bytes 262176 | tf_op jit(solution)/shard_map/ppermute | solution.py:290
  118.6 0.8 finish.1
Async XLA Ops:
  7.2 103.1 %reduce-scatter.2.cloned.1.call-start = ((), (), s32[]{:S(2)}) async-start(), calls=%async_computation.5 | async-start | bytes 4718592 | tf_op jit(solution)/shard_map/reduce_scatter | solution.py:251
  7.2 43.5 %copy-start.1 = (bf16[4,4,256,256]{3,2,1,0:T(8,128)(2,1)S(1)}, bf16[4,4,256,256]{3,2,1,0:T(8,128)(2,1)}, u32[]{:S(2)}) copy-start(bf16[4,4,256,256]{3,2,1,0:T(8,128)(2,1)} %wout_ref.5) | copy-start | bytes 6291460
  8.6 42.2 %copy-start = (bf16[4,4,256,256]{3,2,1,0:T(8,128)(2,1)S(1)}, bf16[4,4,256,256]{3,2,1,0:T(8,128)(2,1)}, u32[]{:S(2)}) copy-start(bf16[4,4,256,256]{3,2,1,0:T(8,128)(2,1)} %win_ref.5) | copy-start | bytes 6291460
  49.4 3.6 %collective-permute-start = (bf16[8,8,32,256]{3,2,1,0:T(8,128)(2,1)S(1)}, bf16[8,8,32,256]{3,2,1,0:T(8,128)(2,1)S(1)}, u32[]{:S(2)}, u32[]{:S(2)}) collective-permute-start(bf16[8,8,32,256]{3,2,1,0:T(8,128)(2,1)S(1)} %all_to_all.21.own_ref), channel_id=1, source_target_pairs={{0,1},{1,0},{2,3},{3,2},{4,5},{5,4},{6,7},{7,6},{8,9},{9,8},{10,11... | collective-permute-start | bytes 3145736 | tf_op jit(solution)/shard_map/ppermute | solution.py:226
  56.3 1.6 %copy-start.2 = (bf16[4,4,256,256]{3,2,1,0:T(8,128)(2,1)S(1)}, bf16[4,4,256,256]{3,2,1,0:T(8,128)(2,1)}, u32[]{:S(2)}) copy-start(bf16[4,4,256,256]{3,2,1,0:T(8,128)(2,1)} %wout_ref.5) | copy-start | bytes 6291460
  59.2 2.7 %collective-permute-start.1 = (bf16[8,8,32,256]{3,2,1,0:T(8,128)(2,1)S(1)}, bf16[8,8,32,256]{3,2,1,0:T(8,128)(2,1)S(1)}, u32[]{:S(2)}, u32[]{:S(2)}) collective-permute-start(bf16[8,8,32,256]{3,2,1,0:T(8,128)(2,1)S(1)} %get-tuple-element.26), channel_id=1, source_target_pairs={{0,1},{1,0},{2,3},{3,2},{4,5},{5,4},{6,7},{7,6},{8,9},{9,8},{10,11... | collective-permute-start | bytes 3145736 | tf_op jit(solution)/shard_map/ppermute | solution.py:263
  111.3 7.3 %collective-permute-start.2 = (bf16[2,4,4,16,256]{4,3,2,1,0:T(8,128)(2,1)S(1)}, bf16[2,4,4,16,256]{4,3,2,1,0:T(8,128)(2,1)S(1)}, u32[]{:S(2)}, u32[]{:S(2)}) collective-permute-start(bf16[2,4,4,16,256]{4,3,2,1,0:T(8,128)(2,1)S(1)} %fetch_away.1), channel_id=1, source_target_pairs={{0,16},{16,0},{32,48},{48,32},{64,80},{80,64},{96,112},{112,96},{1... | collective-permute-start | bytes 786440 | tf_op jit(solution)/shard_map/ppermute | solution.py:290
Sparse Core Ops, SparseCore 0:
  56.4 53.8 reduce-scatter.1

commit v8 on v7

--- a/solution.py
+++ b/solution.py
@@ -173,20 +173,17 @@
                 out_ref[owner, rows, pl.ds(half, SIDE)] = total.astype(BF16)
 
 
-def fetch_kernel(which, sum_ref, half_ref, sem):
-    copy = pltpu.make_async_copy(sum_ref.at[which], half_ref, sem)
+def fetch_kernel(half, which, sum_ref, part_ref, sem):
+    copy = pltpu.make_async_copy(sum_ref.at[half, which], part_ref, sem)
     copy.start()
     copy.wait()
 
 
-def finish_kernel(scale, own_ref, came_ref, in_ref, out_ref, held, sems):
-    copies = []
-    for which, ref in enumerate((in_ref, out_ref)):
-        held[which] = (own_ref[which].astype(F32) + came_ref[which].astype(F32)) * scale
-        copies.append(pltpu.make_async_copy(held.at[which], ref, sems.at[which]))
-        copies[-1].start()
-    for copy in copies:
-        copy.wait()
+def finish_kernel(scale, own_ref, came_ref, out_ref, held, sem):
+    held[...] = (own_ref[...].astype(F32) + came_ref[...].astype(F32)) * scale
+    copy = pltpu.make_async_copy(held, out_ref, sem)
+    copy.start()
+    copy.wait()
 
 
 def shards(tokens, cotangent, w_in, w_out, in_blocks, out_blocks):
@@ -278,30 +275,31 @@
     grad_sum, output, grad_tokens = lax.optimization_barrier((grad_sum, output, grad_tokens))
     halves = grad_sum.reshape(2, 2, 4, 4, SLICE, SIDE)
     summed = in_hbm(halves)
-    fetch = lambda which, name: pl.pallas_call(
-        functools.partial(fetch_kernel, which),
-        out_shape=jax.ShapeDtypeStruct((2, 4, 4, SLICE, SIDE), BF16),
+    part = (4, 4, SLICE, SIDE)
+    fetch = lambda half, which, name: pl.pallas_call(
+        functools.partial(fetch_kernel, half, which),
+        out_shape=jax.ShapeDtypeStruct(part, BF16),
         in_specs=[HBM],
         out_specs=VMEM,
         scratch_shapes=[pltpu.SemaphoreType.DMA],
         compiler_params=params(),
         name=name,
     )(summed)
-    came = lax.ppermute(fetch(1, "fetch_away"), "dp", [(i, i ^ 1) for i in range(n_dp)])
-    mine = fetch(0, "fetch_own")
-    grad_shape = pltpu.HBM((4, 4, SLICE, SIDE), F32)
-    grad_in, grad_out = pl.pallas_call(
-        functools.partial(finish_kernel, 1.0 / math.sqrt(total_tok)),
-        out_shape=(grad_shape, grad_shape),
-        in_specs=[VMEM, VMEM],
-        out_specs=(HBM, HBM),
-        scratch_shapes=[
-            pltpu.VMEM((2, 4, 4, SLICE, SIDE), F32),
-            pltpu.SemaphoreType.DMA((2,)),
-        ],
-        compiler_params=params(),
-        name="finish",
-    )(mine, came)
+    across = [(i, i ^ 1) for i in range(n_dp)]
+    came = [lax.ppermute(fetch(1, which, "fetch_away"), "dp", across) for which in range(2)]
+    mine = [fetch(0, which, "fetch_own") for which in range(2)]
+    grad_in, grad_out = [
+        pl.pallas_call(
+            functools.partial(finish_kernel, 1.0 / math.sqrt(total_tok)),
+            out_shape=pltpu.HBM(part, F32),
+            in_specs=[VMEM, VMEM],
+            out_specs=HBM,
+            scratch_shapes=[pltpu.VMEM(part, F32), pltpu.SemaphoreType.DMA],
+            compiler_params=params(),
+            name="finish",
+        )(mine[which], came[which])
+        for which in range(2)
+    ]
     return output, grad_tokens, grad_in, grad_out
 
 

time: 127 us -> 127 us (level)
  waiting for transfers between devices: 20.5 us -> 17.8 us
  Pallas kernels: 11 us -> 13.3 us
    ppermute x1 -> x2, waiting for transfers between devices: 5.08 us -> 2.46 us  [shards(): lax.ppermute(fetch(1, which, 'fetch_away'), 'dp', across)]
    pallas_call x2 -> x4, Pallas kernels: 1.91 us -> 3.65 us  [shards(): pl.pallas_call(functools.partial(fetch_kernel, half, which), out_shape=ja...]
  transfers between devices with their start and end apart: 4 -> 5, of which waited for: 4 -> 5; matrix products, arithmetic and copies ran while one was open for 1% -> 1% of each run, Pallas kernels for 3% -> 5%
where the time goes in v8:
time: 127 us; the launch traced here: 126 us
  blocking collectives  74.8 us (59%)
  waiting for transfers between devices  17.8 us (14%)
  between operations  14.2 us (11%)
  Pallas kernels  13.3 us (10%)
  starting transfers between devices  3.41 us (3%)
  local copies, waits for them, and re-layouts  2.42 us (2%)
    all_to_all x1, blocking collectives, shards(): got = lax.all_to_all(packed, 'mp', 0, 0, tiled=True)  21.1 us
    all_to_all x1, blocking collectives, shards(): lax.all_to_all(chosen, 'mp', 0, 0, axis_index_groups=same_core, tiled=True)  19.3 us
    all_to_all x1, blocking collectives, shards(): lax.all_to_all(part, 'mp', 0, 0, axis_index_groups=same_core, tiled=True)  19 us
    all_to_all x1, blocking collectives, shards(): final = lax.all_to_all(sorted_, 'mp', 0, 0, tiled=True)  15.4 us
    reduce_scatter x1, waiting for transfers between devices, shards(): lax.psum_scatter(grads.reshape(-1, SIDE), 'dp', scatter_dimension=0, axis...  11.9 us
    pallas_call x4, Pallas kernels, shards(): pl.pallas_call(functools.partial(fetch_kernel, half, which), out_shape=ja...  3.65 us
    pallas_call x1, Pallas kernels, shards(): pl.pallas_call(hidden_kernel, out_shape=(pltpu.HBM((zs, 2, 2, 4, 4, SLICE...  3.27 us
  transfers between devices with their start and end apart: 5, of which 5 were waited for; matrix products, arithmetic and copies ran while one was open for 1% of the time, Pallas kernels for 5%

profile of v8, /device:TPU:1, one launch (start us, length us, event | category | flops | bytes accessed | tf_op | source)
XLA Modules:
  0.0 126.4 jit_solution(9117952468506556109)
XLA Ops:
  7.2 0.0 reduce-scatter.2.cloned.1.call-start
  7.2 0.0 copy-start.1
  7.2 1.3 %pack.1 = bf16[16,144,128]{2,1,0:T(8,128)(2,1)S(1)} custom-call(bf16[16,16,512]{2,1,0:T(8,128)(2,1)} %bitcast.11, bf16[16,16,512]{2,1,0:T(8,128)(2,1)} %bitcast.12, s32[4,4]{1,0:T(4,128)} %p_ref.1, s32[4,4]{1,0:T(4,128)} %q_ref.1), custom_call_target="tpu_custom_call" | custom-call | tf_op jit(solution)/shard_map/pack/pallas_call | solution.py:198
  8.6 0.0 copy-start
  8.6 21.1 %all_to_all.20.got_ref = bf16[16,144,128]{2,1,0:T(8,128)(2,1)S(1)} all-to-all(bf16[16,144,128]{2,1,0:T(8,128)(2,1)S(1)} %pack.1), channel_id=1, replica_groups=mesh['dp'=16,'mp'=16] {'mp'}, dimensions={0} | all-to-all | bytes 1179648 | tf_op jit(solution)/shard_map/all_to_all | solution.py:212
  29.7 0.4 select.1
  30.1 19.3 %all_to_all.21.own_ref = bf16[8,8,32,256]{3,2,1,0:T(8,128)(2,1)S(1)} all-to-all(bf16[8,8,32,256]{3,2,1,0:T(8,128)(2,1)S(1)} %get-tuple-element.16), channel_id=1, replica_groups={{0,2,4,6,8,10,12,14},{1,3,5,7,9,11,13,15},{16,18,20,22,24,26,28,30},{17..., dimensions={0} | all-to-all | bytes 2097152 | tf_op jit(solution)/shard_map/all_to_all | solution.py:222
  49.4 1.3 %collective-permute-start = (bf16[8,8,32,256]{3,2,1,0:T(8,128)(2,1)S(1)}, bf16[8,8,32,256]{3,2,1,0:T(8,128)(2,1)S(1)}, u32[]{:S(2)}, u32[]{:S(2)}) collective-permute-start(bf16[8,8,32,256]{3,2,1,0:T(8,128)(2,1)S(1)} %all_to_all.21.own_ref), channel_id=1, source_target_pairs={{0,1},{1,0},{2,3},{3,2},{4,5},{5,4},{6,7},{7,6},{8,9},{9,8},{10,11... | collective-permute-start | bytes 3145736 | tf_op jit(solution)/shard_map/ppermute | solution.py:223
  50.7 0.0 copy-done.1
  50.7 0.0 copy-done
  50.7 1.1 first.1
  51.8 1.2 collective-permute-done.oth_ref
  53.0 3.3 %hidden.1 = (bf16[8,2,2,4,4,16,256]{6,5,4,3,2,1,0:T(8,128)(2,1)}, bf16[128,1024]{1,0:T(8,128)(2,1)S(1)}, bf16[128,1024]{1,0:T(8,128)(2,1)S(1)}) custom-call(bf16[8,8,32,256]{3,2,1,0:T(8,128)(2,1)S(1)} %all_to_all.21.own_ref, bf16[8,8,32,256]{3,2,1,0:T(8,128)(2,1)S(1)} %collective-permute-done.oth_ref, bf16[128,1024]{1,0:T(8,128)(2,1)S(1)} %get-tuple-element.17.act_ref, ...), custom_call_target="tpu_custom_call" | custom-call | tf_op jit(solution)/shard_map/hidden/pallas_call | solution.py:234
  56.3 0.0 reduce-scatter.2.cloned.1.call-update
  56.3 0.0 copy-start.2
  56.3 1.6 %copy-done.2 = bf16[4,4,256,256]{3,2,1,0:T(8,128)(2,1)S(1)} copy-done((bf16[4,4,256,256]{3,2,1,0:T(8,128)(2,1)S(1)}, bf16[4,4,256,256]{3,2,1,0:T(8,128)(2,1)}, u32[]{:S(2)}) %copy-start.2) | copy-done | bytes 2097176
  57.9 1.3 project.1
  59.2 0.5 collective-permute-start.1
  59.6 2.3 %collective-permute-done.1 = bf16[8,8,32,256]{3,2,1,0:T(8,128)(2,1)S(1)} collective-permute-done((bf16[8,8,32,256]{3,2,1,0:T(8,128)(2,1)S(1)}, bf16[8,8,32,256]{3,2,1,0:T(8,128)(2,1)S(1)}, u32[]{:S(2)}, u32[]{:S(2)}) %collective-permute-start.1) | collective-permute-done | bytes 1048608 | tf_op jit(solution)/shard_map/ppermute | solution.py:260
  61.9 0.4 add_convert_fusion
  62.3 19.0 %all_to_all.22.got_ref = bf16[8,8,32,256]{3,2,1,0:T(8,128)(2,1)S(1)} all-to-all(bf16[8,8,32,256]{3,2,1,0:T(8,128)(2,1)S(1)} %add_convert_fusion), channel_id=1, replica_groups={{0,2,4,6,8,10,12,14},{1,3,5,7,9,11,13,15},{16,18,20,22,24,26,28,30},{17..., dimensions={0} | all-to-all | bytes 2097152 | tf_op jit(solution)/shard_map/all_to_all | solution.py:262
  81.3 0.8 sort.1
  82.1 15.4 %all_to_all.23 = bf16[16,32,512]{2,1,0:T(8,128)(2,1)S(1)} all-to-all(bf16[16,32,512]{2,1,0:T(8,128)(2,1)S(1)} %sort.1), channel_id=1, replica_groups=mesh['dp'=16,'mp'=16] {'mp'}, dimensions={0} | all-to-all | bytes 1048576 | tf_op jit(solution)/shard_map/all_to_all | solution.py:271
  97.6 0.8 fusion
  98.4 11.9 %reduce-scatter.2.cloned.1.call-done = bf16[1024,256]{1,0:T(8,128)(2,1)} async-done(((bf16[8192,256]{1,0:T(8,128)(2,1)}), bf16[1024,256]{1,0:T(8,128)(2,1)}) %reduce-scatter.2.cloned.1.call-update) | async-done | bytes 524304 | tf_op jit(solution)/shard_map/reduce_scatter | solution.py:248
  110.3 0.9 fetch_away.2
  111.2 1.3 %collective-permute-start.2 = (bf16[4,4,16,256]{3,2,1,0:T(8,128)(2,1)S(1)}, bf16[4,4,16,256]{3,2,1,0:T(8,128)(2,1)S(1)}, u32[]{:S(2)}, u32[]{:S(2)}) collective-permute-start(bf16[4,4,16,256]{3,2,1,0:T(8,128)(2,1)S(1)} %fetch_away.2), channel_id=1, source_target_pairs={{0,16},{16,0},{32,48},{48,32},{64,80},{80,64},{96,112},{112,96},{1... | collective-permute-start | bytes 393224 | tf_op jit(solution)/shard_map/ppermute | solution.py:289
  112.5 0.9 fetch_away.3
  113.4 0.4 collective-permute-start.3
  113.8 0.9 fetch_own.3.own_ref
  114.7 0.9 fetch_own.2.own_ref
  115.6 0.1 collective-permute-done.2.came_ref
  115.7 0.7 finish.2
  116.5 2.4 %collective-permute-done.3.came_ref = bf16[4,4,16,256]{3,2,1,0:T(8,128)(2,1)S(1)} collective-permute-done((bf16[4,4,16,256]{3,2,1,0:T(8,128)(2,1)S(1)}, bf16[4,4,16,256]{3,2,1,0:T(8,128)(2,1)S(1)}, u32[]{:S(2)}, u32[]{:S(2)}) %collective-permute-start.3) | collective-permute-done | bytes 131104 | tf_op jit(solution)/shard_map/ppermute | solution.py:289
  118.8 0.7 finish.3
Async XLA Ops:
  7.2 103.1 %reduce-scatter.2.cloned.1.call-start = ((), (), s32[]{:S(2)}) async-start(), calls=%async_computation.5 | async-start | bytes 4718592 | tf_op jit(solution)/shard_map/reduce_scatter | solution.py:248
  7.2 43.5 %copy-start.1 = (bf16[4,4,256,256]{3,2,1,0:T(8,128)(2,1)S(1)}, bf16[4,4,256,256]{3,2,1,0:T(8,128)(2,1)}, u32[]{:S(2)}) copy-start(bf16[4,4,256,256]{3,2,1,0:T(8,128)(2,1)} %wout_ref.5) | copy-start | bytes 6291460
  8.6 42.2 %copy-start = (bf16[4,4,256,256]{3,2,1,0:T(8,128)(2,1)S(1)}, bf16[4,4,256,256]{3,2,1,0:T(8,128)(2,1)}, u32[]{:S(2)}) copy-start(bf16[4,4,256,256]{3,2,1,0:T(8,128)(2,1)} %win_ref.5) | copy-start | bytes 6291460
  49.4 3.6 %collective-permute-start = (bf16[8,8,32,256]{3,2,1,0:T(8,128)(2,1)S(1)}, bf16[8,8,32,256]{3,2,1,0:T(8,128)(2,1)S(1)}, u32[]{:S(2)}, u32[]{:S(2)}) collective-permute-start(bf16[8,8,32,256]{3,2,1,0:T(8,128)(2,1)S(1)} %all_to_all.21.own_ref), channel_id=1, source_target_pairs={{0,1},{1,0},{2,3},{3,2},{4,5},{5,4},{6,7},{7,6},{8,9},{9,8},{10,11... | collective-permute-start | bytes 3145736 | tf_op jit(solution)/shard_map/ppermute | solution.py:223
  56.3 1.6 %copy-start.2 = (bf16[4,4,256,256]{3,2,1,0:T(8,128)(2,1)S(1)}, bf16[4,4,256,256]{3,2,1,0:T(8,128)(2,1)}, u32[]{:S(2)}) copy-start(bf16[4,4,256,256]{3,2,1,0:T(8,128)(2,1)} %wout_ref.5) | copy-start | bytes 6291460
  59.2 2.7 %collective-permute-start.1 = (bf16[8,8,32,256]{3,2,1,0:T(8,128)(2,1)S(1)}, bf16[8,8,32,256]{3,2,1,0:T(8,128)(2,1)S(1)}, u32[]{:S(2)}, u32[]{:S(2)}) collective-permute-start(bf16[8,8,32,256]{3,2,1,0:T(8,128)(2,1)S(1)} %get-tuple-element.24), channel_id=1, source_target_pairs={{0,1},{1,0},{2,3},{3,2},{4,5},{5,4},{6,7},{7,6},{8,9},{9,8},{10,11... | collective-permute-start | bytes 3145736 | tf_op jit(solution)/shard_map/ppermute | solution.py:260
  111.2 4.5 %collective-permute-start.2 = (bf16[4,4,16,256]{3,2,1,0:T(8,128)(2,1)S(1)}, bf16[4,4,16,256]{3,2,1,0:T(8,128)(2,1)S(1)}, u32[]{:S(2)}, u32[]{:S(2)}) collective-permute-start(bf16[4,4,16,256]{3,2,1,0:T(8,128)(2,1)S(1)} %fetch_away.2), channel_id=1, source_target_pairs={{0,16},{16,0},{32,48},{48,32},{64,80},{80,64},{96,112},{112,96},{1... | collective-permute-start | bytes 393224 | tf_op jit(solution)/shard_map/ppermute | solution.py:289
  113.4 5.4 %collective-permute-start.3 = (bf16[4,4,16,256]{3,2,1,0:T(8,128)(2,1)S(1)}, bf16[4,4,16,256]{3,2,1,0:T(8,128)(2,1)S(1)}, u32[]{:S(2)}, u32[]{:S(2)}) collective-permute-start(bf16[4,4,16,256]{3,2,1,0:T(8,128)(2,1)S(1)} %fetch_away.3), channel_id=1, source_target_pairs={{0,16},{16,0},{32,48},{48,32},{64,80},{80,64},{96,112},{112,96},{1... | collective-permute-start | bytes 393224 | tf_op jit(solution)/shard_map/ppermute | solution.py:289
Sparse Core Ops, SparseCore 0:
  56.4 53.8 reduce-scatter.1

commit v9 on v8

--- a/solution.py
+++ b/solution.py
@@ -173,10 +173,15 @@
                 out_ref[owner, rows, pl.ds(half, SIDE)] = total.astype(BF16)
 
 
-def fetch_kernel(half, which, sum_ref, part_ref, sem):
-    copy = pltpu.make_async_copy(sum_ref.at[half, which], part_ref, sem)
-    copy.start()
-    copy.wait()
+def fetch_kernel(half, sum_ref, in_ref, out_ref, sems):
+    copies = [
+        pltpu.make_async_copy(sum_ref.at[half, which], ref, sems.at[which])
+        for which, ref in enumerate((in_ref, out_ref))
+    ]
+    for copy in copies:
+        copy.start()
+    for copy in copies:
+        copy.wait()
 
 
 def finish_kernel(scale, own_ref, came_ref, out_ref, held, sem):
@@ -276,18 +281,19 @@
     halves = grad_sum.reshape(2, 2, 4, 4, SLICE, SIDE)
     summed = in_hbm(halves)
     part = (4, 4, SLICE, SIDE)
-    fetch = lambda half, which, name: pl.pallas_call(
-        functools.partial(fetch_kernel, half, which),
-        out_shape=jax.ShapeDtypeStruct(part, BF16),
+    fetched = jax.ShapeDtypeStruct(part, BF16)
+    fetch = lambda half, name: pl.pallas_call(
+        functools.partial(fetch_kernel, half),
+        out_shape=(fetched, fetched),
         in_specs=[HBM],
-        out_specs=VMEM,
-        scratch_shapes=[pltpu.SemaphoreType.DMA],
+        out_specs=(VMEM, VMEM),
+        scratch_shapes=[pltpu.SemaphoreType.DMA((2,))],
         compiler_params=params(),
         name=name,
     )(summed)
     across = [(i, i ^ 1) for i in range(n_dp)]
-    came = [lax.ppermute(fetch(1, which, "fetch_away"), "dp", across) for which in range(2)]
-    mine = [fetch(0, which, "fetch_own") for which in range(2)]
+    came = [lax.ppermute(away, "dp", across) for away in fetch(1, "fetch_away")]
+    mine = fetch(0, "fetch_own")
     grad_in, grad_out = [
         pl.pallas_call(
             functools.partial(finish_kernel, 1.0 / math.sqrt(total_tok)),

time: 127 us -> 127 us (level)
  Pallas kernels: 13.3 us -> 11.7 us
  waiting for transfers between devices: 17.8 us -> 19.4 us
    pallas_call x4 -> x2, Pallas kernels: 3.65 us -> 1.97 us  [shards(): pl.pallas_call(functools.partial(fetch_kernel, half), out_shape=(fetched,...]
    ppermute x2, waiting for transfers between devices: 2.46 us -> 4.02 us  [shards(): came = [lax.ppermute(away, 'dp', across) for away in fetch(1, 'fetch_away')]]
  transfers between devices with their start and end apart: 5 -> 5, of which waited for: 5 -> 5; matrix products, arithmetic and copies ran while one was open for 1% -> 1% of each run, Pallas kernels for 5% -> 4%
where the time goes in v9:
time: 127 us; the launch traced here: 126 us
  blocking collectives  74.8 us (59%)
  waiting for transfers between devices  19.4 us (15%)
  between operations  14.2 us (11%)
  Pallas kernels  11.7 us (9%)
  starting transfers between devices  3.33 us (3%)
  local copies, waits for them, and re-layouts  2.42 us (2%)
    all_to_all x1, blocking collectives, shards(): got = lax.all_to_all(packed, 'mp', 0, 0, tiled=True)  21.1 us
    all_to_all x1, blocking collectives, shards(): lax.all_to_all(chosen, 'mp', 0, 0, axis_index_groups=same_core, tiled=True)  19.3 us
    all_to_all x1, blocking collectives, shards(): lax.all_to_all(part, 'mp', 0, 0, axis_index_groups=same_core, tiled=True)  19 us
    all_to_all x1, blocking collectives, shards(): final = lax.all_to_all(sorted_, 'mp', 0, 0, tiled=True)  15.4 us
    reduce_scatter x1, waiting for transfers between devices, shards(): lax.psum_scatter(grads.reshape(-1, SIDE), 'dp', scatter_dimension=0, axis...  11.9 us
    ppermute x2, waiting for transfers between devices, shards(): came = [lax.ppermute(away, 'dp', across) for away in fetch(1, 'fetch_away')]  4.02 us
    pallas_call x1, Pallas kernels, shards(): pl.pallas_call(hidden_kernel, out_shape=(pltpu.HBM((zs, 2, 2, 4, 4, SLICE...  3.34 us
  transfers between devices with their start and end apart: 5, of which 5 were waited for; matrix products, arithmetic and copies ran while one was open for 1% of the time, Pallas kernels for 4%

profile of v9, /device:TPU:1, one launch (start us, length us, event | category | flops | bytes accessed | tf_op | source)
XLA Modules:
  0.0 126.3 jit_solution(952317385540580912)
XLA Ops:
  7.2 0.0 reduce-scatter.2.cloned.1.call-start
  7.2 0.0 copy-start.1
  7.2 1.3 %pack.1 = bf16[16,144,128]{2,1,0:T(8,128)(2,1)S(1)} custom-call(bf16[16,16,512]{2,1,0:T(8,128)(2,1)} %bitcast.9, bf16[16,16,512]{2,1,0:T(8,128)(2,1)} %bitcast.10, s32[4,4]{1,0:T(4,128)} %p_ref.1, s32[4,4]{1,0:T(4,128)} %q_ref.1), custom_call_target="tpu_custom_call" | custom-call | tf_op jit(solution)/shard_map/pack/pallas_call | solution.py:203
  8.6 0.0 copy-start
  8.6 21.1 %all_to_all.20.got_ref = bf16[16,144,128]{2,1,0:T(8,128)(2,1)S(1)} all-to-all(bf16[16,144,128]{2,1,0:T(8,128)(2,1)S(1)} %pack.1), channel_id=1, replica_groups=mesh['dp'=16,'mp'=16] {'mp'}, dimensions={0} | all-to-all | bytes 1179648 | tf_op jit(solution)/shard_map/all_to_all | solution.py:217
  29.7 0.4 select.1
  30.1 19.3 %all_to_all.21.own_ref = bf16[8,8,32,256]{3,2,1,0:T(8,128)(2,1)S(1)} all-to-all(bf16[8,8,32,256]{3,2,1,0:T(8,128)(2,1)S(1)} %get-tuple-element.20), channel_id=1, replica_groups={{0,2,4,6,8,10,12,14},{1,3,5,7,9,11,13,15},{16,18,20,22,24,26,28,30},{17..., dimensions={0} | all-to-all | bytes 2097152 | tf_op jit(solution)/shard_map/all_to_all | solution.py:227
  49.4 1.3 %collective-permute-start = (bf16[8,8,32,256]{3,2,1,0:T(8,128)(2,1)S(1)}, bf16[8,8,32,256]{3,2,1,0:T(8,128)(2,1)S(1)}, u32[]{:S(2)}, u32[]{:S(2)}) collective-permute-start(bf16[8,8,32,256]{3,2,1,0:T(8,128)(2,1)S(1)} %all_to_all.21.own_ref), channel_id=1, source_target_pairs={{0,1},{1,0},{2,3},{3,2},{4,5},{5,4},{6,7},{7,6},{8,9},{9,8},{10,11... | collective-permute-start | bytes 3145736 | tf_op jit(solution)/shard_map/ppermute | solution.py:228
  50.7 0.0 copy-done.1
  50.7 0.0 copy-done
  50.7 1.1 first.1
  51.8 1.2 collective-permute-done.oth_ref
  53.0 3.3 %hidden.1 = (bf16[8,2,2,4,4,16,256]{6,5,4,3,2,1,0:T(8,128)(2,1)}, bf16[128,1024]{1,0:T(8,128)(2,1)S(1)}, bf16[128,1024]{1,0:T(8,128)(2,1)S(1)}) custom-call(bf16[8,8,32,256]{3,2,1,0:T(8,128)(2,1)S(1)} %all_to_all.21.own_ref, bf16[8,8,32,256]{3,2,1,0:T(8,128)(2,1)S(1)} %collective-permute-done.oth_ref, bf16[128,1024]{1,0:T(8,128)(2,1)S(1)} %get-tuple-element.21.act_ref, ...), custom_call_target="tpu_custom_call" | custom-call | tf_op jit(solution)/shard_map/hidden/pallas_call | solution.py:239
  56.4 0.0 reduce-scatter.2.cloned.1.call-update
  56.4 0.0 copy-start.2
  56.4 1.6 %copy-done.2 = bf16[4,4,256,256]{3,2,1,0:T(8,128)(2,1)S(1)} copy-done((bf16[4,4,256,256]{3,2,1,0:T(8,128)(2,1)S(1)}, bf16[4,4,256,256]{3,2,1,0:T(8,128)(2,1)}, u32[]{:S(2)}) %copy-start.2) | copy-done | bytes 2097176
  58.0 1.3 project.1
  59.2 0.5 collective-permute-start.1
  59.7 2.3 %collective-permute-done.1 = bf16[8,8,32,256]{3,2,1,0:T(8,128)(2,1)S(1)} collective-permute-done((bf16[8,8,32,256]{3,2,1,0:T(8,128)(2,1)S(1)}, bf16[8,8,32,256]{3,2,1,0:T(8,128)(2,1)S(1)}, u32[]{:S(2)}, u32[]{:S(2)}) %collective-permute-start.1) | collective-permute-done | bytes 1048608 | tf_op jit(solution)/shard_map/ppermute | solution.py:265
  62.0 0.4 add_convert_fusion
  62.4 19.0 %all_to_all.22.got_ref = bf16[8,8,32,256]{3,2,1,0:T(8,128)(2,1)S(1)} all-to-all(bf16[8,8,32,256]{3,2,1,0:T(8,128)(2,1)S(1)} %add_convert_fusion), channel_id=1, replica_groups={{0,2,4,6,8,10,12,14},{1,3,5,7,9,11,13,15},{16,18,20,22,24,26,28,30},{17..., dimensions={0} | all-to-all | bytes 2097152 | tf_op jit(solution)/shard_map/all_to_all | solution.py:267
  81.4 0.8 sort.1
  82.2 15.4 %all_to_all.23 = bf16[16,32,512]{2,1,0:T(8,128)(2,1)S(1)} all-to-all(bf16[16,32,512]{2,1,0:T(8,128)(2,1)S(1)} %sort.1), channel_id=1, replica_groups=mesh['dp'=16,'mp'=16] {'mp'}, dimensions={0} | all-to-all | bytes 1048576 | tf_op jit(solution)/shard_map/all_to_all | solution.py:276
  97.6 0.8 fusion
  98.5 11.9 %reduce-scatter.2.cloned.1.call-done = bf16[1024,256]{1,0:T(8,128)(2,1)} async-done(((bf16[8192,256]{1,0:T(8,128)(2,1)}), bf16[1024,256]{1,0:T(8,128)(2,1)}) %reduce-scatter.2.cloned.1.call-update) | async-done | bytes 524304 | tf_op jit(solution)/shard_map/reduce_scatter | solution.py:253
  110.4 1.0 fetch_away.1
  111.3 1.3 %collective-permute-start.2 = (bf16[4,4,16,256]{3,2,1,0:T(8,128)(2,1)S(1)}, bf16[4,4,16,256]{3,2,1,0:T(8,128)(2,1)S(1)}, u32[]{:S(2)}, u32[]{:S(2)}) collective-permute-start(bf16[4,4,16,256]{3,2,1,0:T(8,128)(2,1)S(1)} %get-tuple-element.33), channel_id=1, source_target_pairs={{0,16},{16,0},{32,48},{48,32},{64,80},{80,64},{96,112},{112,96},{1... | collective-permute-start | bytes 393224 | tf_op jit(solution)/shard_map/ppermute | solution.py:295
  112.6 0.3 collective-permute-start.3
  112.9 1.0 fetch_own.1
  113.9 2.0 %collective-permute-done.2.came_ref = bf16[4,4,16,256]{3,2,1,0:T(8,128)(2,1)S(1)} collective-permute-done((bf16[4,4,16,256]{3,2,1,0:T(8,128)(2,1)S(1)}, bf16[4,4,16,256]{3,2,1,0:T(8,128)(2,1)S(1)}, u32[]{:S(2)}, u32[]{:S(2)}) %collective-permute-start.2) | collective-permute-done | bytes 131104 | tf_op jit(solution)/shard_map/ppermute | solution.py:295
  115.9 0.7 finish.2
  116.6 2.1 %collective-permute-done.3.came_ref = bf16[4,4,16,256]{3,2,1,0:T(8,128)(2,1)S(1)} collective-permute-done((bf16[4,4,16,256]{3,2,1,0:T(8,128)(2,1)S(1)}, bf16[4,4,16,256]{3,2,1,0:T(8,128)(2,1)S(1)}, u32[]{:S(2)}, u32[]{:S(2)}) %collective-permute-start.3) | collective-permute-done | bytes 131104 | tf_op jit(solution)/shard_map/ppermute | solution.py:295
  118.7 0.7 finish.3
Async XLA Ops:
  7.2 103.2 %reduce-scatter.2.cloned.1.call-start = ((), (), s32[]{:S(2)}) async-start(), calls=%async_computation.5 | async-start | bytes 4718592 | tf_op jit(solution)/shard_map/reduce_scatter | solution.py:253
  7.2 43.5 %copy-start.1 = (bf16[4,4,256,256]{3,2,1,0:T(8,128)(2,1)S(1)}, bf16[4,4,256,256]{3,2,1,0:T(8,128)(2,1)}, u32[]{:S(2)}) copy-start(bf16[4,4,256,256]{3,2,1,0:T(8,128)(2,1)} %wout_ref.5) | copy-start | bytes 6291460
  8.6 42.2 %copy-start = (bf16[4,4,256,256]{3,2,1,0:T(8,128)(2,1)S(1)}, bf16[4,4,256,256]{3,2,1,0:T(8,128)(2,1)}, u32[]{:S(2)}) copy-start(bf16[4,4,256,256]{3,2,1,0:T(8,128)(2,1)} %win_ref.5) | copy-start | bytes 6291460
  49.4 3.6 %collective-permute-start = (bf16[8,8,32,256]{3,2,1,0:T(8,128)(2,1)S(1)}, bf16[8,8,32,256]{3,2,1,0:T(8,128)(2,1)S(1)}, u32[]{:S(2)}, u32[]{:S(2)}) collective-permute-start(bf16[8,8,32,256]{3,2,1,0:T(8,128)(2,1)S(1)} %all_to_all.21.own_ref), channel_id=1, source_target_pairs={{0,1},{1,0},{2,3},{3,2},{4,5},{5,4},{6,7},{7,6},{8,9},{9,8},{10,11... | collective-permute-start | bytes 3145736 | tf_op jit(solution)/shard_map/ppermute | solution.py:228
  56.4 1.6 %copy-start.2 = (bf16[4,4,256,256]{3,2,1,0:T(8,128)(2,1)S(1)}, bf16[4,4,256,256]{3,2,1,0:T(8,128)(2,1)}, u32[]{:S(2)}) copy-start(bf16[4,4,256,256]{3,2,1,0:T(8,128)(2,1)} %wout_ref.5) | copy-start | bytes 6291460
  59.2 2.7 %collective-permute-start.1 = (bf16[8,8,32,256]{3,2,1,0:T(8,128)(2,1)S(1)}, bf16[8,8,32,256]{3,2,1,0:T(8,128)(2,1)S(1)}, u32[]{:S(2)}, u32[]{:S(2)}) collective-permute-start(bf16[8,8,32,256]{3,2,1,0:T(8,128)(2,1)S(1)} %get-tuple-element.28), channel_id=1, source_target_pairs={{0,1},{1,0},{2,3},{3,2},{4,5},{5,4},{6,7},{7,6},{8,9},{9,8},{10,11... | collective-permute-start | bytes 3145736 | tf_op jit(solution)/shard_map/ppermute | solution.py:265
  111.3 4.5 %collective-permute-start.2 = (bf16[4,4,16,256]{3,2,1,0:T(8,128)(2,1)S(1)}, bf16[4,4,16,256]{3,2,1,0:T(8,128)(2,1)S(1)}, u32[]{:S(2)}, u32[]{:S(2)}) collective-permute-start(bf16[4,4,16,256]{3,2,1,0:T(8,128)(2,1)S(1)} %get-tuple-element.33), channel_id=1, source_target_pairs={{0,16},{16,0},{32,48},{48,32},{64,80},{80,64},{96,112},{112,96},{1... | collective-permute-start | bytes 393224 | tf_op jit(solution)/shard_map/ppermute | solution.py:295
  112.6 6.0 %collective-permute-start.3 = (bf16[4,4,16,256]{3,2,1,0:T(8,128)(2,1)S(1)}, bf16[4,4,16,256]{3,2,1,0:T(8,128)(2,1)S(1)}, u32[]{:S(2)}, u32[]{:S(2)}) collective-permute-start(bf16[4,4,16,256]{3,2,1,0:T(8,128)(2,1)S(1)} %get-tuple-element.35), channel_id=1, source_target_pairs={{0,16},{16,0},{32,48},{48,32},{64,80},{80,64},{96,112},{112,96},{1... | collective-permute-start | bytes 393224 | tf_op jit(solution)/shard_map/ppermute | solution.py:295
Sparse Core Ops, SparseCore 0:
  56.5 53.8 reduce-scatter.1

commit v10 on v7

--- a/solution.py
+++ b/solution.py
@@ -55,7 +55,7 @@
 
 
 def select_kernel(got_ref, out_ref, lists_ref):
-    lists = jnp.max(got_ref[:, pl.ds(2 * TILES * SLICE, SLICE), :].astype(F32), axis=1).astype(jnp.int32)
+    lists = got_ref[:, pl.ds(2 * TILES * SLICE, SLICE), :].astype(F32)[:, 0, :].astype(jnp.int32)
     lists_ref[...] = lists
     chips = out_ref.shape[0]
     for group in range(chips // 2):
@@ -108,7 +108,7 @@
     grads_ref, more_act_ref, more_dpre_ref, held, sems,
 ):
     side = lax.axis_index("dp") & 1
-    zs = held.shape[2]
+    zs = held.shape[3]
     copies = []
     made = []
     for j in range(4):
@@ -122,13 +122,16 @@
         for k, slot in enumerate(slots_of(j)):
             x = jnp.concatenate([block_of(own_ref, 0, slot), block_of(oth_ref, 0, slot)], axis=0)
             dy = jnp.concatenate([block_of(own_ref, SLICE, slot), block_of(oth_ref, SLICE, slot)], axis=0)
-            g_in = dot(x, d_pre, 0, 0).astype(BF16).reshape(zs, 2, SLICE, SIDE)
-            g_out = dot(act, dy, 0, 0).astype(BF16).reshape(zs, 2, SLICE, SIDE)
-            for away in range(2):
-                held[j, k, :, away ^ side, 0] = g_in[:, away]
-                held[j, k, :, away ^ side, 1] = g_out[:, away]
-            copies.append(pltpu.make_async_copy(held.at[j, k], grads_ref.at[:, :, :, j, k], sems.at[j, k]))
-            copies[-1].start()
+            for which, (left, right) in enumerate(((x, d_pre), (act, dy))):
+                grad = dot(left, right, 0, 0).astype(BF16).reshape(zs, 2, SLICE, SIDE)
+                for away in range(2):
+                    held[j, k, which, :, away ^ side] = grad[:, away]
+                copies.append(
+                    pltpu.make_async_copy(
+                        held.at[j, k, which], grads_ref.at[:, :, which, j, k], sems.at[j, k, which]
+                    )
+                )
+                copies[-1].start()
     for copy in copies:
         copy.wait()
 
@@ -240,8 +243,8 @@
         in_specs=[VMEM] * 6,
         out_specs=(HBM, VMEM, VMEM),
         scratch_shapes=[
-            pltpu.VMEM((4, 4, zs, 2, 2, SLICE, SIDE), BF16),
-            pltpu.SemaphoreType.DMA((4, 4)),
+            pltpu.VMEM((4, 4, 2, zs, 2, SLICE, SIDE), BF16),
+            pltpu.SemaphoreType.DMA((4, 4, 2)),
         ],
         compiler_params=params(),
         name="hidden",

time: 127 us -> 127 us (level)
  no operation moved by 1% of the time
where the time goes in v10:
time: 127 us; the launch traced here: 126 us
  blocking collectives  74.8 us (59%)
  waiting for transfers between devices  20.5 us (16%)
  between operations  14.1 us (11%)
  Pallas kernels  11.1 us (9%)
  starting transfers between devices  3.04 us (2%)
  local copies, waits for them, and re-layouts  2.42 us (2%)
    all_to_all x1, blocking collectives, shards(): got = lax.all_to_all(packed, 'mp', 0, 0, tiled=True)  21.1 us
    all_to_all x1, blocking collectives, shards(): lax.all_to_all(chosen, 'mp', 0, 0, axis_index_groups=same_core, tiled=True)  19.3 us
    all_to_all x1, blocking collectives, shards(): lax.all_to_all(part, 'mp', 0, 0, axis_index_groups=same_core, tiled=True)  19 us
    all_to_all x1, blocking collectives, shards(): final = lax.all_to_all(sorted_, 'mp', 0, 0, tiled=True)  15.4 us
    reduce_scatter x1, waiting for transfers between devices, shards(): lax.psum_scatter(grads.reshape(-1, SIDE), 'dp', scatter_dimension=0, axis...  11.9 us
    ppermute x1, waiting for transfers between devices, shards(): lax.ppermute(fetch(1, 'fetch_away'), 'dp', [(i, i ^ 1) for i in range(n_d...  5.08 us
    pallas_call x1, Pallas kernels, shards(): pl.pallas_call(hidden_kernel, out_shape=(pltpu.HBM((zs, 2, 2, 4, 4, SLICE...  3.39 us
  transfers between devices with their start and end apart: 4, of which 4 were waited for; matrix products, arithmetic and copies ran while one was open for 1% of the time, Pallas kernels for 3%

profile of v10, /device:TPU:1, one launch (start us, length us, event | category | flops | bytes accessed | tf_op | source)
XLA Modules:
  0.0 126.4 jit_solution(6329333639574653552)
XLA Ops:
  7.2 0.0 reduce-scatter.2.cloned.1.call-start
  7.2 0.0 copy-start.1
  7.2 1.3 %pack.1 = bf16[16,144,128]{2,1,0:T(8,128)(2,1)S(1)} custom-call(bf16[16,16,512]{2,1,0:T(8,128)(2,1)} %bitcast.9, bf16[16,16,512]{2,1,0:T(8,128)(2,1)} %bitcast.10, s32[4,4]{1,0:T(4,128)} %p_ref.1, s32[4,4]{1,0:T(4,128)} %q_ref.1), custom_call_target="tpu_custom_call" | custom-call | tf_op jit(solution)/shard_map/pack/pallas_call | solution.py:204
  8.6 0.0 copy-start
  8.6 21.1 %all_to_all.20.got_ref = bf16[16,144,128]{2,1,0:T(8,128)(2,1)S(1)} all-to-all(bf16[16,144,128]{2,1,0:T(8,128)(2,1)S(1)} %pack.1), channel_id=1, replica_groups=mesh['dp'=16,'mp'=16] {'mp'}, dimensions={0} | all-to-all | bytes 1179648 | tf_op jit(solution)/shard_map/all_to_all | solution.py:218
  29.7 0.4 select.1
  30.1 19.3 %all_to_all.21.own_ref = bf16[8,8,32,256]{3,2,1,0:T(8,128)(2,1)S(1)} all-to-all(bf16[8,8,32,256]{3,2,1,0:T(8,128)(2,1)S(1)} %get-tuple-element.18), channel_id=1, replica_groups={{0,2,4,6,8,10,12,14},{1,3,5,7,9,11,13,15},{16,18,20,22,24,26,28,30},{17..., dimensions={0} | all-to-all | bytes 2097152 | tf_op jit(solution)/shard_map/all_to_all | solution.py:228
  49.4 1.3 %collective-permute-start = (bf16[8,8,32,256]{3,2,1,0:T(8,128)(2,1)S(1)}, bf16[8,8,32,256]{3,2,1,0:T(8,128)(2,1)S(1)}, u32[]{:S(2)}, u32[]{:S(2)}) collective-permute-start(bf16[8,8,32,256]{3,2,1,0:T(8,128)(2,1)S(1)} %all_to_all.21.own_ref), channel_id=1, source_target_pairs={{0,1},{1,0},{2,3},{3,2},{4,5},{5,4},{6,7},{7,6},{8,9},{9,8},{10,11... | collective-permute-start | bytes 3145736 | tf_op jit(solution)/shard_map/ppermute | solution.py:229
  50.7 0.0 copy-done.1
  50.7 0.0 copy-done
  50.7 1.1 first.1
  51.8 1.2 collective-permute-done.oth_ref
  53.0 3.4 %hidden.1 = (bf16[8,2,2,4,4,16,256]{6,5,4,3,2,1,0:T(8,128)(2,1)}, bf16[128,1024]{1,0:T(8,128)(2,1)S(1)}, bf16[128,1024]{1,0:T(8,128)(2,1)S(1)}) custom-call(bf16[8,8,32,256]{3,2,1,0:T(8,128)(2,1)S(1)} %all_to_all.21.own_ref, bf16[8,8,32,256]{3,2,1,0:T(8,128)(2,1)S(1)} %collective-permute-done.oth_ref, bf16[128,1024]{1,0:T(8,128)(2,1)S(1)} %get-tuple-element.19.act_ref, ...), custom_call_target="tpu_custom_call" | custom-call | tf_op jit(solution)/shard_map/hidden/pallas_call | solution.py:240
  56.4 0.0 reduce-scatter.2.cloned.1.call-update
  56.4 0.0 copy-start.2
  56.4 1.6 %copy-done.2 = bf16[4,4,256,256]{3,2,1,0:T(8,128)(2,1)S(1)} copy-done((bf16[4,4,256,256]{3,2,1,0:T(8,128)(2,1)S(1)}, bf16[4,4,256,256]{3,2,1,0:T(8,128)(2,1)}, u32[]{:S(2)}) %copy-start.2) | copy-done | bytes 2097176
  58.0 1.3 project.1
  59.3 0.5 collective-permute-start.1
  59.8 2.3 %collective-permute-done.1 = bf16[8,8,32,256]{3,2,1,0:T(8,128)(2,1)S(1)} collective-permute-done((bf16[8,8,32,256]{3,2,1,0:T(8,128)(2,1)S(1)}, bf16[8,8,32,256]{3,2,1,0:T(8,128)(2,1)S(1)}, u32[]{:S(2)}, u32[]{:S(2)}) %collective-permute-start.1) | collective-permute-done | bytes 1048608 | tf_op jit(solution)/shard_map/ppermute | solution.py:266
  62.0 0.4 add_convert_fusion
  62.5 19.0 %all_to_all.22.got_ref = bf16[8,8,32,256]{3,2,1,0:T(8,128)(2,1)S(1)} all-to-all(bf16[8,8,32,256]{3,2,1,0:T(8,128)(2,1)S(1)} %add_convert_fusion), channel_id=1, replica_groups={{0,2,4,6,8,10,12,14},{1,3,5,7,9,11,13,15},{16,18,20,22,24,26,28,30},{17..., dimensions={0} | all-to-all | bytes 2097152 | tf_op jit(solution)/shard_map/all_to_all | solution.py:268
  81.4 0.8 sort.1
  82.3 15.4 %all_to_all.23 = bf16[16,32,512]{2,1,0:T(8,128)(2,1)S(1)} all-to-all(bf16[16,32,512]{2,1,0:T(8,128)(2,1)S(1)} %sort.1), channel_id=1, replica_groups=mesh['dp'=16,'mp'=16] {'mp'}, dimensions={0} | all-to-all | bytes 1048576 | tf_op jit(solution)/shard_map/all_to_all | solution.py:277
  97.7 0.8 fusion
  98.5 11.9 %reduce-scatter.2.cloned.1.call-done = bf16[1024,256]{1,0:T(8,128)(2,1)} async-done(((bf16[8192,256]{1,0:T(8,128)(2,1)}), bf16[1024,256]{1,0:T(8,128)(2,1)}) %reduce-scatter.2.cloned.1.call-update) | async-done | bytes 524304 | tf_op jit(solution)/shard_map/reduce_scatter | solution.py:254
  110.4 1.0 fetch_away.1
  111.4 1.3 %collective-permute-start.2 = (bf16[2,4,4,16,256]{4,3,2,1,0:T(8,128)(2,1)S(1)}, bf16[2,4,4,16,256]{4,3,2,1,0:T(8,128)(2,1)S(1)}, u32[]{:S(2)}, u32[]{:S(2)}) collective-permute-start(bf16[2,4,4,16,256]{4,3,2,1,0:T(8,128)(2,1)S(1)} %fetch_away.1), channel_id=1, source_target_pairs={{0,16},{16,0},{32,48},{48,32},{64,80},{80,64},{96,112},{112,96},{1... | collective-permute-start | bytes 786440 | tf_op jit(solution)/shard_map/ppermute | solution.py:293
  112.6 1.0 fetch_own.1.own_ref
  113.6 5.1 %collective-permute-done.2.came_ref = bf16[2,4,4,16,256]{4,3,2,1,0:T(8,128)(2,1)S(1)} collective-permute-done((bf16[2,4,4,16,256]{4,3,2,1,0:T(8,128)(2,1)S(1)}, bf16[2,4,4,16,256]{4,3,2,1,0:T(8,128)(2,1)S(1)}, u32[]{:S(2)}, u32[]{:S(2)}) %collective-permute-start.2) | collective-permute-done | bytes 262176 | tf_op jit(solution)/shard_map/ppermute | solution.py:293
  118.7 0.8 finish.1
Async XLA Ops:
  7.2 103.2 %reduce-scatter.2.cloned.1.call-start = ((), (), s32[]{:S(2)}) async-start(), calls=%async_computation.5 | async-start | bytes 4718592 | tf_op jit(solution)/shard_map/reduce_scatter | solution.py:254
  7.2 43.5 %copy-start.1 = (bf16[4,4,256,256]{3,2,1,0:T(8,128)(2,1)S(1)}, bf16[4,4,256,256]{3,2,1,0:T(8,128)(2,1)}, u32[]{:S(2)}) copy-start(bf16[4,4,256,256]{3,2,1,0:T(8,128)(2,1)} %wout_ref.5) | copy-start | bytes 6291460
  8.6 42.1 %copy-start = (bf16[4,4,256,256]{3,2,1,0:T(8,128)(2,1)S(1)}, bf16[4,4,256,256]{3,2,1,0:T(8,128)(2,1)}, u32[]{:S(2)}) copy-start(bf16[4,4,256,256]{3,2,1,0:T(8,128)(2,1)} %win_ref.5) | copy-start | bytes 6291460
  49.4 3.6 %collective-permute-start = (bf16[8,8,32,256]{3,2,1,0:T(8,128)(2,1)S(1)}, bf16[8,8,32,256]{3,2,1,0:T(8,128)(2,1)S(1)}, u32[]{:S(2)}, u32[]{:S(2)}) collective-permute-start(bf16[8,8,32,256]{3,2,1,0:T(8,128)(2,1)S(1)} %all_to_all.21.own_ref), channel_id=1, source_target_pairs={{0,1},{1,0},{2,3},{3,2},{4,5},{5,4},{6,7},{7,6},{8,9},{9,8},{10,11... | collective-permute-start | bytes 3145736 | tf_op jit(solution)/shard_map/ppermute | solution.py:229
  56.4 1.6 %copy-start.2 = (bf16[4,4,256,256]{3,2,1,0:T(8,128)(2,1)S(1)}, bf16[4,4,256,256]{3,2,1,0:T(8,128)(2,1)}, u32[]{:S(2)}) copy-start(bf16[4,4,256,256]{3,2,1,0:T(8,128)(2,1)} %wout_ref.5) | copy-start | bytes 6291460
  59.3 2.7 %collective-permute-start.1 = (bf16[8,8,32,256]{3,2,1,0:T(8,128)(2,1)S(1)}, bf16[8,8,32,256]{3,2,1,0:T(8,128)(2,1)S(1)}, u32[]{:S(2)}, u32[]{:S(2)}) collective-permute-start(bf16[8,8,32,256]{3,2,1,0:T(8,128)(2,1)S(1)} %get-tuple-element.26), channel_id=1, source_target_pairs={{0,1},{1,0},{2,3},{3,2},{4,5},{5,4},{6,7},{7,6},{8,9},{9,8},{10,11... | collective-permute-start | bytes 3145736 | tf_op jit(solution)/shard_map/ppermute | solution.py:266
  111.4 7.3 %collective-permute-start.2 = (bf16[2,4,4,16,256]{4,3,2,1,0:T(8,128)(2,1)S(1)}, bf16[2,4,4,16,256]{4,3,2,1,0:T(8,128)(2,1)S(1)}, u32[]{:S(2)}, u32[]{:S(2)}) collective-permute-start(bf16[2,4,4,16,256]{4,3,2,1,0:T(8,128)(2,1)S(1)} %fetch_away.1), channel_id=1, source_target_pairs={{0,16},{16,0},{32,48},{48,32},{64,80},{80,64},{96,112},{112,96},{1... | collective-permute-start | bytes 786440 | tf_op jit(solution)/shard_map/ppermute | solution.py:293
Sparse Core Ops, SparseCore 0:
  56.5 53.8 reduce-scatter.1
